TPU v7x, 32 devices: a whole 2x2x4 slice. The times are simulated.
32 devices in a mesh: seq: 8 (over z, y), dp: 4 (over x, core).
Axes of the slice: x: 2, y: 2, z: 4, core: 2. Of those that a mesh axis runs over, the one named last changes fastest.
Arguments:
- residual_in: bfloat16 [8, 6144, 768], P('dp', 'seq'), may hold values from -6 to 6
- cotangent: bfloat16 [8, 6144, 768], P('dp', 'seq'), may hold values from -6 to 6
- norm_gain: float32 [768], replicated, may hold values from 0.1 to 1.9
- in_weight: bfloat16 [768, 3352], P('dp'), may hold values from -0.21875 to 0.21875
- conv_weight: float32 [1792, 4], replicated, may hold values from -3 to 3
- conv_bias: float32 [1792], replicated, may hold values from -3 to 3
- step_bias: float32 [24], replicated, may hold values from -4.5 to -2.5
- decay_log: float32 [24], replicated, may hold values from -5.8 to -0.7
- skip_gain: float32 [24], replicated, may hold values from 0.5 to 1.5
- gate_gain: float32 [1536], replicated, may hold values from 0.1 to 1.9
- out_weight: bfloat16 [1536, 768], P('dp'), may hold values from -0.15625 to 0.15625
- in_down: bfloat16 [8, 768, 16], P('dp'), may hold values from -0.21875 to 0.21875
- in_up: bfloat16 [8, 16, 3352], P('dp'), may hold values from -0.75 to 0.75
- out_down: bfloat16 [8, 1536, 16], P('dp'), may hold values from -0.15625 to 0.15625
- out_up: bfloat16 [8, 16, 768], P('dp'), may hold values from -0.75 to 0.75
- in_index: int32 [8, 1], P('dp'), may hold values from 0 to 7
- out_index: int32 [8, 1], P('dp'), may hold values from 0 to 7
Outputs:
- block_out: bfloat16 [8, 6144, 768], P('dp', 'seq')
- grad_input: bfloat16 [8, 6144, 768], P('dp', 'seq')
- grad_in_down: float32 [8, 768, 16], P('dp')
- grad_in_up: float32 [8, 16, 3352], P('dp')
- grad_out_down: float32 [8, 1536, 16], P('dp')
- grad_out_up: float32 [8, 16, 768], P('dp')
Inputs may be any that keep to these rules, and one draw needn't show every extreme that they name: `in_index`: every adapter is chosen by at least one sequence. `out_index`: every adapter is chosen by at least one sequence.
All inputs are finite; a program needn't handle non-finite values.
Results may differ from a plain program's by a relative error of at most 0.02.
Values may be sent and summed in bfloat16 or wider, within the bound.
A program may use at most 320 MiB of HBM per device.

v0:
```python
import jax
import jax.numpy as jnp
from jax import lax
from jax.sharding import PartitionSpec as P

SPAN = 256


EPS = 1e-05


def from_behind(block, axis, distance):
    devices = range(lax.axis_size(axis))
    route = [(i - distance, i) for i in devices if i - distance in devices]
    return lax.ppermute(block, axis, route)


def carried_in(array, axis, combine, identity):
    count, index = (lax.axis_size(axis), lax.axis_index(axis))
    everything = jax.tree.map(lambda part: lax.all_gather(part, axis), array)
    start = jax.tree.map(
        lambda part, zero: jnp.broadcast_to(jnp.asarray(zero, part.dtype), part.shape),
        array,
        identity,
    )

    def turn(k, before):
        reached = k < index
        new = combine(before, jax.tree.map(lambda part: part[k], everything))
        return jax.tree.map(lambda a, b: jnp.where(reached, a, b), new, before)

    return lax.fori_loop(0, count, turn, start)


def carried_in_2(array, axis, join, neutral):
    count = lax.axis_size(axis)
    place = lax.axis_index(axis)
    ahead = count - 1 - place
    gathered = jax.tree.map(
        lambda a, kind: lax.all_gather(a.astype(kind), axis), array, (jnp.bfloat16, jnp.bfloat16)
    )
    state = jax.tree.map(lambda a, e: jnp.zeros_like(a) + jnp.asarray(e, a.dtype), array, neutral)

    def one(turn, state):
        source = count - 1 - turn
        return join(
            state,
            jax.tree.map(
                lambda a, own: lax.dynamic_index_in_dim(a, source, 0, False).astype(own.dtype),
                gathered,
                array,
            ),
        )

    return lax.fori_loop(0, ahead, one, state)


def block_step(carry_state, values_b, widths_b, inputs_b, reads_b, decay_rate):
    rates = widths_b * decay_rate[:, None]
    cumulative = jnp.cumsum(rates, axis=1)
    length = values_b.shape[2]
    rows_at = lax.broadcasted_iota(jnp.int32, (length, length), 0)
    cols_at = lax.broadcasted_iota(jnp.int32, (length, length), 1)
    lower_mask = rows_at >= cols_at
    spread = cumulative[:, :, None] - cumulative[:, None, :]
    kernel = jnp.exp(jnp.where(lower_mask[None], spread, -1e30))
    scores = lax.dot_general(
        reads_b, inputs_b, (((0,), (0,)), ((), ())), preferred_element_type=jnp.float32
    )
    mixing = kernel * scores[None] * widths_b[:, None, :]
    inner_part = jnp.einsum("hij,hpj->hpi", mixing, values_b, preferred_element_type=jnp.float32)
    carried = jnp.exp(cumulative)[:, None, :] * jnp.einsum(
        "hpn,ni->hpi", carry_state, reads_b, preferred_element_type=jnp.float32
    )
    tail_weight = jnp.exp(cumulative[:, -1:] - cumulative) * widths_b
    update = jnp.einsum(
        "hpj,nj->hpn",
        values_b * tail_weight[:, None, :],
        inputs_b,
        preferred_element_type=jnp.float32,
    )
    carry_state = jnp.exp(cumulative[:, -1])[:, None, None] * carry_state + update
    return (carry_state, inner_part + carried)


def state_space(
    values_t, widths_t, inputs_t, reads_t, decay_rate, start_state, block_size, skip_gain
):
    total_rows = values_t.shape[2]
    step_fn = jax.checkpoint(
        lambda carry_state, vb, wb, ib, rb: block_step(carry_state, vb, wb, ib, rb, decay_rate)
    )
    carry_state = start_state
    pieces = []
    for block_at in range(total_rows // block_size):
        lo_at = block_at * block_size
        hi_at = lo_at + block_size
        carry_state, piece = step_fn(
            carry_state,
            values_t[:, :, lo_at:hi_at],
            widths_t[:, lo_at:hi_at],
            inputs_t[:, lo_at:hi_at],
            reads_t[:, lo_at:hi_at],
        )
        pieces.append(piece)
    outputs = jnp.concatenate(pieces, axis=2)
    return (outputs + skip_gain[:, None, None] * values_t, carry_state)


def convolve(extended, conv_weight, conv_bias):
    taps = conv_weight.shape[1]
    length = extended.shape[0] - taps + 1
    accumulated = conv_bias[None, :] + jnp.zeros((length, conv_weight.shape[0]), jnp.float32)
    for shift_at in range(taps):
        accumulated = (
            accumulated + conv_weight[:, shift_at][None, :] * extended[shift_at : shift_at + length]
        )
    return accumulated


def combine_chain(earlier, later):
    return (earlier[0] * later[0], later[0][:, None, None] * earlier[1] + later[1])


def pick_adapter(onehot, table):
    return jnp.einsum("e,edr->dr", onehot, table, preferred_element_type=jnp.float32).astype(
        jnp.bfloat16
    )


def on_device(
    residual_in,
    cotangent,
    norm_gain,
    in_weight,
    conv_weight,
    conv_bias,
    step_bias,
    decay_log,
    skip_gain,
    gate_gain,
    out_weight,
    in_down,
    in_up,
    out_down,
    out_up,
    in_index,
    out_index,
):
    micro_count, tokens, model_width = residual_in.shape
    head_count = step_bias.shape[0]
    inner_width = gate_gain.shape[0]
    head_width = inner_width // head_count
    mixer_width = conv_weight.shape[0]
    state_width = (mixer_width - inner_width) // 2
    kernel_width = conv_weight.shape[1]
    rank_width = in_down.shape[2]
    proj_width = in_weight.shape[1]
    adapter_count = in_down.shape[0] * lax.axis_size("dp")
    decay_rate = -jnp.exp(decay_log)
    shards = (in_weight, out_weight, in_down, in_up, out_down, out_up)
    zero_state = jnp.zeros((head_count, head_width, state_width), jnp.float32)
    adapter_ids = lax.iota(jnp.int32, adapter_count)
    acc_in_down = jnp.zeros((adapter_count, model_width, rank_width), jnp.float32)
    acc_in_up = jnp.zeros((adapter_count, rank_width, proj_width), jnp.float32)
    acc_out_down = jnp.zeros((adapter_count, inner_width, rank_width), jnp.float32)
    acc_out_up = jnp.zeros((adapter_count, rank_width, model_width), jnp.float32)
    block_outs = []
    input_grads = []
    for micro_index in range(micro_count):
        full_fwd = (
            lax.all_gather(shards[0], "dp", axis=0, tiled=True),
            lax.all_gather(shards[1], "dp", axis=0, tiled=True),
            lax.all_gather(shards[2], "dp", axis=0, tiled=True),
            lax.all_gather(shards[3], "dp", axis=0, tiled=True),
            lax.all_gather(shards[4], "dp", axis=0, tiled=True),
            lax.all_gather(shards[5], "dp", axis=0, tiled=True),
        )
        w_in, w_out, full_in_down, full_in_up, full_out_down, full_out_up = full_fwd
        onehot_in = (in_index[micro_index, 0] == adapter_ids).astype(jnp.bfloat16)
        onehot_out = (out_index[micro_index, 0] == adapter_ids).astype(jnp.bfloat16)
        sel_in_down = pick_adapter(onehot_in, full_in_down)
        sel_in_up = pick_adapter(onehot_in, full_in_up)
        sel_out_down = pick_adapter(onehot_out, full_out_down)
        sel_out_up = pick_adapter(onehot_out, full_out_up)
        source = residual_in[micro_index].astype(jnp.float32)
        scale_in = lax.rsqrt(jnp.mean(source * source, axis=1, keepdims=True) + EPS)
        normed = (source * scale_in * norm_gain[None, :]).astype(jnp.bfloat16)
        low_in = jnp.dot(normed, sel_in_down, preferred_element_type=jnp.float32).astype(
            jnp.bfloat16
        )
        project = (
            jnp.dot(normed, w_in, preferred_element_type=jnp.float32)
            + jnp.dot(low_in, sel_in_up, preferred_element_type=jnp.float32)
        ).astype(jnp.bfloat16)
        gate_part = project[:, :inner_width].astype(jnp.float32)
        mixer_part = project[:, inner_width : inner_width + mixer_width]
        width_raw = project[:, inner_width + mixer_width :].astype(jnp.float32)
        rim_rows = from_behind(mixer_part[tokens - kernel_width + 1 :], "seq", 1)
        extended = jnp.concatenate([rim_rows, mixer_part], axis=0).astype(jnp.float32)
        before_act, conv_pull = jax.vjp(
            lambda ext_rows: convolve(ext_rows, conv_weight, conv_bias), extended
        )
        activated_t = jax.nn.silu(before_act).T
        values_t = activated_t[:inner_width].reshape(head_count, head_width, tokens)
        inputs_t = activated_t[inner_width : inner_width + state_width]
        reads_t = activated_t[inner_width + state_width :]
        widths = jax.nn.softplus(width_raw + step_bias[None, :])
        widths_t = widths.T
        (local_out, local_state), local_pull = jax.vjp(
            lambda val_in, wid_in, inb_in, rdc_in: state_space(
                val_in, wid_in, inb_in, rdc_in, decay_rate, zero_state, SPAN, skip_gain
            ),
            values_t,
            widths_t,
            inputs_t,
            reads_t,
        )
        cumulative = jnp.cumsum(widths_t * decay_rate[:, None], axis=1)
        total_decay = jnp.exp(cumulative[:, -1])
        chain_out = carried_in(
            (total_decay, local_state),
            "seq",
            combine_chain,
            (jnp.ones_like(total_decay), jnp.zeros_like(local_state)),
        )
        start_state = chain_out[1]

        def correction(wid_in, rdc_in):
            cumul_in = jnp.cumsum(wid_in * decay_rate[:, None], axis=1)
            term_out = jnp.exp(cumul_in)[:, None, :] * jnp.einsum(
                "hpn,ni->hpi", start_state, rdc_in, preferred_element_type=jnp.float32
            )
            return (term_out, jnp.exp(cumul_in[:, -1])[:, None, None] * start_state)

        (reads_term, end_part), corr_pull = jax.vjp(correction, widths_t, reads_t)
        ssd_out = (local_out + reads_term).reshape(inner_width, tokens).T
        gate_silu = jax.nn.silu(gate_part)
        gated = ssd_out * gate_silu
        scale_out = lax.rsqrt(jnp.mean(gated * gated, axis=1, keepdims=True) + EPS)
        normed_out = (gated * scale_out * gate_gain[None, :]).astype(jnp.bfloat16)
        low_out = jnp.dot(normed_out, sel_out_down, preferred_element_type=jnp.float32).astype(
            jnp.bfloat16
        )
        result = (
            source
            + jnp.dot(normed_out, w_out, preferred_element_type=jnp.float32)
            + jnp.dot(low_out, sel_out_up, preferred_element_type=jnp.float32)
        )
        block_outs.append(result.astype(jnp.bfloat16))
        full_bwd = (
            lax.all_gather(shards[0], "dp", axis=0, tiled=True),
            lax.all_gather(shards[1], "dp", axis=0, tiled=True),
            lax.all_gather(shards[2], "dp", axis=0, tiled=True),
            lax.all_gather(shards[3], "dp", axis=0, tiled=True),
            lax.all_gather(shards[4], "dp", axis=0, tiled=True),
            lax.all_gather(shards[5], "dp", axis=0, tiled=True),
        )
        w_in_b, w_out_b, back_in_down, back_in_up, back_out_down, back_out_up = full_bwd
        sel_in_down = pick_adapter(onehot_in, back_in_down)
        sel_in_up = pick_adapter(onehot_in, back_in_up)
        sel_out_down = pick_adapter(onehot_out, back_out_down)
        sel_out_up = pick_adapter(onehot_out, back_out_up)
        grad_out = cotangent[micro_index]
        grad_low_out = jnp.dot(grad_out, sel_out_up.T, preferred_element_type=jnp.float32).astype(
            jnp.bfloat16
        )
        grad_out_up_sel = jnp.dot(low_out.T, grad_out, preferred_element_type=jnp.float32)
        grad_out_down_sel = jnp.dot(normed_out.T, grad_low_out, preferred_element_type=jnp.float32)
        grad_normed_out = jnp.dot(
            grad_out, w_out_b.T, preferred_element_type=jnp.float32
        ) + jnp.dot(grad_low_out, sel_out_down.T, preferred_element_type=jnp.float32)
        scaled_grad = grad_normed_out * gate_gain[None, :]
        grad_gated = scale_out * scaled_grad - gated * scale_out**3 * jnp.mean(
            gated * scaled_grad, axis=1, keepdims=True
        )
        grad_ssd_t = (grad_gated * gate_silu).T.reshape(head_count, head_width, tokens)
        gate_sigmoid = jax.nn.sigmoid(gate_part)
        grad_gate = grad_gated * ssd_out * gate_sigmoid * (1.0 + gate_part * (1.0 - gate_sigmoid))
        reach_factor = jnp.exp(cumulative)
        own_grad = jnp.einsum(
            "nt,hpt->hpn",
            reads_t,
            grad_ssd_t * reach_factor[:, None, :],
            preferred_element_type=jnp.float32,
        )
        back_chain = carried_in_2(
            (total_decay, own_grad),
            "seq",
            combine_chain,
            (jnp.ones_like(total_decay), jnp.zeros_like(own_grad)),
        )
        end_grad = back_chain[1]
        grad_values, grad_widths, grad_inputs, grad_reads = local_pull((grad_ssd_t, end_grad))
        corr_widths, corr_reads = corr_pull((grad_ssd_t, end_grad))
        grad_widths = (grad_widths + corr_widths).T
        grad_reads = grad_reads + corr_reads
        grad_activated = jnp.concatenate(
            [grad_values.reshape(inner_width, tokens), grad_inputs, grad_reads], axis=0
        ).T
        act_sigmoid = jax.nn.sigmoid(before_act)
        grad_before = grad_activated * act_sigmoid * (1.0 + before_act * (1.0 - act_sigmoid))
        grad_extended = conv_pull(grad_before)[0]
        rim_back = from_behind(grad_extended[: kernel_width - 1], "seq", -1)
        grad_mixer = grad_extended[kernel_width - 1 :].at[tokens - kernel_width + 1 :].add(rim_back)
        grad_width_raw = grad_widths * jax.nn.sigmoid(width_raw + step_bias[None, :])
        grad_project = jnp.concatenate([grad_gate, grad_mixer, grad_width_raw], axis=1).astype(
            jnp.bfloat16
        )
        grad_low_in = jnp.dot(grad_project, sel_in_up.T, preferred_element_type=jnp.float32).astype(
            jnp.bfloat16
        )
        grad_in_up_sel = jnp.dot(low_in.T, grad_project, preferred_element_type=jnp.float32)
        grad_in_down_sel = jnp.dot(normed.T, grad_low_in, preferred_element_type=jnp.float32)
        grad_normed = jnp.dot(grad_project, w_in_b.T, preferred_element_type=jnp.float32) + jnp.dot(
            grad_low_in, sel_in_down.T, preferred_element_type=jnp.float32
        )
        scaled_in = grad_normed * norm_gain[None, :]
        grad_source = scale_in * scaled_in - source * scale_in**3 * jnp.mean(
            source * scaled_in, axis=1, keepdims=True
        )
        input_grads.append((grad_out.astype(jnp.float32) + grad_source).astype(jnp.bfloat16))
        pick_in = onehot_in.astype(jnp.float32)[:, None, None]
        pick_out = onehot_out.astype(jnp.float32)[:, None, None]
        acc_in_down = acc_in_down + pick_in * grad_in_down_sel[None]
        acc_in_up = acc_in_up + pick_in * grad_in_up_sel[None]
        acc_out_down = acc_out_down + pick_out * grad_out_down_sel[None]
        acc_out_up = acc_out_up + pick_out * grad_out_up_sel[None]
    adapter_grads = (acc_in_down, acc_in_up, acc_out_down, acc_out_up)
    summed = (
        lax.psum(adapter_grads[0].astype(jnp.bfloat16), "seq").astype(jnp.float32),
        lax.psum(adapter_grads[1].astype(jnp.bfloat16), "seq").astype(jnp.float32),
        lax.psum(adapter_grads[2].astype(jnp.bfloat16), "seq").astype(jnp.float32),
        lax.psum(adapter_grads[3].astype(jnp.bfloat16), "seq").astype(jnp.float32),
    )
    shared = (
        lax.psum_scatter(
            summed[0].astype(jnp.bfloat16), "dp", scatter_dimension=0, tiled=True
        ).astype(jnp.float32),
        lax.psum_scatter(
            summed[1].astype(jnp.bfloat16), "dp", scatter_dimension=0, tiled=True
        ).astype(jnp.float32),
        lax.psum_scatter(
            summed[2].astype(jnp.bfloat16), "dp", scatter_dimension=0, tiled=True
        ).astype(jnp.float32),
        lax.psum_scatter(
            summed[3].astype(jnp.bfloat16), "dp", scatter_dimension=0, tiled=True
        ).astype(jnp.float32),
    )
    return (
        jnp.stack(block_outs),
        jnp.stack(input_grads),
        shared[0],
        shared[1],
        shared[2],
        shared[3],
    )


def solution(mesh):
    return jax.shard_map(
        on_device,
        mesh=mesh,
        in_specs=(
            P("dp", "seq", None),
            P("dp", "seq", None),
            P(),
            P("dp", None),
            P(),
            P(),
            P(),
            P(),
            P(),
            P(),
            P("dp", None),
            P("dp", None, None),
            P("dp", None, None),
            P("dp", None, None),
            P("dp", None, None),
            P("dp", None),
            P("dp", None),
        ),
        out_specs=(
            P("dp", "seq", None),
            P("dp", "seq", None),
            P("dp", None, None),
            P("dp", None, None),
            P("dp", None, None),
            P("dp", None, None),
        ),
        check_vma=False,
    )
```

profile of v0, /device:TPU:0, one launch (start us, length us, event | category | flops | bytes accessed | tf_op | source)
XLA Modules:
  0.0 1067.4 jit_solution(7927970903425906028)
XLA Ops:
  10.1 7.0 all_gather.37
  18.8 14.3 %all_gather.38 = bf16[8,16,3352]{2,1,0:T(8,128)(2,1)S(1)} all-gather(bf16[2,16,3352]{2,1,0:T(8,128)(2,1)} %param.41), channel_id=1, replica_groups=mesh['seq'=8,'dp'=4] {'dp'}, dimensions={0}, use_global_device_ids=true | all-gather | bytes 1072640 | tf_op jit(solution)/shard_map/all_gather | solution.py:175
  38.6 18.9 %all-gather.15.cloned.1.call-done = bf16[768,3352]{1,0:T(8,128)(2,1)} async-done(((bf16[192,3352]{1,0:T(8,128)(2,1)}), bf16[768,3352]{1,0:T(8,128)(2,1)}) %all-gather.15.cloned.1.call-update) | async-done | bytes 5148688 | tf_op jit(solution)/shard_map/all_gather | solution.py:172
  57.5 7.2 fusion.577
  72.0 7.2 fusion.582
  95.4 7.0 collective-permute-done
  103.9 12.2 %multiply_bitcast_fusion.1 = (f32[1792,768]{1,0:T(8,128)S(1)}, f32[768,1792]{0,1:T(8,128)}, f32[1792,768]{1,0:T(8,128)}, f32[768,1792]{0,1:T(8,128)}) fusion(f32[771,1792]{0,1:T(8,128)S(1)} %maximum_convert_fusion, f32[1792]{0:T(1024)S(1)} %get-tuple-element.572, f32[1792]{0:T(1024)S(1)} %copy-done.203, f32[1792]{0:T(1024)S(1)} %copy-done.201, ...), kind=kLoop, calls=%fused_computation.122 | loop fusion | flops 33030144 | bytes 66096128 | tf_op jit(solution)/shard_map/transpose | solution.py:204
  170.2 22.0 %all-reduce.52 = (bf16[192]{0:T(256)(128)(2,1)S(1)}, bf16[192]{0:T(256)(128)(2,1)S(1)}) all-reduce(bf16[192]{0:T(256)(128)(2,1)S(1)} %dynamic-update-slice.9, bf16[192]{0:T(256)(128)(2,1)S(1)} %dynamic-update-slice.8), channel_id=9, replica_groups=mesh['seq'=8,'dp'=4] {'seq'}, use_global_device_ids=true, to_apply=%add.49 | all-reduce | flops 384 | bytes 1536
  194.5 17.5 %all-reduce.50 = (f32[192]{0:T(256)S(1)}, f32[192]{0:T(256)S(1)}) all-reduce(f32[192]{0:T(256)S(1)} %dynamic-update-slice.7, f32[192]{0:T(256)S(1)} %dynamic-update-slice.6), channel_id=4, replica_groups=mesh['seq'=8,'dp'=4] {'seq'}, use_global_device_ids=true, to_apply=%add.47 | all-reduce | flops 384 | bytes 3072
  268.2 10.8 %while.60 = (s32[]{:T(128)}, f32[24,64,128]{2,1,0:T(8,128)S(1)}, s32[]{:T(128)}, f32[8,24]{1,0:T(8,128)S(1)}, f32[8,24,64,128]{3,2,1,0:T(8,128)}, /*index=5*/s32[]{:T(128)}, s32[]{:T(128)}) while((s32[]{:T(128)}, f32[24,64,128]{2,1,0:T(8,128)S(1)}, s32[]{:T(128)}, f32[8,24]{1,0:T(8,128)S(1)}, f32[8,24,64,128]{3,2,1,0:T(8,128)}, ...), condition=%wide.region_10.11_spmd.clone, body=%wide.region_9.10_spmd.clone.sunk | while | flops 786436 | bytes 2359697 | solution.py:32
  279.0 7.4 fusion.86
  317.8 21.2 %all-gather.21.cloned.1.call-done = f32[192,64,128]{2,1,0:T(8,128)} async-done(((f32[24,64,128]{2,1,0:T(8,128)}), f32[192,64,128]{2,1,0:T(8,128)}) %all-gather.21.cloned.1.call-update) | async-done | bytes 6291472 | tf_op jit(solution)/shard_map/all_gather | solution.py:20
  339.0 16.1 %while.61 = (s32[]{:T(128)}, f32[24,64,128]{2,1,0:T(8,128)S(1)}, s32[]{:T(128)}, f32[8,24]{1,0:T(8,128)}, f32[8,24,64,128]{3,2,1,0:T(8,128)}, /*index=5*/s32[]{:T(128)}, s32[]{:T(128)}) while((s32[]{:T(128)}, f32[24,64,128]{2,1,0:T(8,128)S(1)}, s32[]{:T(128)}, f32[8,24]{1,0:T(8,128)}, f32[8,24,64,128]{3,2,1,0:T(8,128)}, ...), condition=%wide.region_22.23_spmd.clone, body=%wide.region_21.22_spmd.clone.sunk | while | flops 786436 | bytes 2359697 | solution.py:32
  355.1 45.1 %all-gather.23.cloned.1.call-done = bf16[192,64,128]{2,1,0:T(8,128)(2,1)} async-done(((bf16[24,64,128]{2,1,0:T(8,128)(2,1)}), bf16[192,64,128]{2,1,0:T(8,128)(2,1)}) %all-gather.23.cloned.1.call-update) | async-done | bytes 3145744 | tf_op jit(solution)/shard_map/all_gather | solution.py:40
  400.4 13.4 %while.58 = (s32[]{:T(128)}, f32[24,64,128]{2,1,0:T(8,128)S(1)}, s32[]{:T(128)}, bf16[8,24]{1,0:T(8,128)(2,1)}, bf16[8,24,64,128]{3,2,1,0:T(8,128)(2,1)}, /*index=5*/s32[]{:T(128)}, s32[]{:T(128)}, s32[]{:T(128)}, s32[]{:T(128)}) while((s32[]{:T(128)}, f32[24,64,128]{2,1,0:T(8,128)S(1)}, s32[]{:T(128)}, bf16[8,24]{1,0:T(8,128)(2,1)}, ...), condition=%wide.region_26.27_spmd, body=%wide.region_25.26_spmd.sunk | while | flops 589854 | bytes 1966475 | solution.py:55
  453.3 12.8 %pad_add_fusion.3 = (f32[24,64,768]{2,1,0:T(8,128)}, f32[24,768]{1,0:T(8,128)}, f32[24,64,768]{2,1,0:T(8,128)}, f32[24,64,768]{2,1,0:T(8,128)}) fusion(f32[24,64,256]{2,1,0:T(8,128)} %multiply_add_fusion.3, f32[24,64,256]{2,1,0:T(8,128)} %multiply_add_fusion.4, f32[24,64,256]{2,1,0:T(8,128)} %multiply_add_fusion.5, f32[24,64,768]{2,1,0:T(8,128)S(1)} %bitcast.909, ...), kind=kOutput, calls=%fused_computation.164 | convolution fusion | flops 316127232 | bytes 38879744 | tf_op jit(solution)/shard_map/jvp(hpn,ni->hpi)/dot_general | solution.py:231
  472.2 6.7 fusion.85
  483.7 7.6 reduce-window.194
  526.2 15.2 %all-gather.25.cloned.1.call-done = bf16[192,64,128]{2,1,0:T(8,128)(2,1)} async-done(((bf16[24,64,128]{2,1,0:T(8,128)(2,1)}), bf16[192,64,128]{2,1,0:T(8,128)(2,1)}) %all-gather.25.cloned.1.call-update) | async-done | bytes 3145744 | tf_op jit(solution)/shard_map/all_gather | solution.py:40
  541.5 13.4 %while.59 = (s32[]{:T(128)}, f32[24,64,128]{2,1,0:T(8,128)S(1)}, s32[]{:T(128)}, bf16[8,24]{1,0:T(8,128)(2,1)}, bf16[8,24,64,128]{3,2,1,0:T(8,128)(2,1)}, /*index=5*/s32[]{:T(128)}, s32[]{:T(128)}, s32[]{:T(128)}, s32[]{:T(128)}) while((s32[]{:T(128)}, f32[24,64,128]{2,1,0:T(8,128)S(1)}, s32[]{:T(128)}, bf16[8,24]{1,0:T(8,128)(2,1)}, ...), condition=%wide.region_70.71_spmd, body=%wide.region_69.70_spmd.sunk | while | flops 589854 | bytes 1966475 | solution.py:55
  606.8 9.4 fusion.107
  624.4 17.7 %fusion.99 = (f32[24,256]{1,0:T(8,128)}, f32[24,256]{1,0:T(8,128)}, f32[24,256]{1,0:T(8,128)}, bf16[256,256]{1,0:T(8,128)(2,1)}, bf16[256,256]{1,0:T(8,128)(2,1)...) fusion(f32[24,256]{1,0:T(8,128)S(1)} %copy-done.144, ...), kind=kOutput, calls=%fused_computation.181 | convolution fusion | flops 282779648 | bytes 24150016 | tf_op jit(solution)/shard_map/transpose(jvp(jvp()))/checkpoint/hij,hpj->hpi/dot_general | solution.py:71
  657.7 14.7 %broadcast_multiply_fusion.1 = (f32[768,1792]{0,1:T(8,128)S(1)}, f32[768,1792]{0,1:T(8,128)}, f32[768,1792]{0,1:T(8,128)S(1)}, f32[768,1792]{0,1:T(8,128)}) fusion(f32[1792]{0:T(1024)S(1)} %copy-done.198, f32[768,1792]{0,1:T(8,128)} %get-tuple-element.628, f32[128,768]{1,0:T(8,128)S(1)} %fusion.311, f32[128,768]{1,0:T(8,128)S(1)} %pad_add_fusion.7, ...), kind=kLoop, calls=%fused_computation.267 | loop fusion | flops 30277632 | bytes 44047360 | tf_op jit(solution)/shard_map/transpose(jvp())/mul | solution.py:116
  672.4 18.3 %broadcast_multiply_fusion.2 = (f32[768,1792]{0,1:T(8,128)}, f32[768,1792]{0,1:T(8,128)}, f32[768,1792]{0,1:T(8,128)}, f32[768,1792]{0,1:T(8,128)}, f32[768,1792]{0,1:T(8,128)}, /*index=5*/f32[768,1792]{0,1:T(8,128)}) fusion(f32[768,1792]{0,1:T(8,128)} %get-tuple-element.734, f32[1792]{0:T(1024)S(1)} %copy-done.204, f32[1792]{0:T(1024)S(1)} %copy-done.202, ...), kind=kLoop, calls=%fused_computation.268 | loop fusion | flops 8257536 | bytes 44061696 | tf_op jit(solution)/shard_map/transpose(jvp())/mul | solution.py:116
  694.1 10.2 pad_add_fusion
  720.9 8.1 reduce-window.216
  845.5 7.2 fusion.585
  856.0 8.5 fusion.587
  866.9 16.1 %reduce-scatter.9.cloned.1.call-done = bf16[2,1536,16]{1,2,0:T(8,128)(2,1)} async-done(((bf16[8,1536,16]{1,2,0:T(8,128)(2,1)}), bf16[2,1536,16]{1,2,0:T(8,128)(2,1)}) %reduce-scatter.9.cloned.1.call-update) | async-done | bytes 98320 | tf_op jit(solution)/shard_map/reduce_scatter | solution.py:343
  883.1 26.3 %reduce-scatter.7.cloned.1.call-done = bf16[2,16,3352]{2,1,0:T(8,128)(2,1)} async-done(((bf16[8,16,3352]{2,1,0:T(8,128)(2,1)}), bf16[2,16,3352]{2,1,0:T(8,128)(2,1)}) %reduce-scatter.7.cloned.1.call-update) | async-done | bytes 214544 | tf_op jit(solution)/shard_map/reduce_scatter | solution.py:340
  914.8 68.1 %all-reduce.57.cloned.1.call-done = (bf16[2,768,16]{1,2,0:T(8,128)(2,1)}, bf16[2,16,768]{2,1,0:T(8,128)(2,1)}) async-done(((bf16[2,768,16]{1,2,0:T(8,128)(2,1)}, bf16[2,16,768]{2,1,0:T(8,128)(2,1)}), (bf16[2,768,16]{1,2,0:T(8,128)(2,1)}, bf16[2,16,768]{2,1,0:T(8,128)(2,1)})) %all-reduce.57.cloned.1.call-update) | async-done | bytes 98320 | tf_op jit(solution)/shard_map/psum | solution.py:331
  985.8 71.0 %all-reduce.59.cloned.1.call-done = (bf16[2,16,3352]{2,1,0:T(8,128)(2,1)}, bf16[2,1536,16]{1,2,0:T(8,128)(2,1)}) async-done(((bf16[2,16,3352]{2,1,0:T(8,128)(2,1)}, bf16[2,1536,16]{1,2,0:T(8,128)(2,1)}), (bf16[2,16,3352]{2,1,0:T(8,128)(2,1)}, bf16[2,1536,16]{1,2,0:T(8,128)(2,1)})) %all-reduce.59.cloned.1.call-update) | async-done | bytes 312848 | tf_op jit(solution)/shard_map/psum | solution.py:332
  (1128 shorter events, 542.4 us)
Async XLA Ops:
  7.2 50.3 %all-gather.15.cloned.1.call-start = ((), (), s32[]{:S(2)}) async-start(), calls=%async_computation.4 | async-start | bytes 6635520 | tf_op jit(solution)/shard_map/all_gather | solution.py:172
  7.9 141.9 %all-gather.17.cloned.1.call-start = ((), (), s32[]{:S(2)}) async-start(), calls=%async_computation.5 | async-start | bytes 2949120 | tf_op jit(solution)/shard_map/all_gather | solution.py:173
  8.7 259.5 %all-gather.19.cloned.1.call-start = ((), (), s32[]{:S(2)}) async-start(), calls=%async_computation.6 | async-start | bytes 7077888 | tf_op jit(solution)/shard_map/all_gather | solution.py:20
  35.2 129.0 %copy-start.175 = (f32[24]{0:T(128)}, f32[24]{0:T(128)S(1)}, u32[]{:S(2)}) copy-start(f32[24]{0:T(128)S(1)} %exponential_negate_fusion) | copy-start | bytes 292
  36.5 67.4 %copy-start.197 = (f32[1792]{0:T(1024)}, f32[1792]{0:T(1024)S(1)}, u32[]{:S(2)}) copy-start(f32[1792]{0:T(1024)S(1)} %get-tuple-element.572) | copy-start | bytes 21508
  67.4 25.4 %collective-permute-start.1 = (bf16[3,1792]{0,1:T(8,128)(2,1)}, bf16[3,1792]{0,1:T(8,128)(2,1)}, u32[]{:S(2)}, u32[]{:S(2)}) collective-permute-start(bf16[3,1792]{0,1:T(8,128)(2,1)} %slice.578), channel_id=1, source_target_pairs={{0,4},{4,8},{8,12},{12,16},{16,20},{20,24},{24,28},{1,5},{5,9},{9,... | collective-permute-start | bytes 32264 | tf_op jit(solution)/shard_map/ppermute | solution.py:15
  87.8 160.8 %copy-start.138 = (f32[24,256]{1,0:T(8,128)}, f32[24,256]{1,0:T(8,128)S(1)}, u32[]{:S(2)}) copy-start(f32[24,256]{1,0:T(8,128)S(1)} %get-tuple-element.445) | copy-start | bytes 73732
  87.8 165.2 %copy-start.141 = (f32[24,256]{1,0:T(8,128)}, f32[24,256]{1,0:T(8,128)S(1)}, u32[]{:S(2)}) copy-start(f32[24,256]{1,0:T(8,128)S(1)} %get-tuple-element.439) | copy-start | bytes 73732
  87.8 362.3 %copy-start.136 = (f32[24,256]{1,0:T(8,128)}, f32[24,256]{1,0:T(8,128)S(1)}, u32[]{:S(2)}) copy-start(f32[24,256]{1,0:T(8,128)S(1)} %get-tuple-element.451) | copy-start | bytes 73732
  89.6 12.8 %collective-permute-start = (bf16[3,1792]{0,1:T(8,128)(2,1)S(1)}, bf16[3,1792]{0,1:T(8,128)(2,1)S(1)}, u32[]{:S(2)}, u32[]{:S(2)}) collective-permute-start(bf16[3,1792]{0,1:T(8,128)(2,1)S(1)} %slice.548), channel_id=1, source_target_pairs={{0,4},{4,8},{8,12},{12,16},{16,20},{20,24},{24,28},{1,5},{5,9},{9,... | collective-permute-start | bytes 32264 | tf_op jit(solution)/shard_map/ppermute | solution.py:15
  121.8 217.2 %all-gather.21.cloned.1.call-start = ((), (), s32[]{:S(2)}) async-start(), calls=%async_computation.7 | async-start | bytes 7077888 | tf_op jit(solution)/shard_map/all_gather | solution.py:20
  143.5 87.6 %copy-start.209 = (pred[256,256]{1,0:T(8,128)(4,1)}, pred[256,256]{1,0:T(8,128)(4,1)S(1)}, u32[]{:S(2)}) copy-start(pred[256,256]{1,0:T(8,128)(4,1)S(1)} %iota_compare_fusion) | copy-start | bytes 196612
  167.2 49.7 %copy-start.217 = (f32[24,7]{0,1:T(8,128)}, f32[24,7]{0,1:T(8,128)S(1)}, u32[]{:S(2)}) copy-start(f32[24,7]{0,1:T(8,128)S(1)} %reduce-window.159) | copy-start | bytes 2020
  168.9 48.0 %copy-start.81 = (f32[24,6,128]{2,0,1:T(8,128)}, f32[24,6,128]{2,0,1:T(8,128)S(1)}, u32[]{:S(2)}) copy-start(f32[24,6,128]{2,0,1:T(8,128)S(1)} %reduce-window.170) | copy-start | bytes 221188
  169.1 47.8 %copy-start.216 = (f32[24,7]{0,1:T(8,128)}, f32[24,7]{0,1:T(8,128)S(1)}, u32[]{:S(2)}) copy-start(f32[24,7]{0,1:T(8,128)S(1)} %reduce-window.171) | copy-start | bytes 2020
  213.4 83.8 %copy-start.87 = (f32[24,768]{1,0:T(8,128)}, f32[24,768]{1,0:T(8,128)S(1)}, u32[]{:S(2)}) copy-start(f32[24,768]{1,0:T(8,128)S(1)} %fusion.518) | copy-start | bytes 221188
  241.9 158.3 %all-gather.23.cloned.1.call-start = ((), (), s32[]{:S(2)}) async-start(), calls=%async_computation.8 | async-start | bytes 3538944 | tf_op jit(solution)/shard_map/all_gather | solution.py:40
  278.9 134.8 %copy-start.7 = (f32[24,64,128]{2,1,0:T(8,128)}, f32[24,64,128]{2,1,0:T(8,128)S(1)}, u32[]{:S(2)}) copy-start(f32[24,64,128]{2,1,0:T(8,128)S(1)} %get-tuple-element.434) | copy-start | bytes 2359300
  301.9 239.4 %all-gather.25.cloned.1.call-start = ((), (), s32[]{:S(2)}) async-start(), calls=%async_computation.9 | async-start | bytes 3538944 | tf_op jit(solution)/shard_map/all_gather | solution.py:40
  483.5 383.3 %reduce-scatter.11.cloned.1.call-start = ((), (), s32[]{:S(2)}) async-start(), calls=%async_computation.13 | async-start | bytes 245760 | tf_op jit(solution)/shard_map/reduce_scatter | solution.py:346
  526.1 340.7 %reduce-scatter.5.cloned.1.call-start = ((), (), s32[]{:S(2)}) async-start(), calls=%async_computation.10 | async-start | bytes 245760 | tf_op jit(solution)/shard_map/reduce_scatter | solution.py:337
  707.2 54.1 %copy-start.104 = (f32[24,2,128]{2,0,1:T(8,128)S(1)}, f32[24,2,128]{2,0,1:T(8,128)}, u32[]{:S(2)}) copy-start(f32[24,2,128]{2,0,1:T(8,128)} %copy-done.103) | copy-start | bytes 73732
  707.2 54.1 %copy-start.131 = (f32[24,256]{1,0:T(8,128)S(1)}, f32[24,256]{1,0:T(8,128)}, u32[]{:S(2)}) copy-start(f32[24,256]{1,0:T(8,128)} %copy-done.130) | copy-start | bytes 73732
  707.3 63.3 %copy-start.106 = (f32[24,2,128]{2,0,1:T(8,128)S(1)}, f32[24,2,128]{2,0,1:T(8,128)}, u32[]{:S(2)}) copy-start(f32[24,2,128]{2,0,1:T(8,128)} %copy-done.105) | copy-start | bytes 73732
  713.9 87.5 %copy-start.116 = (f32[24,6,128]{2,0,1:T(8,128)S(1)}, f32[24,6,128]{2,0,1:T(8,128)}, u32[]{:S(2)}) copy-start(f32[24,6,128]{2,0,1:T(8,128)} %copy-done.115) | copy-start | bytes 221188
  713.9 89.1 %copy-start.72 = (bf16[771,1792]{0,1:T(8,128)(2,1)S(1)}, bf16[771,1792]{0,1:T(8,128)(2,1)}, u32[]{:S(2)}) copy-start(bf16[771,1792]{0,1:T(8,128)(2,1)} %pad_add_fusion) | copy-start | bytes 8289796
  791.2 17.6 %collective-permute-start.3 = (f32[3,1792]{1,0:T(4,128)}, f32[3,1792]{1,0:T(4,128)}, u32[]{:S(2)}, u32[]{:S(2)}) collective-permute-start(f32[3,1792]{1,0:T(4,128)} %copy.270), channel_id=1, source_target_pairs={{4,0},{8,4},{12,8},{16,12},{20,16},{24,20},{28,24},{5,1},{9,5},{13... | collective-permute-start | bytes 64520 | tf_op jit(solution)/shard_map/ppermute | solution.py:15
  794.6 28.1 %collective-permute-start.2 = (f32[3,1792]{1,0:T(4,128)}, f32[3,1792]{1,0:T(4,128)}, u32[]{:S(2)}, u32[]{:S(2)}) collective-permute-start(f32[3,1792]{1,0:T(4,128)} %copy.243), channel_id=1, source_target_pairs={{4,0},{8,4},{12,8},{16,12},{20,16},{24,20},{28,24},{5,1},{9,5},{13... | collective-permute-start | bytes 64520 | tf_op jit(solution)/shard_map/ppermute | solution.py:15
  837.8 45.2 %reduce-scatter.9.cloned.1.call-start = ((), (), s32[]{:S(2)}) async-start(), calls=%async_computation.12 | async-start | bytes 491520 | tf_op jit(solution)/shard_map/reduce_scatter | solution.py:343
  838.9 70.5 %reduce-scatter.7.cloned.1.call-start = ((), (), s32[]{:S(2)}) async-start(), calls=%async_computation.11 | async-start | bytes 1105920 | tf_op jit(solution)/shard_map/reduce_scatter | solution.py:340
  856.0 126.9 %all-reduce.57.cloned.1.call-start = ((), (), s32[]{:S(2)}) async-start(), calls=%async_computation.14 | async-start | bytes 196608 | tf_op jit(solution)/shard_map/psum | solution.py:331
  866.9 189.9 %all-reduce.59.cloned.1.call-start = ((), (), s32[]{:S(2)}) async-start(), calls=%async_computation.15 | async-start | bytes 638976 | tf_op jit(solution)/shard_map/psum | solution.py:332
  (299 other events, 2896.9 us)
Sparse Core Ops, SparseCore 0:
  9.6 47.8 all-gather.14
  59.1 24.4 all-gather.16
  121.9 101.2 all-gather.18
  242.1 96.8 all-gather.20
  341.6 58.5 all-gather.22
  483.6 57.6 all-gather.24
  543.8 18.3 reduce-scatter.10
  837.9 21.1 reduce-scatter.4
  862.2 20.8 reduce-scatter.8
  885.5 23.8 reduce-scatter.6
  913.2 69.6 all-reduce.56
  986.5 70.1 all-reduce.58
where the time goes:
time: 1080 us; the launch traced here: 1070 us
  matrix products  299 us (28%)
  waiting for transfers between devices  291 us (27%)
  other arithmetic  261 us (24%)
  local copies, waits for them, and re-layouts  113 us (10%)
  blocking collectives  73.3 us (7%)
  between operations  19.3 us (2%)
  starting transfers between devices  11.2 us (1%)
    another operation x75, other arithmetic  85.5 us
    dot_general x18, matrix products, block_step(): jnp.einsum('hij,hpj->hpi', mixing, values_b, preferred_element_type=jnp.f...  77.9 us
    psum x1, waiting for transfers between devices, on_device(): lax.psum(adapter_grads[1].astype(jnp.bfloat16), 'seq').astype(jnp.float32)  71 us
    psum x1, waiting for transfers between devices, on_device(): lax.psum(adapter_grads[0].astype(jnp.bfloat16), 'seq').astype(jnp.float32)  68.1 us
    all_gather x2, waiting for transfers between devices, carried_in_2(): lax.all_gather(a.astype(kind), axis)  60.3 us
    unnamed x2, blocking collectives  39.5 us
    dot_general x22, matrix products, block_step(): jnp.einsum('hpn,ni->hpi', carry_state, reads_b, preferred_element_type=jn...  36.7 us
    mul x2, other arithmetic, convolve(): conv_weight[:, shift_at][None, :] * extended[shift_at:shift_at + length]  32.9 us
  transfers between devices with their start and end apart: 16, of which 9 were waited for; matrix products, arithmetic and copies ran while one was open for 53% of the time, Pallas kernels for 0%

commit v1 on v0

v1 whole, which is shorter than its diff:
```python
import functools

import jax
import jax.numpy as jnp
from jax import lax
from jax.experimental import pallas as pl
from jax.experimental.pallas import tpu as pltpu
from jax.sharding import PartitionSpec as P

EPS = 1e-05
CHUNK = 128
BLOCK = 256
RIM = 16
LANES = 128
LOG2E = 1.4426950408889634
BF = jnp.bfloat16
F32 = jnp.float32
MESH = pl.DeviceIdType.MESH
VMEM_LIMIT = 56 * 2**20


def nn(a, b):
    return lax.dot_general(a, b, (((1,), (0,)), ((), ())), preferred_element_type=F32)


def nt(a, b):
    return lax.dot_general(a, b, (((1,), (1,)), ((), ())), preferred_element_type=F32)


def tn(a, b):
    return lax.dot_general(a, b, (((0,), (0,)), ((), ())), preferred_element_type=F32)


def exact(a, b):
    return lax.dot_general(
        a, b, (((1,), (0,)), ((), ())), precision=lax.Precision.HIGHEST, preferred_element_type=F32
    )


def sigmoid(v):
    return 0.5 * jnp.tanh(0.5 * v) + 0.5


def spread(values, onehot):
    high = values.astype(BF)
    rest = (values - high.astype(F32)).astype(BF)
    return nn(high, onehot) + nn(rest, onehot)


def gather_heads(values, onehot):
    return nt(values.astype(BF), onehot)


def head_onehot(heads, inner):
    width = inner // heads
    row = lax.broadcasted_iota(jnp.int32, (heads, inner), 0)
    col = lax.broadcasted_iota(jnp.int32, (heads, inner), 1)
    low = row * width
    return jnp.where((col >= low) & (col < low + width), 1.0, 0.0).astype(BF)


def lower_ones(length):
    row = lax.broadcasted_iota(jnp.int32, (length, length), 0)
    col = lax.broadcasted_iota(jnp.int32, (length, length), 1)
    return jnp.where(row >= col, 1.0, 0.0).astype(F32)


def upper_ones(length):
    row = lax.broadcasted_iota(jnp.int32, (length, length), 0)
    col = lax.broadcasted_iota(jnp.int32, (length, length), 1)
    return jnp.where(row <= col, 1.0, 0.0).astype(F32)


def tiles(width):
    return [slice(at, min(at + LANES, width)) for at in range(0, width, LANES)]


def rows_of(j):
    return slice(j * CHUNK, (j + 1) * CHUNK)


def write_normed(dst, src, gain, step):
    rows = src.shape[0]

    def body(k, _):
        at = pl.ds(pl.multiple_of(k * step, step), step)
        v = src[at, :].astype(F32)
        scale = lax.rsqrt(jnp.mean(v * v, axis=1, keepdims=True) + EPS)
        dst[at, :] = (v * scale * gain).astype(BF)
        return 0

    lax.fori_loop(0, rows // step, body, 0)


def project_kernel(
    idx_ref, res_ref, halo_ref, win_ref, down_ref, up_ref, gain_ref, cw_ref, cb_ref, sb_ref, rate_ref,
    low_ref, gate_ref, xbc_ref, dact_ref, wid_ref, cum_ref, sig_ref, sloc_ref, dpre_ref, tot_ref, dtot_ref,
    nrm, ext, state, run, onehot,
):
    blk = pl.program_id(1)
    rows = res_ref.shape[1]
    heads, inner = onehot.shape
    mixer = cb_ref.shape[1]
    states = (mixer - inner) // 2
    proj = win_ref.shape[1]
    gain = gain_ref[...]

    @pl.when(blk == 0)
    def _():
        onehot[...] = head_onehot(heads, inner)
        state[...] = jnp.zeros_like(state)
        run[...] = jnp.zeros_like(run)
        v = halo_ref[0].astype(F32)
        scale = lax.rsqrt(jnp.mean(v * v, axis=1, keepdims=True) + EPS)
        first = (v * scale * gain).astype(BF)
        low_first = nt(first, down_ref[0]).astype(BF)
        for at in range(0, mixer, 2 * LANES):
            cols = slice(inner + at, inner + at + 2 * LANES)
            ext[0:RIM, at : at + 2 * LANES] = nn(first, win_ref[:, cols]) + nn(low_first, up_ref[0, :, cols])

    @pl.when(blk > 0)
    def _():
        ext[0:RIM, :] = ext[rows : rows + RIM, :]

    write_normed(nrm, res_ref.at[0], gain, 32)
    normed = nrm[...]
    low = nt(normed, down_ref[0]).astype(BF)
    low_ref[0] = low
    for at in range(0, mixer, 2 * LANES):
        cols = slice(inner + at, inner + at + 2 * LANES)
        ext[RIM : RIM + rows, at : at + 2 * LANES] = nn(normed, win_ref[:, cols]) + nn(low, up_ref[0, :, cols])
    cols = slice(inner + mixer, proj)
    raw = nn(normed, win_ref[:, cols]) + nn(low, up_ref[0, :, cols]) + sb_ref[...]
    for at in range(0, inner, 2 * LANES):
        cols = slice(at, at + 2 * LANES)
        gate_ref[0, :, cols] = (nn(normed, win_ref[:, cols]) + nn(low, up_ref[0, :, cols])).astype(BF)
    sig_ref[0] = sigmoid(raw)
    widths = jnp.maximum(raw, 0.0) + jnp.log1p(jnp.exp(-jnp.abs(raw)))
    wid_ref[0] = widths
    ones = lower_ones(CHUNK)
    for j in range(rows // CHUNK):
        for t in tiles(mixer):
            pre = cb_ref[:, t]
            for k in range(4):
                at = RIM - 3 + k + j * CHUNK
                pre = pre + cw_ref[k : k + 1, t] * ext[at : at + CHUNK, t]
            s = sigmoid(pre)
            act = pre * s
            xbc_ref[0, rows_of(j), t] = act.astype(BF)
            dact_ref[0, rows_of(j), t] = (s + act * (1.0 - s)).astype(BF)
    for j in range(rows // CHUNK):
        w = widths[rows_of(j)]
        c = exact(ones, w * rate_ref[...])
        cum_ref[0, rows_of(j)] = c
        last = c[CHUNK - 1 : CHUNK]
        tail = spread(jnp.exp(last - c) * w, onehot[...])
        weighted = jnp.concatenate(
            [(xbc_ref[0, rows_of(j), t].astype(F32) * tail[:, t]).astype(BF) for t in tiles(inner)], axis=1
        )
        inputs_t = xbc_ref[0, rows_of(j), inner : inner + states].astype(F32).T.astype(BF)
        update = nn(inputs_t, weighted)
        before = run[...]
        dpre_ref[0, j] = spread(jnp.exp(before), onehot[...])
        keep = spread(jnp.exp(jnp.broadcast_to(last, before.shape)), onehot[...])[0:1]
        for t in tiles(inner):
            old = state[:, t]
            sloc_ref[0, j, :, t] = old.astype(BF)
            state[:, t] = keep[:, t] * old + update[:, t]
        run[...] = before + last

    @pl.when(blk == pl.num_programs(1) - 1)
    def _():
        tot_ref[0] = state[...].astype(BF)
        dtot_ref[0] = spread(jnp.exp(run[...]), onehot[...])


def intra_kernel(xbc_ref, wid_ref, cum_ref, y_ref, onehot):
    heads, inner = onehot.shape
    states = (xbc_ref.shape[2] - inner) // 2
    width = inner // heads

    @pl.when((pl.program_id(0) == 0) & (pl.program_id(1) == 0))
    def _():
        onehot[...] = head_onehot(heads, inner)

    for j in range(xbc_ref.shape[1] // CHUNK):
        c = cum_ref[0, rows_of(j)] * LOG2E
        c_rows = c.T
        wide = spread(wid_ref[0, rows_of(j)], onehot[...])
        inputs = xbc_ref[0, rows_of(j), inner : inner + states]
        reads = xbc_ref[0, rows_of(j), inner + states :]
        scores = nt(reads, inputs) * lower_ones(CHUNK)
        lane = lax.broadcasted_iota(jnp.int32, (CHUNK, LANES), 1)
        per = LANES // width
        for k, t in enumerate(tiles(inner)):
            weighted = xbc_ref[0, rows_of(j), t].astype(F32) * wide[:, t]
            mixing, parts = [], []
            for p in range(per):
                h = k * per + p
                kernel = jnp.exp2(jnp.minimum(c[:, h : h + 1] - c_rows[h : h + 1, :], 0.0))
                mixing.append((kernel * scores).astype(BF))
                inside = (lane >= p * width) & (lane < (p + 1) * width)
                parts.append(jnp.where(inside, weighted, 0.0).astype(BF))
            y_ref[0, rows_of(j), t] = nn(jnp.concatenate(mixing, axis=1), jnp.concatenate(parts, axis=0)).astype(BF)


def output_kernel(
    idx_ref, y_ref, xbc_ref, gate_ref, cum_ref, sloc_ref, dpre_ref, tot_ref, dtot_ref, start_ref,
    res_ref, cot_ref, wout_ref, down_ref, up_ref, ggain_ref, skip_ref,
    out_ref, ggate_ref, dy_ref, dreads_ref, rowt_ref, gloc_ref, dsuf_ref, snext_ref, gown_ref, gup_ref, gdown_ref,
    onehot, snow, cur, adj, run, yp, gated, nout, gno, prod,
):
    blk = pl.program_id(1)
    rows = res_ref.shape[1]
    heads, inner = onehot.shape
    states = (xbc_ref.shape[2] - inner) // 2
    chunks = rows // CHUNK

    @pl.when(blk == 0)
    def _():
        onehot[...] = head_onehot(heads, inner)
        adj[...] = jnp.zeros_like(adj)
        run[...] = jnp.zeros_like(run)
        gup_ref[...] = jnp.zeros_like(gup_ref)
        gdown_ref[...] = jnp.zeros_like(gdown_ref)
        for t in tiles(inner):
            cur[:, t] = tot_ref[0, :, t].astype(F32) + dtot_ref[0, 0:1, t] * start_ref[0, :, t].astype(F32)

    reach = []
    for j in reversed(range(chunks)):
        snext_ref[0, j] = cur[...].astype(BF)
        for t in tiles(inner):
            s = sloc_ref[0, j, :, t].astype(F32) + dpre_ref[0, j, 0:1, t] * start_ref[0, :, t].astype(F32)
            cur[:, t] = s
            snow[j, :, t] = s.astype(BF)
        reads = xbc_ref[0, rows_of(j), inner + states :]
        carried = nn(reads, snow[j])
        grow = spread(jnp.exp(cum_ref[0, rows_of(j)]), onehot[...])
        reach.insert(0, grow)
        for t in tiles(inner):
            yp[rows_of(j), t] = y_ref[0, rows_of(j), t].astype(F32) + grow[:, t] * carried[:, t]

    scale, shrink = [], []
    for j in range(chunks):
        total = jnp.zeros((CHUNK, LANES), F32)
        for t in tiles(inner):
            y = yp[rows_of(j), t] + skip_ref[:, t] * xbc_ref[0, rows_of(j), t].astype(F32)
            g = gate_ref[0, rows_of(j), t].astype(F32)
            v = y * (g * sigmoid(g))
            gated[rows_of(j), t] = v
            total = total + v * v
        r = lax.rsqrt(jnp.sum(total, axis=1, keepdims=True) * (1.0 / inner) + EPS)
        scale.append(r)
        for t in tiles(inner):
            nout[rows_of(j), t] = (gated[rows_of(j), t] * r * ggain_ref[:, t]).astype(BF)

    normed_out = nout[...]
    cot = cot_ref[0]
    low_out = nt(normed_out, down_ref[0]).astype(BF)
    for at in range(0, out_ref.shape[2], 2 * LANES):
        t = slice(at, at + 2 * LANES)
        part = nn(normed_out, wout_ref[:, t]) + nn(low_out, up_ref[0, :, t])
        out_ref[0, :, t] = (res_ref[0, :, t].astype(F32) + part).astype(BF)
    grad_low = nt(cot, up_ref[0]).astype(BF)
    for at in range(0, inner, 2 * LANES):
        t = slice(at, at + 2 * LANES)
        gno[:, t] = nt(cot, wout_ref[t, :]) + nn(grad_low, down_ref[0, :, t])
    gup_ref[0] += tn(low_out, cot)
    gdown_ref[0] += tn(grad_low, normed_out)

    for j in range(chunks):
        total = jnp.zeros((CHUNK, LANES), F32)
        for t in tiles(inner):
            q = gno[rows_of(j), t] * ggain_ref[:, t]
            gno[rows_of(j), t] = q
            total = total + gated[rows_of(j), t] * q
        r = scale[j]
        shrink = jnp.sum(total, axis=1, keepdims=True) * (1.0 / inner) * (r * r * r)
        for t in tiles(inner):
            grad = r * gno[rows_of(j), t] - gated[rows_of(j), t] * shrink
            y_local = yp[rows_of(j), t]
            y = y_local + skip_ref[:, t] * xbc_ref[0, rows_of(j), t].astype(F32)
            g = gate_ref[0, rows_of(j), t].astype(F32)
            s = sigmoid(g)
            dy = grad * (g * s)
            dy_ref[0, rows_of(j), t] = dy.astype(BF)
            ggate_ref[0, rows_of(j), t] = (grad * y * (s * (1.0 + g * (1.0 - s)))).astype(BF)
            prod[rows_of(j), t] = (dy * y_local).astype(BF)
    rowt_ref[0] = nt(prod[...], onehot[...])

    for j in reversed(range(chunks)):
        grow = reach[j]
        scaled = jnp.concatenate(
            [(dy_ref[0, rows_of(j), t].astype(F32) * grow[:, t]).astype(BF) for t in tiles(inner)], axis=1
        )
        reads_t = xbc_ref[0, rows_of(j), inner + states :].astype(F32).T.astype(BF)
        update = nn(reads_t, scaled)
        dreads_ref[0, rows_of(j)] = nt(scaled, snow[j])
        last = cum_ref[0, j * CHUNK + CHUNK - 1 : j * CHUNK + CHUNK]
        before = run[...]
        dsuf_ref[0, j] = spread(jnp.exp(before), onehot[...])
        keep = grow[CHUNK - 1 : CHUNK]
        for t in tiles(inner):
            old = adj[:, t]
            gloc_ref[0, j, :, t] = old.astype(BF)
            adj[:, t] = keep[:, t] * old + update[:, t]
        run[...] = before + last

    @pl.when(blk == pl.num_programs(1) - 1)
    def _():
        gown_ref[0] = adj[...].astype(BF)


def intra_back_kernel(xbc_ref, wid_ref, cum_ref, dy_ref, dreads_ref, z_ref, dinputs_ref, dreads_out_ref, onehot):
    heads, inner = onehot.shape
    states = (xbc_ref.shape[2] - inner) // 2
    width = inner // heads
    per = LANES // width

    @pl.when((pl.program_id(0) == 0) & (pl.program_id(1) == 0))
    def _():
        onehot[...] = head_onehot(heads, inner)

    for j in range(xbc_ref.shape[1] // CHUNK):
        c = cum_ref[0, rows_of(j)] * LOG2E
        c_rows = c.T
        wide = spread(wid_ref[0, rows_of(j)], onehot[...])
        inputs = xbc_ref[0, rows_of(j), inner : inner + states]
        reads = xbc_ref[0, rows_of(j), inner + states :]
        mask = upper_ones(CHUNK)
        scores_t = nt(inputs, reads) * mask
        lane = lax.broadcasted_iota(jnp.int32, (CHUNK, LANES), 1)
        total = jnp.zeros((CHUNK, CHUNK), F32)
        for k, t in enumerate(tiles(inner)):
            weighted = xbc_ref[0, rows_of(j), t].astype(F32) * wide[:, t]
            grads = dy_ref[0, rows_of(j), t]
            mixing, left, right = [], [], []
            for p in range(per):
                inside = (lane >= p * width) & (lane < (p + 1) * width)
                left.append(jnp.where(inside, weighted, 0.0).astype(BF))
                right.append(jnp.where(inside, grads.astype(F32), 0.0).astype(BF))
            products = nt(jnp.concatenate(left, axis=0), grads)
            for p in range(per):
                h = k * per + p
                kernel = jnp.exp2(jnp.minimum(c_rows[h : h + 1, :] - c[:, h : h + 1], 0.0))
                mixing.append((kernel * scores_t).astype(BF))
                total = total + kernel * products[p * CHUNK : (p + 1) * CHUNK]
            z_ref[0, rows_of(j), t] = nn(jnp.concatenate(mixing, axis=1), jnp.concatenate(right, axis=0)).astype(BF)
        total = total * mask
        dinputs_ref[0, rows_of(j)] = nn(total.astype(BF), reads)
        dreads_out_ref[0, rows_of(j)] = dreads_ref[0, rows_of(j)] + nn(total.T.astype(BF), inputs)


def adjoint_kernel(
    xbc_ref, dact_ref, wid_ref, cum_ref, sig_ref, dy_ref, z_ref, dinputs_ref, dreads_ref, rowt_ref,
    gloc_ref, dsuf_ref, end_ref, snext_ref, skip_ref, rate_ref,
    gpre_ref, graw_ref,
    onehot, adj, prod,
):
    heads, inner = onehot.shape
    states = (xbc_ref.shape[2] - inner) // 2

    @pl.when((pl.program_id(0) == 0) & (pl.program_id(1) == 0))
    def _():
        onehot[...] = head_onehot(heads, inner)

    for j in range(xbc_ref.shape[1] // CHUNK):
        at = rows_of(j)
        overlap = []
        for t in tiles(inner):
            g = gloc_ref[0, j, :, t].astype(F32) + dsuf_ref[0, j, 0:1, t] * end_ref[0, :, t].astype(F32)
            adj[:, t] = g.astype(BF)
            overlap.append(jnp.sum(g * snext_ref[0, j, :, t].astype(F32), axis=0, keepdims=True))
        held = jnp.broadcast_to(jnp.concatenate(overlap, axis=1), (8, inner))
        high = held.astype(BF)
        held = (nt(high, onehot[...]) + nt((held - high.astype(F32)).astype(BF), onehot[...]))[0:1]
        c = cum_ref[0, at]
        last = c[CHUNK - 1 : CHUNK]
        w = wid_ref[0, at]
        wide = spread(w, onehot[...])
        tail = spread(jnp.exp(last - c), onehot[...])
        inputs = xbc_ref[0, at, inner : inner + states]
        carried = nn(inputs, adj[...])
        weighted = []
        for t in tiles(inner):
            x = xbc_ref[0, at, t].astype(F32)
            z = z_ref[0, at, t].astype(F32) + tail[:, t] * carried[:, t]
            prod[:, t] = (x * z).astype(BF)
            grad = wide[:, t] * z + skip_ref[:, t] * dy_ref[0, at, t].astype(F32)
            gpre_ref[0, at, t] = (grad * dact_ref[0, at, t].astype(F32)).astype(BF)
            weighted.append((x * (wide[:, t] * tail[:, t])).astype(BF))
        dinputs = dinputs_ref[0, at] + nt(jnp.concatenate(weighted, axis=1), adj[...])
        t = slice(inner, inner + states)
        gpre_ref[0, at, t] = (dinputs * dact_ref[0, at, t].astype(F32)).astype(BF)
        t = slice(inner + states, inner + 2 * states)
        gpre_ref[0, at, t] = (dreads_ref[0, at] * dact_ref[0, at, t].astype(F32)).astype(BF)
        direct = nt(prod[...], onehot[...])
        grad_rate = held + exact(upper_ones(CHUNK), rowt_ref[0, at] - w * direct)
        graw_ref[0, at] = (direct + rate_ref[...] * grad_rate) * sig_ref[0, at]


def input_kernel(
    idx_ref, gpre_ref, rim_ref, ggate_ref, graw_ref, low_ref, res_ref, cot_ref, win_ref, down_ref, up_ref, gain_ref, cw_ref,
    gin_ref, gup_ref, gdown_ref,
    ext, gp, gn, nrm,
):
    blk = pl.program_id(1)
    rows = res_ref.shape[1]
    inner = ggate_ref.shape[2]
    mixer = gpre_ref.shape[2]
    proj = win_ref.shape[1]
    model = res_ref.shape[2]

    @pl.when(blk == 0)
    def _():
        ext[rows : rows + RIM, :] = rim_ref[0].astype(F32)
        gup_ref[...] = jnp.zeros_like(gup_ref)
        gdown_ref[...] = jnp.zeros_like(gdown_ref)

    @pl.when(blk > 0)
    def _():
        ext[rows : rows + RIM, :] = ext[0:RIM, :]

    for j in range(rows // CHUNK):
        for t in tiles(mixer):
            ext[rows_of(j), t] = gpre_ref[0, rows_of(j), t].astype(F32)
    for j in range(rows // CHUNK):
        for t in tiles(mixer):
            total = None
            for k in range(4):
                at = 3 - k + j * CHUNK
                term = cw_ref[k : k + 1, t] * ext[at : at + CHUNK, t]
                total = term if total is None else total + term
            gp[rows_of(j), inner + t.start : inner + t.stop] = total.astype(BF)
    gp[:, :inner] = ggate_ref[0]
    gp[:, inner + mixer : proj] = graw_ref[0].astype(BF)
    whole = slice(0, inner + mixer)
    rest = slice(inner + mixer, proj)
    grads, grads_rest = gp[:, whole], gp[:, rest]
    grad_low = (nt(grads, up_ref[0, :, whole]) + nt(grads_rest, up_ref[0, :, rest])).astype(BF)
    for at in range(0, model, 2 * LANES):
        t = slice(at, at + 2 * LANES)
        gn[:, t] = nt(grads, win_ref[t, whole]) + nt(grads_rest, win_ref[t, rest]) + nn(grad_low, down_ref[0, :, t])

    def body(k, _):
        at = pl.ds(pl.multiple_of(k * 32, 32), 32)
        v = res_ref[0, at, :].astype(F32)
        u = lax.rsqrt(jnp.mean(v * v, axis=1, keepdims=True) + EPS)
        nrm[at, :] = (v * u * gain_ref[...]).astype(BF)
        w = gn[at, :] * gain_ref[...]
        m = jnp.mean(v * w, axis=1, keepdims=True)
        gin_ref[0, at, :] = (cot_ref[0, at, :].astype(F32) + u * w - v * (u * u * u * m)).astype(BF)
        return 0

    lax.fori_loop(0, rows // 32, body, 0)
    gup_ref[0, :, whole] += tn(low_ref[0], grads)
    gup_ref[0, :, rest] += tn(low_ref[0], grads_rest)
    gdown_ref[0] += tn(grad_low, nrm[...])


def carry_kernel(count, backwards, tot_ref, dec_ref, out_ref, theirs, theirs_dec, prefix, passed, tail, mine, sems):
    dp = lax.axis_index("dp")
    seq = lax.axis_index("seq")
    rank = count - 1 - seq if backwards else seq
    pairs = count // 2
    pair, side = rank // 2, rank % 2
    seqs, states, inner = tot_ref.shape
    half = inner // 2
    parts = theirs.shape[0] // seqs
    wide = half // parts

    def device(other):
        return (count - 1 - other if backwards else other, dp)

    partner = device(pair * 2 + 1 - side)
    ahead = device(lax.rem(pair + 1, pairs) * 2 + side)
    behind = device(lax.rem(pair + pairs - 1, pairs) * 2 + side)
    barrier = pltpu.get_barrier_semaphore()
    for other in (partner, ahead, behind):
        pl.semaphore_signal(barrier, inc=1, device_id=other, device_id_type=MESH)
    pl.semaphore_wait(barrier, 3)

    def send(kind, n, src, dst, to):
        return pltpu.make_async_remote_copy(
            src_ref=src, dst_ref=dst, send_sem=sems.at[0, kind, n], recv_sem=sems.at[1, kind, n],
            device_id=to, device_id_type=MESH,
        )

    blocks = [(s, q) for s in range(seqs) for q in range(parts)]

    def cols(base, q):
        return pl.ds(pl.multiple_of(base * half + q * wide, LANES), wide)

    decs = send(3, 0, dec_ref, theirs_dec, partner)
    decs.start()
    swaps = []
    for n, (s, q) in enumerate(blocks):
        copy = send(0, n, tot_ref.at[s, :, cols(1 - side, q)], theirs.at[n], partner)
        copy.start()
        swaps.append(copy)
    decs.wait()
    hops = [send(1, n, passed.at[n], prefix.at[n], ahead) for n in range(len(blocks))]
    gives = [send(2, n, tail.at[n], mine.at[n], partner) for n in range(len(blocks))]
    for n, (s, q) in enumerate(blocks):
        swaps[n].wait()

        @pl.when(pair == 0)
        def _(n=n):
            prefix[n] = jnp.zeros_like(prefix[n])

        @pl.when(pair > 0)
        def _(n=n):
            hops[n].wait_recv()

        own_dec = dec_ref[s, 0:1, cols(side, q)]
        their_dec = theirs_dec[s, 0:1, cols(side, q)]
        own = tot_ref[s, :, cols(side, q)].astype(F32)
        other = theirs[n].astype(F32)
        before = prefix[n].astype(F32)
        first = jnp.where(side == 0, own, other)
        second = jnp.where(side == 0, other, own)
        first_dec = jnp.where(side == 0, own_dec, their_dec)
        second_dec = jnp.where(side == 0, their_dec, own_dec)
        middle = first_dec * before + first
        passed[n] = (second_dec * middle + second).astype(BF)

        @pl.when(pair < pairs - 1)
        def _(n=n):
            hops[n].start()

        out_ref[s, :, cols(side, q)] = jnp.where(side == 0, before, middle).astype(BF)
        tail[n] = jnp.where(side == 0, middle, before).astype(BF)
        gives[n].start()
    for n, (s, q) in enumerate(blocks):
        gives[n].wait()
        out_ref[s, :, cols(1 - side, q)] = mine[n]

        @pl.when(pair < pairs - 1)
        def _(n=n):
            hops[n].wait_send()


def carry(total, decay, count, backwards):
    seqs, states, inner = total.shape
    parts = 2
    blocks = seqs * parts
    slot = pltpu.VMEM((blocks, states, inner // 2 // parts), BF)
    return pl.pallas_call(
        functools.partial(carry_kernel, count, backwards),
        out_shape=jax.ShapeDtypeStruct(total.shape, BF),
        in_specs=[pl.BlockSpec(memory_space=pltpu.VMEM)] * 2,
        out_specs=pl.BlockSpec(memory_space=pltpu.VMEM),
        scratch_shapes=[
            slot,
            pltpu.VMEM(decay.shape, F32),
            slot,
            slot,
            slot,
            slot,
            pltpu.SemaphoreType.DMA((2, 4, blocks)),
        ],
        compiler_params=pltpu.CompilerParams(
            collective_id=2 if backwards else 1, has_side_effects=True, vmem_limit_bytes=VMEM_LIMIT
        ),
        name="adjoint_carry" if backwards else "state_carry",
    )(total, decay)


def call(kernel, grid, ins, outs, scratch, name, prefetch=()):
    arrays = [a for a, _, _ in ins]
    specs = [pl.BlockSpec(block, index) for _, block, index in ins]
    return pl.pallas_call(
        kernel,
        out_shape=[jax.ShapeDtypeStruct(shape, kind) for shape, kind, _, _ in outs],
        grid_spec=pltpu.PrefetchScalarGridSpec(
            num_scalar_prefetch=len(prefetch),
            grid=grid,
            in_specs=specs,
            out_specs=[pl.BlockSpec(block, index) for _, _, block, index in outs],
            scratch_shapes=scratch,
        ),
        compiler_params=pltpu.CompilerParams(
            dimension_semantics=("arbitrary",) * len(grid), vmem_limit_bytes=VMEM_LIMIT
        ),
        name=name,
    )(*prefetch, *arrays)


def on_device(
    residual_in,
    cotangent,
    norm_gain,
    in_weight,
    conv_weight,
    conv_bias,
    step_bias,
    decay_log,
    skip_gain,
    gate_gain,
    out_weight,
    in_down,
    in_up,
    out_down,
    out_up,
    in_index,
    out_index,
):
    seqs, tokens, model = residual_in.shape
    heads = step_bias.shape[0]
    inner = gate_gain.shape[0]
    mixer = conv_weight.shape[0]
    states = (mixer - inner) // 2
    rank = in_up.shape[1]
    proj = in_weight.shape[1]
    seq_count = lax.axis_size("seq")
    dp_count = lax.axis_size("dp")
    adapters = in_down.shape[0] * dp_count
    chunks = tokens // CHUNK
    blocks = tokens // BLOCK
    per = BLOCK // CHUNK

    rate = -jnp.exp(decay_log)[None, :]
    taps = conv_weight.T
    gain = norm_gain[None, :]
    skip_wide = jnp.repeat(skip_gain, inner // heads)[None, :]
    route = [(i, i + 1) for i in range(seq_count - 1)]
    halo = lax.ppermute(residual_in[:, tokens - RIM :], "seq", route)

    def gathered(part):
        return lax.all_gather(part, "dp", axis=0, tiled=True)

    w_in = gathered(in_weight)
    w_out = gathered(out_weight)
    full_in_down = gathered(in_down.transpose(0, 2, 1))
    full_in_up = gathered(in_up)
    full_out_down = gathered(out_down.transpose(0, 2, 1))
    full_out_up = gathered(out_up)

    grid = (seqs, blocks)

    def fixed(a):
        return (a, a.shape, lambda s, b, *_: (0,) * a.ndim)

    def by_seq(a):
        return (a, (1,) + a.shape[1:], lambda s, b, *_: (s,) + (0,) * (a.ndim - 1))

    def picked(a):
        return (a, (1,) + a.shape[1:], lambda s, b, idx, *_: (idx[s],) + (0,) * (a.ndim - 1))

    def by_row(a, turn=False):
        if turn:
            return (a, (1, BLOCK, a.shape[2]), lambda s, b, *_: (s, blocks - 1 - b, 0))
        return (a, (1, BLOCK, a.shape[2]), lambda s, b, *_: (s, b, 0))

    def by_chunk(a, turn=False):
        if turn:
            return (a, (1, per) + a.shape[2:], lambda s, b, *_: (s, blocks - 1 - b, 0, 0))
        return (a, (1, per) + a.shape[2:], lambda s, b, *_: (s, b, 0, 0))

    def out(pick, shape, kind, *rest):
        spec = pick(jax.ShapeDtypeStruct(shape, kind), *rest)
        return (shape, kind, spec[1], spec[2])

    row_of = lambda width: (seqs, tokens, width)
    low, gate, xbc, dact, wid, cum, sig, sloc, dpre, tot, dtot = call(
        project_kernel,
        grid,
        [
            by_row(residual_in),
            by_seq(halo),
            fixed(w_in),
            picked(full_in_down),
            picked(full_in_up),
            fixed(gain),
            fixed(taps),
            fixed(conv_bias[None, :]),
            fixed(step_bias[None, :]),
            fixed(rate),
        ],
        [
            out(by_row, row_of(rank), BF),
            out(by_row, row_of(inner), BF),
            out(by_row, row_of(mixer), BF),
            out(by_row, row_of(mixer), BF),
            out(by_row, row_of(heads), F32),
            out(by_row, row_of(heads), F32),
            out(by_row, row_of(heads), F32),
            out(by_chunk, (seqs, chunks, states, inner), BF),
            out(by_chunk, (seqs, chunks, 8, inner), F32),
            out(by_seq, (seqs, states, inner), BF),
            out(by_seq, (seqs, 8, inner), F32),
        ],
        [
            pltpu.VMEM((BLOCK, model), BF),
            pltpu.VMEM((BLOCK + RIM, mixer), F32),
            pltpu.VMEM((states, inner), F32),
            pltpu.VMEM((8, heads), F32),
            pltpu.VMEM((heads, inner), BF),
        ],
        "project",
        prefetch=(in_index[:, 0],),
    )
    start = carry(tot, dtot, seq_count, False)
    (y_intra,) = call(
        intra_kernel,
        grid,
        [by_row(xbc), by_row(wid), by_row(cum)],
        [out(by_row, row_of(inner), BF)],
        [pltpu.VMEM((heads, inner), BF)],
        "intra",
    )
    block_out, ggate, dy, dreads, rowt, gloc, dsuf, snext, gown, gout_up, gout_down = call(
        output_kernel,
        grid,
        [
            by_row(y_intra, True),
            by_row(xbc, True),
            by_row(gate, True),
            by_row(cum, True),
            by_chunk(sloc, True),
            by_chunk(dpre, True),
            by_seq(tot),
            by_seq(dtot),
            by_seq(start),
            by_row(residual_in, True),
            by_row(cotangent, True),
            fixed(w_out),
            picked(full_out_down),
            picked(full_out_up),
            fixed(gate_gain[None, :]),
            fixed(skip_wide),
        ],
        [
            out(by_row, row_of(model), BF, True),
            out(by_row, row_of(inner), BF, True),
            out(by_row, row_of(inner), BF, True),
            out(by_row, row_of(states), F32, True),
            out(by_row, row_of(heads), F32, True),
            out(by_chunk, (seqs, chunks, states, inner), BF, True),
            out(by_chunk, (seqs, chunks, 8, inner), F32, True),
            out(by_chunk, (seqs, chunks, states, inner), BF, True),
            out(by_seq, (seqs, states, inner), BF),
            out(by_seq, (seqs, rank, model), F32),
            out(by_seq, (seqs, rank, inner), F32),
        ],
        [
            pltpu.VMEM((heads, inner), BF),
            pltpu.VMEM((per, states, inner), BF),
            pltpu.VMEM((states, inner), F32),
            pltpu.VMEM((states, inner), F32),
            pltpu.VMEM((8, heads), F32),
            pltpu.VMEM((BLOCK, inner), F32),
            pltpu.VMEM((BLOCK, inner), F32),
            pltpu.VMEM((BLOCK, inner), BF),
            pltpu.VMEM((BLOCK, inner), F32),
            pltpu.VMEM((BLOCK, inner), BF),
        ],
        "output",
        prefetch=(out_index[:, 0],),
    )
    end = carry(gown, dtot, seq_count, True)
    z, dinputs, dreads = call(
        intra_back_kernel,
        grid,
        [by_row(xbc), by_row(wid), by_row(cum), by_row(dy), by_row(dreads)],
        [out(by_row, row_of(inner), BF), out(by_row, row_of(states), F32), out(by_row, row_of(states), F32)],
        [pltpu.VMEM((heads, inner), BF)],
        "intra_back",
    )
    gpre, graw = call(
        adjoint_kernel,
        grid,
        [
            by_row(xbc),
            by_row(dact),
            by_row(wid),
            by_row(cum),
            by_row(sig),
            by_row(dy),
            by_row(z),
            by_row(dinputs),
            by_row(dreads),
            by_row(rowt),
            by_chunk(gloc),
            by_chunk(dsuf),
            by_seq(end),
            by_chunk(snext),
            fixed(skip_wide),
            fixed(rate),
        ],
        [out(by_row, row_of(mixer), BF), out(by_row, row_of(heads), F32)],
        [pltpu.VMEM((heads, inner), BF), pltpu.VMEM((states, inner), BF), pltpu.VMEM((CHUNK, inner), BF)],
        "adjoint",
    )
    rim = lax.ppermute(gpre[:, :RIM], "seq", [(j, i) for i, j in route])
    grad_input, gin_up, gin_down = call(
        input_kernel,
        grid,
        [
            by_row(gpre, True),
            by_seq(rim),
            by_row(ggate, True),
            by_row(graw, True),
            by_row(low, True),
            by_row(residual_in, True),
            by_row(cotangent, True),
            fixed(w_in),
            picked(full_in_down),
            picked(full_in_up),
            fixed(gain),
            fixed(taps),
        ],
        [
            out(by_row, row_of(model), BF, True),
            out(by_seq, (seqs, rank, proj), F32),
            out(by_seq, (seqs, rank, model), F32),
        ],
        [
            pltpu.VMEM((BLOCK + RIM, mixer), F32),
            pltpu.VMEM((BLOCK, proj), BF),
            pltpu.VMEM((BLOCK, model), F32),
            pltpu.VMEM((BLOCK, model), BF),
        ],
        "input",
        prefetch=(in_index[:, 0],),
    )

    def owned(grads, index):
        grads = lax.psum(grads.astype(BF), "seq")
        onehot = (index[:, 0][None, :] == jnp.arange(adapters)[:, None]).astype(BF)
        mine = jnp.einsum("as,srn->arn", onehot, grads, preferred_element_type=F32).astype(BF)
        return lax.psum_scatter(mine, "dp", scatter_dimension=0, tiled=True).astype(F32)

    from_in = owned(jnp.concatenate([gin_up, gin_down], axis=2), in_index)
    from_out = owned(jnp.concatenate([gout_up, gout_down], axis=2), out_index)
    return (
        block_out,
        grad_input,
        from_in[:, :, proj:].transpose(0, 2, 1),
        from_in[:, :, :proj],
        from_out[:, :, model:].transpose(0, 2, 1),
        from_out[:, :, :model],
    )


def solution(mesh):
    rows = P("dp", "seq", None)
    split = P("dp", None, None)
    return jax.shard_map(
        on_device,
        mesh=mesh,
        in_specs=(
            rows,
            rows,
            P(),
            P("dp", None),
            P(),
            P(),
            P(),
            P(),
            P(),
            P(),
            P("dp", None),
            split,
            split,
            split,
            split,
            P("dp", None),
            P("dp", None),
        ),
        out_specs=(rows, rows, split, split, split, split),
        check_vma=False,
    )
```

time: 1080 us -> 444 us (0.41); the launches traced: 1070 us -> 442 us
  matrix products: 299 us -> 2.87 us
  other arithmetic: 261 us -> 8.36 us
  Pallas kernels: 0 us -> 233 us
  waiting for transfers between devices: 291 us -> 121 us
  local copies, waits for them, and re-layouts: 113 us -> 14.9 us
  blocking collectives: 73.3 us -> 41.8 us
    dot_general x128 -> x2, matrix products: 299 us -> 2.87 us  [owned(): jnp.einsum('as,srn->arn', onehot, grads, preferred_element_type=F32)]
    pallas_call x0 -> x8, Pallas kernels: none -> 233 us  [the longest x6 169 us: call(): pl.pallas_call(kernel, out_shape=[jax.ShapeDtypeStruct(shape, kind) for s...]
    all_gather x6 -> x2, waiting for transfers between devices: 100 us -> 0.01 us  [gathered(): return lax.all_gather(part, 'dp', axis=0, tiled=True)]
    another operation x78 -> x4, other arithmetic: 92.5 us -> 3.77 us
    psum x2 -> x1, waiting for transfers between devices: 139 us -> 71.5 us  [owned(): grads = lax.psum(grads.astype(BF), 'seq')]
    mul x20 -> x0, other arithmetic: 46.4 us -> none  [the longest x2 32.9 us: convolve(): conv_weight[:, shift_at][None, :] * extended[shift_at:shift_at + length]]
    unnamed x2 -> x0, blocking collectives: 39.5 us -> none
    convert_element_type x28 -> x2, other arithmetic: 27.5 us -> 1.92 us  [owned(): lax.psum_scatter(mine, 'dp', scatter_dimension=0, tiled=True).astype(F32)]
  transfers between devices with their start and end apart: 16 -> 7, of which waited for: 9 -> 4; matrix products, arithmetic and copies ran while one was open for 53% -> 3% of each run, Pallas kernels for 0% -> 18%
where the time goes in v1:
time: 444 us; the launch traced here: 442 us
  Pallas kernels  233 us (52%)
  waiting for transfers between devices  121 us (27%)
  blocking collectives  41.8 us (9%)
  local copies, waits for them, and re-layouts  14.9 us (3%)
  between operations  13.9 us (3%)
  other arithmetic  8.36 us (2%)
  starting transfers between devices  6.34 us (1%)
    pallas_call x6, Pallas kernels, call(): pl.pallas_call(kernel, out_shape=[jax.ShapeDtypeStruct(shape, kind) for s...  169 us
    psum x1, waiting for transfers between devices, owned(): grads = lax.psum(grads.astype(BF), 'seq')  71.5 us
    pallas_call x2, Pallas kernels, carry(): pl.pallas_call(functools.partial(carry_kernel, count, backwards), out_sha...  64.5 us
    reduce_scatter x2, waiting for transfers between devices, owned(): lax.psum_scatter(mine, 'dp', scatter_dimension=0, tiled=True).astype(F32)  43.5 us
    all_gather x4, blocking collectives, gathered(): return lax.all_gather(part, 'dp', axis=0, tiled=True)  41.8 us
  transfers between devices with their start and end apart: 7, of which 4 were waited for; matrix products, arithmetic and copies ran while one was open for 3% of the time, Pallas kernels for 18%

profile of v1, /device:TPU:0, one launch (start us, length us, event | category | flops | bytes accessed | tf_op | source)
XLA Modules:
  0.0 442.5 jit_solution(16224179983124673899)
XLA Ops:
  9.5 4.9 %collective-permute-start = (bf16[2,16,768]{2,1,0:T(8,128)(2,1)S(1)}, bf16[2,16,768]{2,1,0:T(8,128)(2,1)S(1)}, u32[]{:S(2)}, u32[]{:S(2)}) collective-permute-start(bf16[2,16,768]{2,1,0:T(8,128)(2,1)S(1)} %slice.18), channel_id=1, source_target_pairs={{0,4},{4,8},{8,12},{12,16},{16,20},{20,24},{24,28},{1,5},{5,9},{9,... | collective-permute-start | bytes 147464 | tf_op jit(solution)/shard_map/ppermute | solution.py:627
  14.4 1.3 broadcast_in_dim.18.gain_ref
  15.7 1.3 broadcast_in_dim.21.ggain_ref
  17.0 1.3 broadcast_in_dim.19.cb_ref
  19.7 8.2 %all_gather.19.down_ref = bf16[8,16,768]{2,1,0:T(8,128)(2,1)} all-gather(bf16[2,16,768]{2,1,0:T(8,128)(2,1)} %bitcast.21), channel_id=1, replica_groups=mesh['seq'=8,'dp'=4] {'dp'}, dimensions={0}, use_global_device_ids=true | all-gather | bytes 245760 | tf_op jit(solution)/shard_map/all_gather | solution.py:630
  27.8 9.9 %all_gather.22.down_ref = bf16[8,16,1536]{2,1,0:T(8,128)(2,1)} all-gather(bf16[2,16,1536]{2,1,0:T(8,128)(2,1)} %bitcast.20), channel_id=1, replica_groups=mesh['seq'=8,'dp'=4] {'dp'}, dimensions={0}, use_global_device_ids=true | all-gather | bytes 491520 | tf_op jit(solution)/shard_map/all_gather | solution.py:630
  37.7 1.2 negate_bitcast_fusion.rate_ref
  38.9 17.3 %all_gather.20.up_ref = bf16[8,16,3352]{2,1,0:T(8,128)(2,1)} all-gather(bf16[2,16,3352]{2,1,0:T(8,128)(2,1)} %param.29), channel_id=1, replica_groups=mesh['seq'=8,'dp'=4] {'dp'}, dimensions={0}, use_global_device_ids=true | all-gather | bytes 1072640 | tf_op jit(solution)/shard_map/all_gather | solution.py:630
  56.2 6.5 %all_gather.23.up_ref = bf16[8,16,768]{2,1,0:T(8,128)(2,1)} all-gather(bf16[2,16,768]{2,1,0:T(8,128)(2,1)} %param.31), channel_id=1, replica_groups=mesh['seq'=8,'dp'=4] {'dp'}, dimensions={0}, use_global_device_ids=true | all-gather | bytes 245760 | tf_op jit(solution)/shard_map/all_gather | solution.py:630
  63.2 45.1 %project.1 = (bf16[2,768,16]{2,1,0:T(8,128)(2,1)}, bf16[2,768,1536]{2,1,0:T(8,128)(2,1)}, bf16[2,768,1792]{2,1,0:T(8,128)(2,1)}, bf16[2,768,1792]{2,1,0:T(8,128)...) custom-call(s32[2]{0:T(128)} %bitcast.22, ...), custom_call_target="tpu_custom_call" | custom-call | tf_op jit(solution)/shard_map/project/pallas_call | solution.py:572
  108.3 25.5 %state_carry.1.start_ref = bf16[2,128,1536]{2,1,0:T(8,128)(2,1)} custom-call(bf16[2,128,1536]{2,1,0:T(8,128)(2,1)} %get-tuple-element.42.tot_ref, f32[2,8,1536]{2,1,0:T(8,128)} %get-tuple-element.43.dec_ref.dtot_ref), custom_call_target="tpu_custom_call" | custom-call | tf_op jit(solution)/shard_map/state_carry/pallas_call | solution.py:548
  133.9 10.7 %intra.1.y_ref = bf16[2,768,1536]{2,1,0:T(8,128)(2,1)} custom-call(bf16[2,768,1792]{2,1,0:T(8,128)(2,1)} %get-tuple-element.36.xbc_ref, f32[2,768,24]{2,1,0:T(8,128)} %get-tuple-element.37.wid_ref, f32[2,768,24]{2,1,0:T(8,128)} %get-tuple-element.38.cum_ref), custom_call_target="tpu_custom_call" | custom-call | tf_op jit(solution)/shard_map/intra/pallas_call | solution.py:572
  144.6 43.1 %output.1 = (bf16[2,768,768]{2,1,0:T(8,128)(2,1)}, bf16[2,768,1536]{2,1,0:T(8,128)(2,1)}, bf16[2,768,1536]{2,1,0:T(8,128)(2,1)}, f32[2,768,128]{2,1,0:T(8,128)},...) custom-call(s32[2]{0:T(128)} %bitcast.25, ...), custom_call_target="tpu_custom_call" | custom-call | tf_op jit(solution)/shard_map/output/pallas_call | solution.py:572
  188.6 0.9 convert.15
  189.6 39.0 %adjoint_carry.1.end_ref = bf16[2,128,1536]{2,1,0:T(8,128)(2,1)} custom-call(bf16[2,128,1536]{2,1,0:T(8,128)(2,1)} %get-tuple-element.55.tot_ref, f32[2,8,1536]{2,1,0:T(8,128)} %get-tuple-element.43.dec_ref.dtot_ref), custom_call_target="tpu_custom_call" | custom-call | tf_op jit(solution)/shard_map/adjoint_carry/pallas_call | solution.py:548
  228.6 13.6 %intra_back.1 = (bf16[2,768,1536]{2,1,0:T(8,128)(2,1)}, f32[2,768,128]{2,1,0:T(8,128)}, f32[2,768,128]{2,1,0:T(8,128)}) custom-call(bf16[2,768,1792]{2,1,0:T(8,128)(2,1)} %get-tuple-element.36.xbc_ref, f32[2,768,24]{2,1,0:T(8,128)} %get-tuple-element.37.wid_ref, f32[2,768,24]{2,1,0:T(8,128)} %get-tuple-element.38.cum_ref, ...), custom_call_target="tpu_custom_call" | custom-call | tf_op jit(solution)/shard_map/intra_back/pallas_call | solution.py:572
  242.2 21.3 %adjoint.1 = (bf16[2,768,1792]{2,1,0:T(8,128)(2,1)}, f32[2,768,24]{2,1,0:T(8,128)}) custom-call(bf16[2,768,1792]{2,1,0:T(8,128)(2,1)} %get-tuple-element.36.xbc_ref, bf16[2,768,1792]{2,1,0:T(8,128)(2,1)} %get-tuple-element.45.dact_ref, f32[2,768,24]{2,1,0:T(8,128)} %get-tuple-element.37.wid_ref, f32[2,768,24]{2,1,0:T(8,128)} %get-tuple-element.38.cum_ref, ...), custom_call_target="tpu_custom_call" | custom-call | tf_op jit(solution)/shard_map/adjoint/pallas_call | solution.py:572
  264.4 1.3 collective-permute-start.1
  266.3 4.8 %collective-permute-done.1.rim_ref = bf16[2,16,1792]{2,1,0:T(8,128)(2,1)S(1)} collective-permute-done((bf16[2,16,1792]{2,1,0:T(8,128)(2,1)S(1)}, bf16[2,16,1792]{2,1,0:T(8,128)(2,1)S(1)}, u32[]{:S(2)}, u32[]{:S(2)}) %collective-permute-start.1) | collective-permute-done | bytes 114720 | tf_op jit(solution)/shard_map/ppermute | solution.py:795
  271.8 34.8 %input.1 = (bf16[2,768,768]{2,1,0:T(8,128)(2,1)}, f32[2,16,3352]{2,1,0:T(8,128)}, f32[2,16,768]{2,1,0:T(8,128)}) custom-call(s32[2]{0:T(128)} %bitcast.23, bf16[2,768,1792]{2,1,0:T(8,128)(2,1)} %get-tuple-element.57.gpre_ref, bf16[2,16,1792]{2,1,0:T(8,128)(2,1)} %copy-done, bf16[2,768,1536]{2,1,0:T(8,128)(2,1)} %get-tuple-element.58.ggate_ref, ...), custom_call_target="tpu_custom_call" | custom-call | tf_op jit(solution)/shard_map/input/pallas_call | solution.py:572
  307.5 1.0 convert.12
  309.4 71.5 %all-reduce.3.cloned.1.call-done = (bf16[2,16,4120]{2,1,0:T(8,128)(2,1)}, bf16[2,16,2304]{2,1,0:T(8,128)(2,1)}) async-done(((bf16[2,16,4120]{2,1,0:T(8,128)(2,1)}, bf16[2,16,2304]{2,1,0:T(8,128)(2,1)}), (bf16[2,16,4120]{2,1,0:T(8,128)(2,1)}, bf16[2,16,2304]{2,1,0:T(8,128)(2,1)})) %all-reduce.3.cloned.1.call-update) | async-done | bytes 411152 | tf_op jit(solution)/shard_map/psum | solution.py:829
  380.9 1.3 convolution_convert_fusion.1
  382.2 0.9 copy.32
  383.3 1.5 convolution_convert_fusion
  384.8 1.1 copy.30
  385.9 18.9 %reduce-scatter.5.cloned.1.call-done = bf16[2,16,2304]{2,1,0:T(8,128)(2,1)} async-done(((bf16[8,16,2304]{2,1,0:T(8,128)(2,1)}), bf16[2,16,2304]{2,1,0:T(8,128)(2,1)}) %reduce-scatter.5.cloned.1.call-update) | async-done | bytes 147472 | tf_op jit(solution)/shard_map/reduce_scatter | solution.py:832
  404.8 1.4 slice.27
  406.2 0.9 convert_element_type.19
  407.9 24.6 %reduce-scatter.3.cloned.1.call-done = bf16[2,16,4120]{2,1,0:T(8,128)(2,1)} async-done(((bf16[8,16,4120]{2,1,0:T(8,128)(2,1)}), bf16[2,16,4120]{2,1,0:T(8,128)(2,1)}) %reduce-scatter.3.cloned.1.call-update) | async-done | bytes 263696 | tf_op jit(solution)/shard_map/reduce_scatter | solution.py:832
  432.5 1.0 convert_element_type.17
  434.2 1.7 slice.25
  (31 shorter events, 10.7 us)
Async XLA Ops:
  7.2 55.5 %all-gather.3.cloned.1.call-start = ((), (), s32[]{:S(2)}) async-start(), calls=%async_computation.2 | async-start | bytes 6635520 | tf_op jit(solution)/shard_map/all_gather | solution.py:630
  7.9 136.7 %all-gather.5.cloned.1.call-start = ((), (), s32[]{:S(2)}) async-start(), calls=%async_computation.3 | async-start | bytes 2949120 | tf_op jit(solution)/shard_map/all_gather | solution.py:630
  8.6 372.2 %all-reduce.3.cloned.1.call-start = ((), (), s32[]{:S(2)}) async-start(), calls=%async_computation.6 | async-start | bytes 835584 | tf_op jit(solution)/shard_map/psum | solution.py:829
  9.5 53.1 %collective-permute-start = (bf16[2,16,768]{2,1,0:T(8,128)(2,1)S(1)}, bf16[2,16,768]{2,1,0:T(8,128)(2,1)S(1)}, u32[]{:S(2)}, u32[]{:S(2)}) collective-permute-start(bf16[2,16,768]{2,1,0:T(8,128)(2,1)S(1)} %slice.18), channel_id=1, source_target_pairs={{0,4},{4,8},{8,12},{12,16},{16,20},{20,24},{24,28},{1,5},{5,9},{9,... | collective-permute-start | bytes 147464 | tf_op jit(solution)/shard_map/ppermute | solution.py:627
  62.6 0.6 copy-start.1
  264.4 6.7 %collective-permute-start.1 = (bf16[2,16,1792]{2,1,0:T(8,128)(2,1)S(1)}, bf16[2,16,1792]{2,1,0:T(8,128)(2,1)S(1)}, u32[]{:S(2)}, u32[]{:S(2)}) collective-permute-start(bf16[2,16,1792]{2,1,0:T(8,128)(2,1)S(1)} %slice.19), channel_id=1, source_target_pairs={{4,0},{8,4},{12,8},{16,12},{20,16},{24,20},{28,24},{5,1},{9,5},{13... | collective-permute-start | bytes 344072 | tf_op jit(solution)/shard_map/ppermute | solution.py:795
  271.1 0.6 copy-start
  271.8 109.1 %copy-start.3 = (s32[2,1]{0,1:T(1,128)S(1)}, s32[2,1]{0,1:T(1,128)}, u32[]{:S(2)}) copy-start(s32[2,1]{0,1:T(1,128)} %param.33) | copy-start | bytes 28
  271.8 111.5 %copy-start.2 = (s32[2,1]{0,1:T(1,128)S(1)}, s32[2,1]{0,1:T(1,128)}, u32[]{:S(2)}) copy-start(s32[2,1]{0,1:T(1,128)} %param.32) | copy-start | bytes 28
  309.3 95.5 %reduce-scatter.5.cloned.1.call-start = ((), (), s32[]{:S(2)}) async-start(), calls=%async_computation.5 | async-start | bytes 737280 | tf_op jit(solution)/shard_map/reduce_scatter | solution.py:832
  383.2 49.3 %reduce-scatter.3.cloned.1.call-start = ((), (), s32[]{:S(2)}) async-start(), calls=%async_computation.4 | async-start | bytes 1351680 | tf_op jit(solution)/shard_map/reduce_scatter | solution.py:832
Sparse Core Ops, SparseCore 0:
  9.6 51.3 all-gather.2
  62.5 24.1 all-gather.4
  309.4 71.3 all-reduce.2
  383.4 21.3 reduce-scatter.4
  407.3 25.1 reduce-scatter.2

commit v2 on v1

--- a/solution.py
+++ b/solution.py
@@ -17,6 +17,7 @@
 F32 = jnp.float32
 MESH = pl.DeviceIdType.MESH
 VMEM_LIMIT = 56 * 2**20
+CONV_BIAS, GATE_GAIN, NORM_GAIN, SKIP, STEP_BIAS, RATE = (slice(4 + n, 5 + n) for n in range(6))
 
 
 def nn(a, b):
@@ -93,17 +94,16 @@
 
 
 def project_kernel(
-    idx_ref, res_ref, halo_ref, win_ref, down_ref, up_ref, gain_ref, cw_ref, cb_ref, sb_ref, rate_ref,
-    low_ref, gate_ref, xbc_ref, dact_ref, wid_ref, cum_ref, sig_ref, sloc_ref, dpre_ref, tot_ref, dtot_ref,
+    idx_ref, res_ref, halo_ref, win_ref, down_ref, up_ref, par_ref,
+    low_ref, xbc_ref, dact_ref, wid_ref, cum_ref, sig_ref, sloc_ref, dpre_ref, tot_ref, dtot_ref,
     nrm, ext, state, run, onehot,
 ):
     blk = pl.program_id(1)
     rows = res_ref.shape[1]
     heads, inner = onehot.shape
-    mixer = cb_ref.shape[1]
+    mixer = xbc_ref.shape[2]
     states = (mixer - inner) // 2
-    proj = win_ref.shape[1]
-    gain = gain_ref[...]
+    gain = par_ref[NORM_GAIN, : res_ref.shape[2]]
 
     @pl.when(blk == 0)
     def _():
@@ -116,11 +116,14 @@
         low_first = nt(first, down_ref[0]).astype(BF)
         for at in range(0, mixer, 2 * LANES):
             cols = slice(inner + at, inner + at + 2 * LANES)
-            ext[0:RIM, at : at + 2 * LANES] = nn(first, win_ref[:, cols]) + nn(low_first, up_ref[0, :, cols])
+            t = slice(at, at + 2 * LANES)
+            v2 = nn(first, win_ref[:, t]) + nn(low_first, up_ref[0, :, cols])
+            ext[at // LANES, 0:RIM, :] = v2[:, :LANES]
+            ext[at // LANES + 1, 0:RIM, :] = v2[:, LANES:]
 
     @pl.when(blk > 0)
     def _():
-        ext[0:RIM, :] = ext[rows : rows + RIM, :]
+        ext[:, 0:RIM, :] = ext[:, rows : rows + RIM, :]
 
     write_normed(nrm, res_ref.at[0], gain, 32)
     normed = nrm[...]
@@ -128,29 +131,29 @@
     low_ref[0] = low
     for at in range(0, mixer, 2 * LANES):
         cols = slice(inner + at, inner + at + 2 * LANES)
-        ext[RIM : RIM + rows, at : at + 2 * LANES] = nn(normed, win_ref[:, cols]) + nn(low, up_ref[0, :, cols])
-    cols = slice(inner + mixer, proj)
-    raw = nn(normed, win_ref[:, cols]) + nn(low, up_ref[0, :, cols]) + sb_ref[...]
-    for at in range(0, inner, 2 * LANES):
-        cols = slice(at, at + 2 * LANES)
-        gate_ref[0, :, cols] = (nn(normed, win_ref[:, cols]) + nn(low, up_ref[0, :, cols])).astype(BF)
+        t = slice(at, at + 2 * LANES)
+        v2 = nn(normed, win_ref[:, t]) + nn(low, up_ref[0, :, cols])
+        ext[at // LANES, RIM : RIM + rows, :] = v2[:, :LANES]
+        ext[at // LANES + 1, RIM : RIM + rows, :] = v2[:, LANES:]
+    cols = slice(inner + mixer, inner + mixer + heads)
+    raw = nn(normed, win_ref[:, mixer : mixer + heads]) + nn(low, up_ref[0, :, cols]) + par_ref[STEP_BIAS, :heads]
     sig_ref[0] = sigmoid(raw)
     widths = jnp.maximum(raw, 0.0) + jnp.log1p(jnp.exp(-jnp.abs(raw)))
     wid_ref[0] = widths
     ones = lower_ones(CHUNK)
     for j in range(rows // CHUNK):
         for t in tiles(mixer):
-            pre = cb_ref[:, t]
+            pre = par_ref[CONV_BIAS, t]
             for k in range(4):
                 at = RIM - 3 + k + j * CHUNK
-                pre = pre + cw_ref[k : k + 1, t] * ext[at : at + CHUNK, t]
+                pre = pre + par_ref[k : k + 1, t] * ext[t.start // LANES, at : at + CHUNK, :]
             s = sigmoid(pre)
             act = pre * s
             xbc_ref[0, rows_of(j), t] = act.astype(BF)
             dact_ref[0, rows_of(j), t] = (s + act * (1.0 - s)).astype(BF)
     for j in range(rows // CHUNK):
         w = widths[rows_of(j)]
-        c = exact(ones, w * rate_ref[...])
+        c = exact(ones, w * par_ref[RATE, :heads])
         cum_ref[0, rows_of(j)] = c
         last = c[CHUNK - 1 : CHUNK]
         tail = spread(jnp.exp(last - c) * w, onehot[...])
@@ -174,8 +177,16 @@
         dtot_ref[0] = spread(jnp.exp(run[...]), onehot[...])
 
 
-def intra_kernel(xbc_ref, wid_ref, cum_ref, y_ref, onehot):
+def intra_kernel(
+    idx_ref, xbc_ref, wid_ref, cum_ref, res_ref, low_ref, win_ref, up_ref, par_ref, y_ref, gate_ref, nrm, onehot
+):
     heads, inner = onehot.shape
+    write_normed(nrm, res_ref.at[0], par_ref[NORM_GAIN, : res_ref.shape[2]], 32)
+    normed, low = nrm[...], low_ref[0]
+    for at in range(0, inner, 2 * LANES):
+        t = slice(at, at + 2 * LANES)
+        gate_ref[0, :, t] = (nn(normed, win_ref[:, t]) + nn(low, up_ref[0, :, t])).astype(BF)
+
     states = (xbc_ref.shape[2] - inner) // 2
     width = inner // heads
 
@@ -206,7 +217,7 @@
 
 def output_kernel(
     idx_ref, y_ref, xbc_ref, gate_ref, cum_ref, sloc_ref, dpre_ref, tot_ref, dtot_ref, start_ref,
-    res_ref, cot_ref, wout_ref, down_ref, up_ref, ggain_ref, skip_ref,
+    res_ref, cot_ref, wout_ref, down_ref, up_ref, par_ref,
     out_ref, ggate_ref, dy_ref, dreads_ref, rowt_ref, gloc_ref, dsuf_ref, snext_ref, gown_ref, gup_ref, gdown_ref,
     onehot, snow, cur, adj, run, yp, gated, nout, gno, prod,
 ):
@@ -244,7 +255,7 @@
     for j in range(chunks):
         total = jnp.zeros((CHUNK, LANES), F32)
         for t in tiles(inner):
-            y = yp[rows_of(j), t] + skip_ref[:, t] * xbc_ref[0, rows_of(j), t].astype(F32)
+            y = yp[rows_of(j), t] + par_ref[SKIP, t] * xbc_ref[0, rows_of(j), t].astype(F32)
             g = gate_ref[0, rows_of(j), t].astype(F32)
             v = y * (g * sigmoid(g))
             gated[rows_of(j), t] = v
@@ -252,7 +263,7 @@
         r = lax.rsqrt(jnp.sum(total, axis=1, keepdims=True) * (1.0 / inner) + EPS)
         scale.append(r)
         for t in tiles(inner):
-            nout[rows_of(j), t] = (gated[rows_of(j), t] * r * ggain_ref[:, t]).astype(BF)
+            nout[rows_of(j), t] = (gated[rows_of(j), t] * r * par_ref[GATE_GAIN, t]).astype(BF)
 
     normed_out = nout[...]
     cot = cot_ref[0]
@@ -271,7 +282,7 @@
     for j in range(chunks):
         total = jnp.zeros((CHUNK, LANES), F32)
         for t in tiles(inner):
-            q = gno[rows_of(j), t] * ggain_ref[:, t]
+            q = gno[rows_of(j), t] * par_ref[GATE_GAIN, t]
             gno[rows_of(j), t] = q
             total = total + gated[rows_of(j), t] * q
         r = scale[j]
@@ -279,7 +290,7 @@
         for t in tiles(inner):
             grad = r * gno[rows_of(j), t] - gated[rows_of(j), t] * shrink
             y_local = yp[rows_of(j), t]
-            y = y_local + skip_ref[:, t] * xbc_ref[0, rows_of(j), t].astype(F32)
+            y = y_local + par_ref[SKIP, t] * xbc_ref[0, rows_of(j), t].astype(F32)
             g = gate_ref[0, rows_of(j), t].astype(F32)
             s = sigmoid(g)
             dy = grad * (g * s)
@@ -353,7 +364,7 @@
 
 def adjoint_kernel(
     xbc_ref, dact_ref, wid_ref, cum_ref, sig_ref, dy_ref, z_ref, dinputs_ref, dreads_ref, rowt_ref,
-    gloc_ref, dsuf_ref, end_ref, snext_ref, skip_ref, rate_ref,
+    gloc_ref, dsuf_ref, end_ref, snext_ref, par_ref,
     gpre_ref, graw_ref,
     onehot, adj, prod,
 ):
@@ -386,7 +397,7 @@
             x = xbc_ref[0, at, t].astype(F32)
             z = z_ref[0, at, t].astype(F32) + tail[:, t] * carried[:, t]
             prod[:, t] = (x * z).astype(BF)
-            grad = wide[:, t] * z + skip_ref[:, t] * dy_ref[0, at, t].astype(F32)
+            grad = wide[:, t] * z + par_ref[SKIP, t] * dy_ref[0, at, t].astype(F32)
             gpre_ref[0, at, t] = (grad * dact_ref[0, at, t].astype(F32)).astype(BF)
             weighted.append((x * (wide[:, t] * tail[:, t])).astype(BF))
         dinputs = dinputs_ref[0, at] + nt(jnp.concatenate(weighted, axis=1), adj[...])
@@ -396,11 +407,11 @@
         gpre_ref[0, at, t] = (dreads_ref[0, at] * dact_ref[0, at, t].astype(F32)).astype(BF)
         direct = nt(prod[...], onehot[...])
         grad_rate = held + exact(upper_ones(CHUNK), rowt_ref[0, at] - w * direct)
-        graw_ref[0, at] = (direct + rate_ref[...] * grad_rate) * sig_ref[0, at]
+        graw_ref[0, at] = (direct + par_ref[RATE, :heads] * grad_rate) * sig_ref[0, at]
 
 
 def input_kernel(
-    idx_ref, gpre_ref, rim_ref, ggate_ref, graw_ref, low_ref, res_ref, cot_ref, win_ref, down_ref, up_ref, gain_ref, cw_ref,
+    idx_ref, gpre_ref, rim_ref, ggate_ref, graw_ref, low_ref, res_ref, cot_ref, wgate_ref, win_ref, down_ref, up_ref, par_ref,
     gin_ref, gup_ref, gdown_ref,
     ext, gp, gn, nrm,
 ):
@@ -408,28 +419,30 @@
     rows = res_ref.shape[1]
     inner = ggate_ref.shape[2]
     mixer = gpre_ref.shape[2]
-    proj = win_ref.shape[1]
+    proj = inner + win_ref.shape[1]
     model = res_ref.shape[2]
+    gain = par_ref[NORM_GAIN, :model]
 
     @pl.when(blk == 0)
     def _():
-        ext[rows : rows + RIM, :] = rim_ref[0].astype(F32)
+        for n, t in enumerate(tiles(mixer)):
+            ext[n, rows : rows + RIM, :] = rim_ref[0, :, t].astype(F32)
         gup_ref[...] = jnp.zeros_like(gup_ref)
         gdown_ref[...] = jnp.zeros_like(gdown_ref)
 
     @pl.when(blk > 0)
     def _():
-        ext[rows : rows + RIM, :] = ext[0:RIM, :]
+        ext[:, rows : rows + RIM, :] = ext[:, 0:RIM, :]
 
     for j in range(rows // CHUNK):
         for t in tiles(mixer):
-            ext[rows_of(j), t] = gpre_ref[0, rows_of(j), t].astype(F32)
+            ext[t.start // LANES, rows_of(j), :] = gpre_ref[0, rows_of(j), t].astype(F32)
     for j in range(rows // CHUNK):
         for t in tiles(mixer):
             total = None
             for k in range(4):
                 at = 3 - k + j * CHUNK
-                term = cw_ref[k : k + 1, t] * ext[at : at + CHUNK, t]
+                term = par_ref[k : k + 1, t] * ext[t.start // LANES, at : at + CHUNK, :]
                 total = term if total is None else total + term
             gp[rows_of(j), inner + t.start : inner + t.stop] = total.astype(BF)
     gp[:, :inner] = ggate_ref[0]
@@ -440,14 +453,15 @@
     grad_low = (nt(grads, up_ref[0, :, whole]) + nt(grads_rest, up_ref[0, :, rest])).astype(BF)
     for at in range(0, model, 2 * LANES):
         t = slice(at, at + 2 * LANES)
-        gn[:, t] = nt(grads, win_ref[t, whole]) + nt(grads_rest, win_ref[t, rest]) + nn(grad_low, down_ref[0, :, t])
+        part = nt(gp[:, :inner], wgate_ref[t, :]) + nt(gp[:, inner : inner + mixer], win_ref[t, :mixer])
+        gn[:, t] = part + nt(grads_rest, win_ref[t, mixer:]) + nn(grad_low, down_ref[0, :, t])
 
     def body(k, _):
         at = pl.ds(pl.multiple_of(k * 32, 32), 32)
         v = res_ref[0, at, :].astype(F32)
         u = lax.rsqrt(jnp.mean(v * v, axis=1, keepdims=True) + EPS)
-        nrm[at, :] = (v * u * gain_ref[...]).astype(BF)
-        w = gn[at, :] * gain_ref[...]
+        nrm[at, :] = (v * u * gain).astype(BF)
+        w = gn[at, :] * gain
         m = jnp.mean(v * w, axis=1, keepdims=True)
         gin_ref[0, at, :] = (cot_ref[0, at, :].astype(F32) + u * w - v * (u * u * u * m)).astype(BF)
         return 0
@@ -564,6 +578,281 @@
         ),
         name="adjoint_carry" if backwards else "state_carry",
     )(total, decay)
+
+
+def gather_kernel(count, seq_count, res_ref, win_ref, ad_ref, win_out, ad_out, halo_out, sems, local):
+    dp = lax.axis_index("dp")
+    seq = lax.axis_index("seq")
+    side = lax.rem(seq, 2)
+    partner = (seq + 1 - 2 * side, dp)
+    sibling = (seq, dp + 1 - 2 * lax.rem(dp, 2))
+    later = (lax.rem(seq + 1, seq_count), dp)
+    earlier = (lax.rem(seq + seq_count - 1, seq_count), dp)
+    chips = count // 2
+    barrier = pltpu.get_barrier_semaphore()
+    others = [(seq, lax.rem(dp + 2 * k, count)) for k in range(1, chips)]
+    for other in [partner, sibling, later, earlier] + others:
+        pl.semaphore_signal(barrier, inc=1, device_id=other, device_id_type=MESH)
+    pl.semaphore_wait(barrier, 4 + len(others))
+
+    def send(src, dst, to, *at):
+        return pltpu.make_async_remote_copy(
+            src_ref=src, dst_ref=dst, send_sem=sems.at[(0,) + at], recv_sem=sems.at[(1,) + at],
+            device_id=to, device_id_type=MESH,
+        )
+
+    share, width = win_ref.shape[0], win_out.shape[1]
+    half = share // 2
+    owned = ad_ref.shape[1]
+    split = width // 2 // LANES * LANES
+    start = win_ref.shape[1] - width
+
+    def columns(at, wide, piece):
+        def source(which):
+            return win_ref.at[pl.ds(pl.multiple_of(which * half, 16), half), pl.ds(start + at, wide)]
+
+        def target(owner, which):
+            return win_out.at[pl.ds(pl.multiple_of(owner * share + which * half, 16), half), pl.ds(at, wide)]
+
+        return source, target, piece
+
+    pieces = [
+        (lambda which: ad_ref.at[which], lambda owner, which: ad_out.at[which, pl.ds(owner * owned, owned)], 0),
+        columns(0, split, 1),
+        columns(split, width - split, 2),
+    ]
+    out_going = []
+    for source, target, n in pieces:
+        for k in range(1, chips):
+            copy = send(source(side), target(dp, side), others[k - 1], 0, k, n)
+            copy.start()
+            out_going.append(copy)
+    rim = halo_out.shape[1]
+    edge = send(res_ref.at[:, pl.ds(res_ref.shape[1] - rim, rim)], halo_out, later, 6, 0, 0)
+
+    @pl.when(seq < seq_count - 1)
+    def _():
+        edge.start()
+
+    kept = []
+    for source, target, n in pieces:
+        for which in range(2):
+            copy = pltpu.make_async_copy(source(which), target(dp, which), local.at[which, n])
+            copy.start()
+            kept.append(copy)
+            copy = send(source(which), target(dp, which), sibling, 3 + which, 0, n)
+            copy.start()
+            kept.append(copy)
+    passed = []
+    for source, target, n in pieces:
+        for k in range(1, chips):
+            owner = lax.rem(dp - 2 * k + count, count)
+            here = target(owner, side)
+            send(source(side), here, others[k - 1], 0, k, n).wait_recv()
+            across = send(here, here, partner, 1, k, n)
+            over = send(here, here, sibling, 2, k, n)
+            across.start()
+            over.start()
+            passed += [(across, False), (over, True)]
+    for source, target, n in pieces:
+        for k in range(1, chips):
+            owner = lax.rem(dp - 2 * k + count, count)
+            there = target(owner, 1 - side)
+            send(there, there, partner, 1, k, n).wait_recv()
+            over = send(there, there, sibling, 5, k, n)
+            over.start()
+            passed.append((over, True))
+    for copy in out_going:
+        copy.wait_send()
+    for copy in kept:
+        copy.wait()
+    for copy, both in passed:
+        copy.wait_send()
+        if both:
+            copy.wait_recv()
+
+    @pl.when(seq == 0)
+    def _():
+        halo_out[...] = jnp.zeros_like(halo_out)
+
+    @pl.when(seq > 0)
+    def _():
+        edge.wait_recv()
+
+    @pl.when(seq < seq_count - 1)
+    def _():
+        edge.wait_send()
+
+
+def gather(residual, in_weight, packed, first, count, seq_count):
+    pieces = 3
+    return pl.pallas_call(
+        functools.partial(gather_kernel, count, seq_count),
+        out_shape=[
+            jax.ShapeDtypeStruct((in_weight.shape[0] * count, in_weight.shape[1] - first), BF),
+            jax.ShapeDtypeStruct((2, packed.shape[1] * count) + packed.shape[2:], BF),
+            jax.ShapeDtypeStruct((residual.shape[0], RIM, residual.shape[2]), BF),
+        ],
+        in_specs=[pl.BlockSpec(memory_space=pl.ANY)] * 3,
+        out_specs=[pl.BlockSpec(memory_space=pltpu.VMEM)] * 3,
+        scratch_shapes=[
+            pltpu.SemaphoreType.DMA((2, 7, count // 2, pieces)),
+            pltpu.SemaphoreType.DMA((2, pieces)),
+        ],
+        compiler_params=pltpu.CompilerParams(collective_id=3, has_side_effects=True, vmem_limit_bytes=VMEM_LIMIT),
+        name="gather",
+    )(residual, in_weight, packed)
+
+
+def sums_kernel(
+    count, dp_count, up_in_ref, down_in_ref, up_out_ref, down_out_ref, coef_ref,
+    final,
+    pack, half, half_sent, first, line, red, give, owners, sems,
+):
+    dp = lax.axis_index("dp")
+    seq = lax.axis_index("seq")
+    pair, side = seq // 2, lax.rem(seq, 2)
+    pairs = count // 2
+    share = red.shape[0]
+    seqs, rank, _ = up_in_ref.shape
+    owned = final.shape[1] // rank
+    partner = (seq + 1 - 2 * side, dp)
+    along = [(lax.rem(pair + k, pairs) * 2 + side, dp) for k in range(1, pairs)]
+    across = [(seq, lax.rem(dp + k, dp_count)) for k in range(1, dp_count)]
+    barrier = pltpu.get_barrier_semaphore()
+    for other in [partner] + along + across:
+        pl.semaphore_signal(barrier, inc=1, device_id=other, device_id_type=MESH)
+
+    places = []
+    for n, ref in enumerate((up_in_ref, down_in_ref, up_out_ref, down_out_ref)):
+        if n == 2:
+            in_tiles = len(places)
+        places += [(ref, t.start, t.stop - t.start) for t in tiles(ref.shape[2])]
+    for n, (ref, at, wide) in enumerate(places):
+        for s in range(seqs):
+            v = ref[s, :, at : at + wide]
+            if wide < LANES:
+                v = jnp.concatenate([v, jnp.zeros((rank, LANES - wide), F32)], axis=1)
+            pack[n, s * rank : (s + 1) * rank, :] = v.astype(BF)
+    for n in range(len(places), pack.shape[0]):
+        pack[n] = jnp.zeros_like(pack[n])
+    pl.semaphore_wait(barrier, 1 + len(along) + len(across))
+
+    def send(src, dst, to, *at):
+        return pltpu.make_async_remote_copy(
+            src_ref=src, dst_ref=dst, send_sem=sems.at[(0,) + at], recv_sem=sems.at[(1,) + at],
+            device_id=to, device_id_type=MESH,
+        )
+
+    wide = pairs * share
+    copy = send(pack.at[pl.ds((1 - side) * wide, wide)], first, partner, 0, 0)
+    copy.start()
+    copy.wait()
+
+    def add(n, _):
+        v = pack[side * wide + n].astype(F32) + first[n].astype(F32)
+        half[n] = v
+        half_sent[n] = v.astype(BF)
+        return 0
+
+    lax.fori_loop(0, wide, add, 0)
+    copies = []
+    for k in range(1, pairs):
+        there = lax.rem(pair + k, pairs)
+        copies.append(send(half_sent.at[pl.ds(there * share, share)], line.at[k - 1], along[k - 1], 1, k))
+        copies[-1].start()
+    for copy in copies:
+        copy.wait()
+    for n in range(share):
+        v = half[pair * share + n]
+        for k in range(pairs - 1):
+            v = v + line[k, n].astype(F32)
+        red[n] = v
+
+    def part(owner, n, a):
+        tile = (side * pairs + pair) * share + n
+        kind = jnp.where(tile < in_tiles, 0, 1)
+        total = None
+        for s in range(seqs):
+            c = coef_ref[kind, (owner * owned + a) * seqs + s]
+            term = c * red[n, s * rank : (s + 1) * rank, :]
+            total = term if total is None else total + term
+        return total
+
+    copies = []
+    for k in range(1, dp_count):
+        owner = lax.rem(dp + k, dp_count)
+        for n in range(share):
+            for a in range(owned):
+                give[k - 1, n, a * rank : (a + 1) * rank, :] = part(owner, n, a).astype(BF)
+        copies.append(send(give.at[k - 1], owners.at[k - 1], across[k - 1], 2, k))
+        copies[-1].start()
+    mine = [[part(dp, n, a) for a in range(owned)] for n in range(share)]
+    for copy in copies:
+        copy.wait()
+    here = pl.ds((side * pairs + pair) * share, share)
+    for n in range(share):
+        for a in range(owned):
+            v = mine[n][a]
+            for k in range(dp_count - 1):
+                v = v + owners[k, n, a * rank : (a + 1) * rank, :].astype(F32)
+            final[(side * pairs + pair) * share + n, a * rank : (a + 1) * rank, :] = v.astype(BF)
+    copies = []
+    for k in range(1, pairs):
+        copies.append(send(final.at[here], final.at[here], along[k - 1], 3, k))
+        copies[-1].start()
+    for copy in copies:
+        copy.wait()
+    ours = final.at[pl.ds(side * wide, wide)]
+    copy = send(ours, ours, partner, 4, 0)
+    copy.start()
+    copy.wait()
+
+def unpack_kernel(final, up_in_out, down_in_out, up_out_out, down_out_out):
+    owned, rank, _ = up_in_out.shape
+    n = 0
+    for out in (up_in_out, down_in_out, up_out_out, down_out_out):
+        for t in tiles(out.shape[2]):
+            for a in range(owned):
+                out[a, :, t] = final[n, a * rank : (a + 1) * rank, : t.stop - t.start].astype(F32)
+            n += 1
+
+
+def adapter_sums(grads, coef, owned, count, dp_count):
+    up_in, down_in, up_out, down_out = grads
+    seqs, rank, _ = up_in.shape
+    total = sum(-(-g.shape[2] // LANES) for g in grads)
+    share = -(-total // count)
+    pairs = count // 2
+    rows = seqs * rank
+    own_rows = owned * rank
+    whole = pl.BlockSpec(memory_space=pltpu.VMEM)
+    final = pl.pallas_call(
+        functools.partial(sums_kernel, count, dp_count),
+        out_shape=jax.ShapeDtypeStruct((share * count, own_rows, LANES), BF),
+        in_specs=[whole] * 4 + [pl.BlockSpec(memory_space=pltpu.SMEM)],
+        out_specs=whole,
+        scratch_shapes=[
+            pltpu.VMEM((share * count, rows, LANES), BF),
+            pltpu.VMEM((share * pairs, rows, LANES), F32),
+            pltpu.VMEM((share * pairs, rows, LANES), BF),
+            pltpu.VMEM((share * pairs, rows, LANES), BF),
+            pltpu.VMEM((max(pairs - 1, 1), share, rows, LANES), BF),
+            pltpu.VMEM((share, rows, LANES), F32),
+            pltpu.VMEM((max(dp_count - 1, 1), share, own_rows, LANES), BF),
+            pltpu.VMEM((max(dp_count - 1, 1), share, own_rows, LANES), BF),
+            pltpu.SemaphoreType.DMA((2, 5, max(pairs, dp_count))),
+        ],
+        compiler_params=pltpu.CompilerParams(collective_id=4, has_side_effects=True, vmem_limit_bytes=VMEM_LIMIT),
+        name="adapter_sums",
+    )(up_in, down_in, up_out, down_out, coef)
+    return pl.pallas_call(
+        unpack_kernel,
+        out_shape=[jax.ShapeDtypeStruct((owned, rank, g.shape[2]), F32) for g in grads],
+        in_specs=[whole],
+        out_specs=[whole] * 4,
+        name="unpack",
+    )(final)
 
 
 def call(kernel, grid, ins, outs, scratch, name, prefetch=()):
@@ -619,22 +908,21 @@
     blocks = tokens // BLOCK
     per = BLOCK // CHUNK
 
-    rate = -jnp.exp(decay_log)[None, :]
     taps = conv_weight.T
-    gain = norm_gain[None, :]
-    skip_wide = jnp.repeat(skip_gain, inner // heads)[None, :]
+    small = [conv_bias, gate_gain, norm_gain, jnp.repeat(skip_gain, inner // heads), step_bias, -jnp.exp(decay_log)]
+    small = [jnp.pad(v, (0, mixer - v.shape[0]))[None, :] for v in small]
+    params = jnp.concatenate([taps] + small, axis=0)
     route = [(i, i + 1) for i in range(seq_count - 1)]
-    halo = lax.ppermute(residual_in[:, tokens - RIM :], "seq", route)
-
-    def gathered(part):
-        return lax.all_gather(part, "dp", axis=0, tiled=True)
-
-    w_in = gathered(in_weight)
-    w_out = gathered(out_weight)
-    full_in_down = gathered(in_down.transpose(0, 2, 1))
-    full_in_up = gathered(in_up)
-    full_out_down = gathered(out_down.transpose(0, 2, 1))
-    full_out_up = gathered(out_up)
+
+    lanes = -(-proj // LANES) * LANES
+    downs = jnp.concatenate([out_down.transpose(0, 2, 1), in_down.transpose(0, 2, 1), out_up], axis=2)
+    packed = jnp.stack(
+        [jnp.pad(part, ((0, 0), (0, 0), (0, lanes - part.shape[2]))) for part in (in_up, downs)]
+    )
+    w_mix, table, halo = gather(residual_in, in_weight, packed, inner, dp_count, seq_count)
+    w_mix, own_gate, own_out = lax.optimization_barrier((w_mix, in_weight[:, :inner], out_weight))
+    w_gate = lax.all_gather(own_gate, "dp", axis=0, tiled=True)
+    w_out = lax.all_gather(own_out, "dp", axis=0, tiled=True)
 
     grid = (seqs, blocks)
 
@@ -644,8 +932,11 @@
     def by_seq(a):
         return (a, (1,) + a.shape[1:], lambda s, b, *_: (s,) + (0,) * (a.ndim - 1))
 
-    def picked(a):
-        return (a, (1,) + a.shape[1:], lambda s, b, idx, *_: (idx[s],) + (0,) * (a.ndim - 1))
+    def picked(kind, width, at):
+        return (table, (None, 1, rank, width), lambda s, b, idx, *_: (kind, idx[s], 0, at // width))
+
+    in_adapter = [picked(1, model, inner), picked(0, lanes, 0)]
+    out_adapter = [picked(1, inner, 0), picked(1, model, inner + model)]
 
     def by_row(a, turn=False):
         if turn:
@@ -662,24 +953,18 @@
         return (shape, kind, spec[1], spec[2])
 
     row_of = lambda width: (seqs, tokens, width)
-    low, gate, xbc, dact, wid, cum, sig, sloc, dpre, tot, dtot = call(
+    low, xbc, dact, wid, cum, sig, sloc, dpre, tot, dtot = call(
         project_kernel,
         grid,
         [
             by_row(residual_in),
             by_seq(halo),
-            fixed(w_in),
-            picked(full_in_down),
-            picked(full_in_up),
-            fixed(gain),
-            fixed(taps),
-            fixed(conv_bias[None, :]),
-            fixed(step_bias[None, :]),
-            fixed(rate),
+            fixed(w_mix),
+            *in_adapter,
+            fixed(params),
         ],
         [
             out(by_row, row_of(rank), BF),
-            out(by_row, row_of(inner), BF),
             out(by_row, row_of(mixer), BF),
             out(by_row, row_of(mixer), BF),
             out(by_row, row_of(heads), F32),
@@ -692,7 +977,7 @@
         ],
         [
             pltpu.VMEM((BLOCK, model), BF),
-            pltpu.VMEM((BLOCK + RIM, mixer), F32),
+            pltpu.VMEM((mixer // LANES, BLOCK + RIM, LANES), F32),
             pltpu.VMEM((states, inner), F32),
             pltpu.VMEM((8, heads), F32),
             pltpu.VMEM((heads, inner), BF),
@@ -701,13 +986,23 @@
         prefetch=(in_index[:, 0],),
     )
     start = carry(tot, dtot, seq_count, False)
-    (y_intra,) = call(
+    y_intra, gate = call(
         intra_kernel,
         grid,
-        [by_row(xbc), by_row(wid), by_row(cum)],
-        [out(by_row, row_of(inner), BF)],
-        [pltpu.VMEM((heads, inner), BF)],
+        [
+            by_row(xbc),
+            by_row(wid),
+            by_row(cum),
+            by_row(residual_in),
+            by_row(low),
+            fixed(w_gate),
+            in_adapter[1],
+            fixed(params),
+        ],
+        [out(by_row, row_of(inner), BF), out(by_row, row_of(inner), BF)],
+        [pltpu.VMEM((BLOCK, model), BF), pltpu.VMEM((heads, inner), BF)],
         "intra",
+        prefetch=(in_index[:, 0],),
     )
     block_out, ggate, dy, dreads, rowt, gloc, dsuf, snext, gown, gout_up, gout_down = call(
         output_kernel,
@@ -725,10 +1020,8 @@
             by_row(residual_in, True),
             by_row(cotangent, True),
             fixed(w_out),
-            picked(full_out_down),
-            picked(full_out_up),
-            fixed(gate_gain[None, :]),
-            fixed(skip_wide),
+            *out_adapter,
+            fixed(params),
         ],
         [
             out(by_row, row_of(model), BF, True),
@@ -785,8 +1078,7 @@
             by_chunk(dsuf),
             by_seq(end),
             by_chunk(snext),
-            fixed(skip_wide),
-            fixed(rate),
+            fixed(params),
         ],
         [out(by_row, row_of(mixer), BF), out(by_row, row_of(heads), F32)],
         [pltpu.VMEM((heads, inner), BF), pltpu.VMEM((states, inner), BF), pltpu.VMEM((CHUNK, inner), BF)],
@@ -804,11 +1096,10 @@
             by_row(low, True),
             by_row(residual_in, True),
             by_row(cotangent, True),
-            fixed(w_in),
-            picked(full_in_down),
-            picked(full_in_up),
-            fixed(gain),
-            fixed(taps),
+            fixed(w_gate),
+            fixed(w_mix),
+            *in_adapter,
+            fixed(params),
         ],
         [
             out(by_row, row_of(model), BF, True),
@@ -816,7 +1107,7 @@
             out(by_seq, (seqs, rank, model), F32),
         ],
         [
-            pltpu.VMEM((BLOCK + RIM, mixer), F32),
+            pltpu.VMEM((mixer // LANES, BLOCK + RIM, LANES), F32),
             pltpu.VMEM((BLOCK, proj), BF),
             pltpu.VMEM((BLOCK, model), F32),
             pltpu.VMEM((BLOCK, model), BF),
@@ -825,22 +1116,13 @@
         prefetch=(in_index[:, 0],),
     )
 
-    def owned(grads, index):
-        grads = lax.psum(grads.astype(BF), "seq")
-        onehot = (index[:, 0][None, :] == jnp.arange(adapters)[:, None]).astype(BF)
-        mine = jnp.einsum("as,srn->arn", onehot, grads, preferred_element_type=F32).astype(BF)
-        return lax.psum_scatter(mine, "dp", scatter_dimension=0, tiled=True).astype(F32)
-
-    from_in = owned(jnp.concatenate([gin_up, gin_down], axis=2), in_index)
-    from_out = owned(jnp.concatenate([gout_up, gout_down], axis=2), out_index)
-    return (
-        block_out,
-        grad_input,
-        from_in[:, :, proj:].transpose(0, 2, 1),
-        from_in[:, :, :proj],
-        from_out[:, :, model:].transpose(0, 2, 1),
-        from_out[:, :, :model],
+    owners = jnp.arange(adapters)[:, None]
+    coef = jnp.stack([(index[:, 0][None, :] == owners).astype(F32).reshape(-1) for index in (in_index, out_index)])
+    gin_up, gin_down, gout_up, gout_down = adapter_sums(
+        (gin_up, gin_down, gout_up, gout_down), coef, in_down.shape[0], seq_count, dp_count
     )
+    gin_down, gout_down = (g.transpose(0, 2, 1) for g in (gin_down, gout_down))
+    return (block_out, grad_input, gin_down, gin_up, gout_down, gout_up)
 
 
 def solution(mesh):

time: 444 us -> 322 us (0.73)
  waiting for transfers between devices: 121 us -> 5.38 us
  Pallas kernels: 233 us -> 293 us
  blocking collectives: 41.8 us -> 0 us
  local copies, waits for them, and re-layouts: 14.9 us -> 5.21 us
  other arithmetic: 8.36 us -> 2.46 us
  starting transfers between devices: 6.34 us -> 1.36 us
    psum x1 -> x0, waiting for transfers between devices: 71.5 us -> none  [owned(): grads = lax.psum(grads.astype(BF), 'seq')]
    pallas_call x0 -> x3, Pallas kernels: none -> 61.7 us  [the longest x1 31.4 us: adapter_sums(): pl.pallas_call(functools.partial(sums_kernel, count, dp_count), out_shape...]
    reduce_scatter x2 -> x0, waiting for transfers between devices: 43.5 us -> none  [owned(): lax.psum_scatter(mine, 'dp', scatter_dimension=0, tiled=True).astype(F32)]
    all_gather x4 -> x0, blocking collectives: 41.8 us -> none  [gathered(): return lax.all_gather(part, 'dp', axis=0, tiled=True)]
    ppermute x1 -> x0, starting transfers between devices: 4.86 us -> none  [on_device(): halo = lax.ppermute(residual_in[:, tokens - RIM:], 'seq', route)]
    broadcast_in_dim x4 -> x7, local copies, waits for them, and re-layouts: 4.6 us -> 0.11 us  [the longest x1 0.07 us: on_device(): jnp.repeat(skip_gain, inner // heads)]
  transfers between devices with their start and end apart: 7 -> 3, of which waited for: 4 -> 1; matrix products, arithmetic and copies ran while one was open for 3% -> 1% of each run, Pallas kernels for 18% -> 26%
where the time goes in v2:
time: 322 us
  Pallas kernels  293 us (91%)
  between operations  14.3 us (4%)
  waiting for transfers between devices  5.38 us (2%)
  local copies, waits for them, and re-layouts  5.21 us (2%)
    pallas_call x6, Pallas kernels, call(): pl.pallas_call(kernel, out_shape=[jax.ShapeDtypeStruct(shape, kind) for s...  166 us
    pallas_call x2, Pallas kernels, carry(): pl.pallas_call(functools.partial(carry_kernel, count, backwards), out_sha...  65.3 us
    pallas_call x1, Pallas kernels, adapter_sums(): pl.pallas_call(functools.partial(sums_kernel, count, dp_count), out_shape...  31.4 us
    pallas_call x1, Pallas kernels, gather(): pl.pallas_call(functools.partial(gather_kernel, count, seq_count), out_sh...  28.4 us
  transfers between devices with their start and end apart: 3, of which 1 were waited for; matrix products, arithmetic and copies ran while one was open for 1% of the time, Pallas kernels for 26%

profile of v2, /device:TPU:0, one launch (start us, length us, event | category | flops | bytes accessed | tf_op | source)
XLA Modules:
  0.0 321.7 jit_solution(15940333600545057901)
XLA Ops:
  7.2 0.0 copy-start.7
  7.2 0.0 copy-start.9
  7.2 0.0 all-gather.3.cloned.1.call-start
  7.3 1.9 slice.6
  9.2 1.1 fusion.5
  10.3 0.8 pad_maximum_fusion.ad_ref
  11.1 28.4 %gather.1 = (bf16[768,1816]{1,0:T(8,128)(2,1)}, bf16[2,8,16,3456]{3,2,1,0:T(8,128)(2,1)}, bf16[2,16,768]{2,1,0:T(8,128)(2,1)}) custom-call(bf16[2,768,768]{2,1,0:T(8,128)(2,1)} %res_ref.9, bf16[192,3352]{1,0:T(8,128)(2,1)} %win_ref.1, bf16[2,2,16,3456]{3,2,1,0:T(8,128)(2,1)} %pad_maximum_fusion.ad_ref), custom_call_target="tpu_custom_call" | custom-call | tf_op jit(solution)/shard_map/gather/pallas_call | solution.py:689
  39.5 0.0 all-gather.3.cloned.1.call-update
  39.5 0.0 all-gather.5.cloned.1.call-start
  39.5 0.7 all-gather.5.cloned.1.call-update
  40.2 0.1 broadcast_in_dim.25
  40.3 0.1 reshape.71
  40.6 1.3 concatenate.7.par_ref
  41.9 35.0 %project.1 = (bf16[2,768,16]{2,1,0:T(8,128)(2,1)}, bf16[2,768,1792]{2,1,0:T(8,128)(2,1)}, bf16[2,768,1792]{2,1,0:T(8,128)(2,1)}, f32[2,768,24]{2,1,0:T(8,128)}, ...) custom-call(s32[2]{0:T(128)} %bitcast.14, ...), custom_call_target="tpu_custom_call" | custom-call | tf_op jit(solution)/shard_map/project/pallas_call | solution.py:861
  76.9 26.4 %state_carry.1.start_ref = bf16[2,128,1536]{2,1,0:T(8,128)(2,1)} custom-call(bf16[2,128,1536]{2,1,0:T(8,128)(2,1)} %get-tuple-element.60.tot_ref, f32[2,8,1536]{2,1,0:T(8,128)} %get-tuple-element.61.dec_ref.dtot_ref), custom_call_target="tpu_custom_call" | custom-call | tf_op jit(solution)/shard_map/state_carry/pallas_call | solution.py:562
  103.4 0.0 all-gather.3.cloned.1.call-done.win_ref.wgate_ref
  103.4 23.0 %intra.1 = (bf16[2,768,1536]{2,1,0:T(8,128)(2,1)}, bf16[2,768,1536]{2,1,0:T(8,128)(2,1)}) custom-call(s32[2]{0:T(128)} %bitcast.15, bf16[2,768,1792]{2,1,0:T(8,128)(2,1)} %get-tuple-element.51.xbc_ref, f32[2,768,24]{2,1,0:T(8,128)} %get-tuple-element.52.wid_ref, f32[2,768,24]{2,1,0:T(8,128)} %get-tuple-element.53.cum_ref, bf16[2,768,768]{2,1,0:T(8,128)(2,1)} %res_ref.9, ...), custom_call_target="tpu_custom_call" | custom-call | tf_op jit(solution)/shard_map/intra/pallas_call | solution.py:861
  126.4 0.0 all-gather.5.cloned.1.call-done.wout_ref
  126.4 43.1 %output.1 = (bf16[2,768,768]{2,1,0:T(8,128)(2,1)}, bf16[2,768,1536]{2,1,0:T(8,128)(2,1)}, bf16[2,768,1536]{2,1,0:T(8,128)(2,1)}, f32[2,768,128]{2,1,0:T(8,128)},...) custom-call(s32[2]{0:T(128)} %bitcast.18, ...), custom_call_target="tpu_custom_call" | custom-call | tf_op jit(solution)/shard_map/output/pallas_call | solution.py:861
  169.5 38.9 %adjoint_carry.1.end_ref = bf16[2,128,1536]{2,1,0:T(8,128)(2,1)} custom-call(bf16[2,128,1536]{2,1,0:T(8,128)(2,1)} %get-tuple-element.74.tot_ref, f32[2,8,1536]{2,1,0:T(8,128)} %get-tuple-element.61.dec_ref.dtot_ref), custom_call_target="tpu_custom_call" | custom-call | tf_op jit(solution)/shard_map/adjoint_carry/pallas_call | solution.py:562
  208.4 13.6 %intra_back.1 = (bf16[2,768,1536]{2,1,0:T(8,128)(2,1)}, f32[2,768,128]{2,1,0:T(8,128)}, f32[2,768,128]{2,1,0:T(8,128)}) custom-call(bf16[2,768,1792]{2,1,0:T(8,128)(2,1)} %get-tuple-element.51.xbc_ref, f32[2,768,24]{2,1,0:T(8,128)} %get-tuple-element.52.wid_ref, f32[2,768,24]{2,1,0:T(8,128)} %get-tuple-element.53.cum_ref, ...), custom_call_target="tpu_custom_call" | custom-call | tf_op jit(solution)/shard_map/intra_back/pallas_call | solution.py:861
  222.0 21.2 %adjoint.1 = (bf16[2,768,1792]{2,1,0:T(8,128)(2,1)}, f32[2,768,24]{2,1,0:T(8,128)}) custom-call(bf16[2,768,1792]{2,1,0:T(8,128)(2,1)} %get-tuple-element.51.xbc_ref, bf16[2,768,1792]{2,1,0:T(8,128)(2,1)} %get-tuple-element.64.dact_ref, f32[2,768,24]{2,1,0:T(8,128)} %get-tuple-element.52.wid_ref, f32[2,768,24]{2,1,0:T(8,128)} %get-tuple-element.53.cum_ref, ...), custom_call_target="tpu_custom_call" | custom-call | tf_op jit(solution)/shard_map/adjoint/pallas_call | solution.py:861
  243.3 0.9 slice.7
  244.2 1.3 collective-permute-start
  245.5 0.1 convert_element_type.34
  245.6 0.1 convert_element_type.35
  245.6 0.6 add_convert_fusion.coef_ref
  246.2 4.6 %collective-permute-done.rim_ref = bf16[2,16,1792]{2,1,0:T(8,128)(2,1)S(1)} collective-permute-done((bf16[2,16,1792]{2,1,0:T(8,128)(2,1)S(1)}, bf16[2,16,1792]{2,1,0:T(8,128)(2,1)S(1)}, u32[]{:S(2)}, u32[]{:S(2)}) %collective-permute-start) | collective-permute-done | bytes 114720 | tf_op jit(solution)/shard_map/ppermute | solution.py:1087
  250.8 0.6 copy-done
  251.5 30.1 %input.1 = (bf16[2,768,768]{2,1,0:T(8,128)(2,1)}, f32[2,16,3352]{2,1,0:T(8,128)}, f32[2,16,768]{2,1,0:T(8,128)}) custom-call(s32[2]{0:T(128)} %bitcast.16, bf16[2,768,1792]{2,1,0:T(8,128)(2,1)} %get-tuple-element.76.gpre_ref, bf16[2,16,1792]{2,1,0:T(8,128)(2,1)} %copy-done, bf16[2,768,1536]{2,1,0:T(8,128)(2,1)} %get-tuple-element.77.ggate_ref, ...), custom_call_target="tpu_custom_call" | custom-call | tf_op jit(solution)/shard_map/input/pallas_call | solution.py:861
  281.6 31.4 %adapter_sums.1.final = bf16[56,32,128]{2,1,0:T(8,128)(2,1)} custom-call(f32[2,16,3352]{2,1,0:T(8,128)} %get-tuple-element.80.up_in_ref, f32[2,16,768]{2,1,0:T(8,128)} %get-tuple-element.81.down_in_ref, f32[2,16,768]{2,1,0:T(8,128)} %get-tuple-element.82.up_out_ref, f32[2,16,1536]{2,1,0:T(8,128)} %get-tuple-element.83.down_out_ref, ...), custom_call_target="tpu_custom_call" | custom-call | tf_op jit(solution)/shard_map/adapter_sums/pallas_call | solution.py:830
  313.0 1.9 unpack.1
  (31 shorter events, 0.1 us)
Async XLA Ops:
  7.2 33.1 %copy-start.7 = (f32[24]{0:T(128)S(1)}, f32[24]{0:T(128)}, u32[]{:S(2)}) copy-start(f32[24]{0:T(128)} %param.25) | copy-start | bytes 292
  7.2 33.2 %copy-start.9 = (f32[24]{0:T(128)S(1)}, f32[24]{0:T(128)}, u32[]{:S(2)}) copy-start(f32[24]{0:T(128)} %param.24) | copy-start | bytes 292
  7.2 33.3 %copy-start.2 = (f32[1536]{0:T(1024)S(1)}, f32[1536]{0:T(1024)}, u32[]{:S(2)}) copy-start(f32[1536]{0:T(1024)} %param.26) | copy-start | bytes 18436
  7.2 33.3 %copy-start.5 = (f32[768]{0:T(1024)S(1)}, f32[768]{0:T(1024)}, u32[]{:S(2)}) copy-start(f32[768]{0:T(1024)} %param.19) | copy-start | bytes 9220
  7.2 33.3 %copy-start.8 = (f32[24]{0:T(128)S(1)}, f32[24]{0:T(128)}, u32[]{:S(2)}) copy-start(f32[24]{0:T(128)} %param.23) | copy-start | bytes 292
  7.2 33.4 %copy-start.3 = (f32[1792]{0:T(1024)S(1)}, f32[1792]{0:T(1024)}, u32[]{:S(2)}) copy-start(f32[1792]{0:T(1024)} %param.22) | copy-start | bytes 21508
  7.2 33.4 %copy-start.1 = (f32[1792,4]{0,1:T(4,128)S(1)}, f32[1792,4]{0,1:T(4,128)}, u32[]{:S(2)}) copy-start(f32[1792,4]{0,1:T(4,128)} %param.21) | copy-start | bytes 86020
  7.2 96.2 %all-gather.3.cloned.1.call-start = ((), (), s32[]{:S(2)}) async-start(), calls=%async_computation | async-start | bytes 2949120 | tf_op jit(solution)/shard_map/all_gather | solution.py:924
  39.5 86.9 %all-gather.5.cloned.1.call-start = ((), (), s32[]{:S(2)}) async-start(), calls=%async_computation.1 | async-start | bytes 2949120 | tf_op jit(solution)/shard_map/all_gather | solution.py:925
  41.9 61.5 %copy-start.4 = (s32[2,1]{0,1:T(1,128)S(1)}, s32[2,1]{0,1:T(1,128)}, u32[]{:S(2)}) copy-start(s32[2,1]{0,1:T(1,128)} %param.32) | copy-start | bytes 28
  222.0 23.4 %copy-start.6 = (s32[2,1]{0,1:T(1,128)S(1)}, s32[2,1]{0,1:T(1,128)}, u32[]{:S(2)}) copy-start(s32[2,1]{0,1:T(1,128)} %param.33) | copy-start | bytes 28
  244.2 6.7 %collective-permute-start = (bf16[2,16,1792]{2,1,0:T(8,128)(2,1)S(1)}, bf16[2,16,1792]{2,1,0:T(8,128)(2,1)S(1)}, u32[]{:S(2)}, u32[]{:S(2)}) collective-permute-start(bf16[2,16,1792]{2,1,0:T(8,128)(2,1)S(1)} %slice.7), channel_id=1, source_target_pairs={{4,0},{8,4},{12,8},{16,12},{20,16},{24,20},{28,24},{5,1},{9,5},{13... | collective-permute-start | bytes 344072 | tf_op jit(solution)/shard_map/ppermute | solution.py:1087
  250.8 0.6 copy-start
Sparse Core Ops, SparseCore 0:
  39.6 23.4 all-gather.2
  64.6 24.1 all-gather.4

commit v3 on v2

v3 whole, which is shorter than its diff:
```python
import functools

import jax
import jax.numpy as jnp
from jax import lax
from jax.experimental import pallas as pl
from jax.experimental.pallas import tpu as pltpu
from jax.sharding import PartitionSpec as P

EPS = 1e-05
CHUNK = 128
BLOCK = 256
RIM = 16
LANES = 128
LOG2E = 1.4426950408889634
BF = jnp.bfloat16
F32 = jnp.float32
MESH = pl.DeviceIdType.MESH
VMEM_LIMIT = 62 * 2**20
PARTS = 3
CONV_BIAS, GATE_GAIN, NORM_GAIN, SKIP, STEP_BIAS, RATE = (slice(4 + n, 5 + n) for n in range(6))


def nn(a, b):
    return lax.dot_general(a, b, (((1,), (0,)), ((), ())), preferred_element_type=F32)


def nt(a, b):
    return lax.dot_general(a, b, (((1,), (1,)), ((), ())), preferred_element_type=F32)


def tn(a, b):
    return lax.dot_general(a, b, (((0,), (0,)), ((), ())), preferred_element_type=F32)


def exact(a, b):
    return lax.dot_general(
        a, b, (((1,), (0,)), ((), ())), precision=lax.Precision.HIGHEST, preferred_element_type=F32
    )


def sigmoid(v):
    return 0.5 * jnp.tanh(0.5 * v) + 0.5


def spread(values, onehot):
    high = values.astype(BF)
    rest = (values - high.astype(F32)).astype(BF)
    return nn(high, onehot) + nn(rest, onehot)


def gather_heads(values, onehot):
    return nt(values.astype(BF), onehot)


def head_onehot(heads, inner):
    width = inner // heads
    row = lax.broadcasted_iota(jnp.int32, (heads, inner), 0)
    col = lax.broadcasted_iota(jnp.int32, (heads, inner), 1)
    low = row * width
    return jnp.where((col >= low) & (col < low + width), 1.0, 0.0).astype(BF)


def lower_ones(length):
    row = lax.broadcasted_iota(jnp.int32, (length, length), 0)
    col = lax.broadcasted_iota(jnp.int32, (length, length), 1)
    return jnp.where(row >= col, 1.0, 0.0).astype(F32)


def upper_ones(length):
    row = lax.broadcasted_iota(jnp.int32, (length, length), 0)
    col = lax.broadcasted_iota(jnp.int32, (length, length), 1)
    return jnp.where(row <= col, 1.0, 0.0).astype(F32)


def tiles(width):
    return [slice(at, min(at + LANES, width)) for at in range(0, width, LANES)]


def rows_of(j):
    return slice(j * CHUNK, (j + 1) * CHUNK)


def write_normed(dst, src, gain, step):
    rows = src.shape[0]

    def body(k, _):
        at = pl.ds(pl.multiple_of(k * step, step), step)
        v = src[at, :].astype(F32)
        scale = lax.rsqrt(jnp.mean(v * v, axis=1, keepdims=True) + EPS)
        dst[at, :] = (v * scale * gain).astype(BF)
        return 0

    lax.fori_loop(0, rows // step, body, 0)


def project_step(first_block, normed, halo, win, down, up, par, low_ref, xbc, dact, wid, cum, sig, sloc, cpre, ext, state, run, onehot):
    rows = normed.shape[0]
    heads, inner = onehot.shape
    mixer = xbc.shape[1]
    states = (mixer - inner) // 2

    @pl.when(first_block)
    def _():
        state[...] = jnp.zeros_like(state)
        run[...] = jnp.zeros_like(run)
        v = halo[...].astype(F32)
        scale = lax.rsqrt(jnp.mean(v * v, axis=1, keepdims=True) + EPS)
        first = (v * scale * par[NORM_GAIN, : normed.shape[1]]).astype(BF)
        low_first = nt(first, down[...]).astype(BF)
        for at in range(0, mixer, 2 * LANES):
            t = slice(at, at + 2 * LANES)
            v = nn(first, win[:, t]) + nn(low_first, up[:, inner + at : inner + at + 2 * LANES])
            ext[at // LANES, 0:RIM, :] = v[:, :LANES]
            ext[at // LANES + 1, 0:RIM, :] = v[:, LANES:]

    @pl.when(jnp.logical_not(first_block))
    def _():
        ext[:, 0:RIM, :] = ext[:, rows : rows + RIM, :]

    tokens = normed[...]
    low = nt(tokens, down[...]).astype(BF)
    low_ref[...] = low
    for at in range(0, mixer, 2 * LANES):
        t = slice(at, at + 2 * LANES)
        v = nn(tokens, win[:, t]) + nn(low, up[:, inner + at : inner + at + 2 * LANES])
        ext[at // LANES, RIM : RIM + rows, :] = v[:, :LANES]
        ext[at // LANES + 1, RIM : RIM + rows, :] = v[:, LANES:]
    cols = slice(inner + mixer, inner + mixer + heads)
    raw = nn(tokens, win[:, mixer : mixer + heads]) + nn(low, up[:, cols]) + par[STEP_BIAS, :heads]
    sig[...] = sigmoid(raw)
    widths = jnp.maximum(raw, 0.0) + jnp.log1p(jnp.exp(-jnp.abs(raw)))
    wid[...] = widths
    ones = lower_ones(CHUNK)
    for j in range(rows // CHUNK):
        for n, t in enumerate(tiles(mixer)):
            pre = par[CONV_BIAS, t]
            for k in range(4):
                at = RIM - 3 + k + j * CHUNK
                pre = pre + par[k : k + 1, t] * ext[n, at : at + CHUNK, :]
            s = sigmoid(pre)
            act = pre * s
            xbc[rows_of(j), t] = act.astype(BF)
            dact[rows_of(j), t] = (s + act * (1.0 - s)).astype(BF)
    for j in range(rows // CHUNK):
        w = widths[rows_of(j)]
        c = exact(ones, w * par[RATE, :heads])
        cum[rows_of(j)] = c
        last = c[CHUNK - 1 : CHUNK]
        tail = spread(jnp.exp(last - c) * w, onehot[...])
        weighted = jnp.concatenate(
            [(xbc[rows_of(j), t].astype(F32) * tail[:, t]).astype(BF) for t in tiles(inner)], axis=1
        )
        inputs_t = xbc[rows_of(j), inner : inner + states].astype(F32).T.astype(BF)
        update = nn(inputs_t, weighted)
        before = run[...]
        cpre[j] = before
        keep = spread(jnp.exp(jnp.broadcast_to(last, before.shape)), onehot[...])[0:1]
        for t in tiles(inner):
            old = state[:, t]
            sloc[j, :, t] = old.astype(BF)
            state[:, t] = keep[:, t] * old + update[:, t]
        run[...] = before + last


def intra_step(normed, low_ref, win, up, xbc, wid, cum, gate, y, onehot):
    heads, inner = onehot.shape
    states = (xbc.shape[1] - inner) // 2
    width = inner // heads
    per = LANES // width
    tokens, low = normed[...], low_ref[...]
    for at in range(0, inner, 2 * LANES):
        t = slice(at, at + 2 * LANES)
        gate[:, t] = (nn(tokens, win[:, t]) + nn(low, up[:, t])).astype(BF)
    lane = lax.broadcasted_iota(jnp.int32, (CHUNK, LANES), 1)
    mask = lower_ones(CHUNK)
    for j in range(xbc.shape[0] // CHUNK):
        c = cum[rows_of(j)] * LOG2E
        c_rows = c.T
        wide = spread(wid[rows_of(j)], onehot[...])
        inputs = xbc[rows_of(j), inner : inner + states]
        reads = xbc[rows_of(j), inner + states :]
        scores = nt(reads, inputs) * mask
        for k, t in enumerate(tiles(inner)):
            weighted = xbc[rows_of(j), t].astype(F32) * wide[:, t]
            mixing, parts = [], []
            for p in range(per):
                h = k * per + p
                kernel = jnp.exp2(jnp.minimum(c[:, h : h + 1] - c_rows[h : h + 1, :], 0.0))
                mixing.append((kernel * scores).astype(BF))
                inside = (lane >= p * width) & (lane < (p + 1) * width)
                parts.append(jnp.where(inside, weighted, 0.0).astype(BF))
            y[rows_of(j), t] = nn(jnp.concatenate(mixing, axis=1), jnp.concatenate(parts, axis=0)).astype(BF)


def output_step(
    first_block, middle, loaded, y, xbc, gate, cum, sloc, cpre, csuf, start, res, cot, out, wout, down, up, par,
    dreads, rowt, gup, gdown, onehot, snow, adj, run, gated, nout, gno, prod,
):
    rows = res.shape[0]
    heads, inner = onehot.shape
    states = (xbc.shape[1] - inner) // 2
    chunks = rows // CHUNK

    @pl.when(first_block)
    def _():
        adj[...] = jnp.zeros_like(adj)
        run[...] = jnp.zeros_like(run)
        gup[...] = jnp.zeros_like(gup)
        gdown[...] = jnp.zeros_like(gdown)

    reach, scale = [], []
    for j in range(chunks):
        since = spread(jnp.exp(cpre[j]), onehot[...])
        for t in tiles(inner):
            snow[j, :, t] = (sloc[j, :, t].astype(F32) + since[0:1, t] * start[:, t].astype(F32)).astype(BF)
        carried = nn(xbc[rows_of(j), inner + states :], snow[j])
        grow = spread(jnp.exp(cum[rows_of(j)]), onehot[...])
        reach.append(grow)
        total = jnp.zeros((CHUNK, LANES), F32)
        for t in tiles(inner):
            local = y[rows_of(j), t].astype(F32) + grow[:, t] * carried[:, t]
            y[rows_of(j), t] = local.astype(BF)
            g = gate[rows_of(j), t].astype(F32)
            v = (local + par[SKIP, t] * xbc[rows_of(j), t].astype(F32)) * (g * sigmoid(g))
            gated[rows_of(j), t] = v.astype(BF)
            total = total + v * v
        r = lax.rsqrt(jnp.sum(total, axis=1, keepdims=True) * (1.0 / inner) + EPS)
        scale.append(r)
        for t in tiles(inner):
            nout[rows_of(j), t] = (gated[rows_of(j), t].astype(F32) * r * par[GATE_GAIN, t]).astype(BF)

    middle()
    loaded()
    normed_out = nout[...]
    cot_rows = cot[...]
    low_out = nt(normed_out, down[...]).astype(BF)
    for at in range(0, out.shape[1], 2 * LANES):
        t = slice(at, at + 2 * LANES)
        part = nn(normed_out, wout[:, t]) + nn(low_out, up[:, t])
        out[:, t] = (res[:, t].astype(F32) + part).astype(BF)
    grad_low = nt(cot_rows, up[...]).astype(BF)
    for at in range(0, inner, 2 * LANES):
        t = slice(at, at + 2 * LANES)
        v = nt(cot_rows, wout[t, :]) + nn(grad_low, down[:, t])
        gno[at // LANES, 0:rows, :] = v[:, :LANES]
        gno[at // LANES + 1, 0:rows, :] = v[:, LANES:]
    gup[...] += tn(low_out, cot_rows)
    gdown[...] += tn(grad_low, normed_out)

    for j in reversed(range(chunks)):
        total = jnp.zeros((CHUNK, LANES), F32)
        for n, t in enumerate(tiles(inner)):
            q = gno[n, rows_of(j), :] * par[GATE_GAIN, t]
            total = total + gated[rows_of(j), t].astype(F32) * q
        r = scale[j]
        shrink = jnp.sum(total, axis=1, keepdims=True) * (1.0 / inner) * (r * r * r)
        scaled = []
        for n, t in enumerate(tiles(inner)):
            q = gno[n, rows_of(j), :] * par[GATE_GAIN, t]
            grad = r * q - gated[rows_of(j), t].astype(F32) * shrink
            local = y[rows_of(j), t].astype(F32)
            g = gate[rows_of(j), t].astype(F32)
            s = sigmoid(g)
            dy = grad * (g * s)
            y[rows_of(j), t] = dy.astype(BF)
            full = local + par[SKIP, t] * xbc[rows_of(j), t].astype(F32)
            gate[rows_of(j), t] = (grad * full * (s * (1.0 + g * (1.0 - s)))).astype(BF)
            prod[:, t] = (dy * local).astype(BF)
            scaled.append((dy * reach[j][:, t]).astype(BF))
        rowt[rows_of(j)] = nt(prod[...], onehot[...])
        scaled = jnp.concatenate(scaled, axis=1)
        reads_t = xbc[rows_of(j), inner + states :].astype(F32).T.astype(BF)
        update = nn(reads_t, scaled)
        dreads[rows_of(j)] = nt(scaled, snow[j])
        last = cum[j * CHUNK + CHUNK - 1 : j * CHUNK + CHUNK]
        before = run[...]
        csuf[j] = before
        keep = reach[j][CHUNK - 1 : CHUNK]
        for t in tiles(inner):
            old = adj[:, t]
            sloc[j, :, t] = old.astype(BF)
            adj[:, t] = keep[:, t] * old + update[:, t]
        run[...] = before + last


def adjoint_step(first_block, between, xbc, dact, wid, cum, sig, dy, dreads, rowt, gloc, csuf, end, final, par, onehot, adj, prod, z, held):
    heads, inner = onehot.shape
    states = (xbc.shape[1] - inner) // 2
    width = inner // heads
    per = LANES // width
    mask = upper_ones(CHUNK)
    lane = lax.broadcasted_iota(jnp.int32, (CHUNK, LANES), 1)

    @pl.when(first_block)
    def _():
        overlap = []
        for t in tiles(inner):
            overlap.append(jnp.sum(end[:, t].astype(F32) * final(t), axis=0, keepdims=True))
        v = jnp.broadcast_to(jnp.concatenate(overlap, axis=1), (8, inner))
        high = v.astype(BF)
        held[...] = nt(high, onehot[...]) + nt((v - high.astype(F32)).astype(BF), onehot[...])

    for j in reversed(range(xbc.shape[0] // CHUNK)):
        at = rows_of(j)
        c = cum[at]
        w = wid[at]
        c_two = c * LOG2E
        c_rows = c_two.T
        wide = spread(w, onehot[...])
        inputs = xbc[at, inner : inner + states]
        reads = xbc[at, inner + states :]
        scores_t = nt(inputs, reads) * mask
        total = jnp.zeros((CHUNK, CHUNK), F32)
        for k, t in enumerate(tiles(inner)):
            weighted = xbc[at, t].astype(F32) * wide[:, t]
            grads = dy[at, t]
            mixing, left, right = [], [], []
            for p in range(per):
                inside = (lane >= p * width) & (lane < (p + 1) * width)
                left.append(jnp.where(inside, weighted, 0.0).astype(BF))
                right.append(jnp.where(inside, grads.astype(F32), 0.0).astype(BF))
            products = nt(jnp.concatenate(left, axis=0), grads)
            for p in range(per):
                h = k * per + p
                kernel = jnp.exp2(jnp.minimum(c_rows[h : h + 1, :] - c_two[:, h : h + 1], 0.0))
                mixing.append((kernel * scores_t).astype(BF))
                total = total + kernel * products[p * CHUNK : (p + 1) * CHUNK]
            z[:, t] = nn(jnp.concatenate(mixing, axis=1), jnp.concatenate(right, axis=0))
        total = total * mask
        dinputs = nn(total.astype(BF), reads)
        dreads_all = dreads[at] + nn(total.T.astype(BF), inputs)

        since = spread(jnp.exp(csuf[j]), onehot[...])
        for t in tiles(inner):
            adj[:, t] = (gloc[j, :, t].astype(F32) + since[0:1, t] * end[:, t].astype(F32)).astype(BF)
        last = c[CHUNK - 1 : CHUNK]
        tail = spread(jnp.exp(last - c), onehot[...])
        carried = nn(inputs, adj[...])
        weighted = []
        for t in tiles(inner):
            x = xbc[at, t].astype(F32)
            v = z[:, t] + tail[:, t] * carried[:, t]
            prod[:, t] = (x * v).astype(BF)
            grad = wide[:, t] * v + par[SKIP, t] * dy[at, t].astype(F32)
            dact[at, t] = (grad * dact[at, t].astype(F32)).astype(BF)
            weighted.append((x * (wide[:, t] * tail[:, t])).astype(BF))
        dinputs = dinputs + nt(jnp.concatenate(weighted, axis=1), adj[...])
        t = slice(inner, inner + states)
        dact[at, t] = (dinputs * dact[at, t].astype(F32)).astype(BF)
        t = slice(inner + states, inner + 2 * states)
        dact[at, t] = (dreads_all * dact[at, t].astype(F32)).astype(BF)
        direct = nt(prod[...], onehot[...])
        grad_rate = held[0:1] + exact(mask, rowt[at] - w * direct)
        held[...] = jnp.broadcast_to(grad_rate[0:1], held.shape)
        sig[at] = (direct + par[RATE, :heads] * grad_rate) * sig[at]
        between(j)


def input_step(first_block, loaded, following, gpre, ggate, graw, low_ref, res, cot, gin, wgate, win, down, up, par, gup, gdown, ext, gn, nrm):
    rows = res.shape[0]
    inner = ggate.shape[1]
    mixer = gpre.shape[1]
    proj = inner + win.shape[1]
    model = res.shape[1]
    gain = par[NORM_GAIN, :model]

    @pl.when(first_block)
    def _():
        gup[...] = jnp.zeros_like(gup)
        gdown[...] = jnp.zeros_like(gdown)

    for n, t in enumerate(tiles(mixer)):
        for j in range(rows // CHUNK):
            ext[n, rows_of(j), :] = gpre[rows_of(j), t].astype(F32)
    following()
    for j in range(rows // CHUNK):
        for n, t in enumerate(tiles(mixer)):
            total = None
            for k in range(4):
                at = 3 - k + j * CHUNK
                term = par[k : k + 1, t] * ext[n, at : at + CHUNK, :]
                total = term if total is None else total + term
            gpre[rows_of(j), t] = total.astype(BF)
    whole = slice(inner, inner + mixer)
    rest = slice(inner + mixer, proj)
    grads_gate, grads_mix, grads_rest = ggate[...], gpre[...], graw[...].astype(BF)
    grad_low = (nt(grads_gate, up[:, :inner]) + nt(grads_mix, up[:, whole]) + nt(grads_rest, up[:, rest])).astype(BF)
    for at in range(0, model, 2 * LANES):
        t = slice(at, at + 2 * LANES)
        part = nt(grads_gate, wgate[t, :]) + nt(grads_mix, win[t, :mixer])
        gn[:, t] = part + nt(grads_rest, win[t, mixer:]) + nn(grad_low, down[:, t])
    loaded()

    def body(k, _):
        at = pl.ds(pl.multiple_of(k * 32, 32), 32)
        v = res[at, :].astype(F32)
        u = lax.rsqrt(jnp.mean(v * v, axis=1, keepdims=True) + EPS)
        nrm[at, :] = (v * u * gain).astype(BF)
        w = gn[at, :] * gain
        m = jnp.mean(v * w, axis=1, keepdims=True)
        gin[at, :] = (cot[at, :].astype(F32) + u * w - v * (u * u * u * m)).astype(BF)
        return 0

    lax.fori_loop(0, rows // 32, body, 0)
    low = low_ref[...]
    gup[:, :inner] += tn(low, grads_gate)
    gup[:, whole] += tn(low, grads_mix)
    gup[:, rest] += tn(low, grads_rest)
    gdown[...] += tn(grad_low, nrm[...])


def block_kernel(
    dp_count, seq_count,
    in_idx, out_idx, res_ref, cot_ref, win_ref, wout_ref, early_ref, late_ref, par,
    out_ref, gin_ref, gup_in, gdown_in, gup_out, gdown_out,
    xbc, dact, gate, yb, sloc, low, wid, cum, sig, rowt, dreads, cpre, csuf, tot, dtot, start, gown, end,
    theirs, theirs_dec, prefix, passed, tail, wmix, wgate, wout, early, late, up_in, down_in, up_out, down_out,
    halo, rim, stage_res, stage_cot, stage_out, ext, state, snow, gated, nout, prod, run, held, onehot, z, gn,
    wsems, csems, hsems, lsems,
):
    dp = lax.axis_index("dp")
    seq = lax.axis_index("seq")
    seqs, tokens, model = res_ref.shape
    blocks = tokens // BLOCK
    per = BLOCK // CHUNK
    heads, inner = onehot.shape
    mixer = xbc.shape[2]
    rank = up_in.shape[1]
    pairs = seq_count // 2
    side = lax.rem(seq, 2)
    pair = seq // 2
    chips = dp_count // 2
    partner = (seq + 1 - 2 * side, dp)
    sibling = (seq, dp + 1 - 2 * lax.rem(dp, 2))
    later = (lax.rem(seq + 1, seq_count), dp)
    earlier = (lax.rem(seq + seq_count - 1, seq_count), dp)
    upper = (lax.rem(pair + 1, pairs) * 2 + side, dp)
    lower = (lax.rem(pair + pairs - 1, pairs) * 2 + side, dp)
    others = [(seq, lax.rem(dp + 2 * k, dp_count)) for k in range(1, chips)]
    barrier = pltpu.get_barrier_semaphore()
    greeted = [partner, sibling, later, earlier, upper, lower] + others
    for other in greeted:
        pl.semaphore_signal(barrier, inc=1, device_id=other, device_id_type=MESH)

    def load(n):
        s, k = n // blocks, lax.rem(n, blocks) if not isinstance(n, int) else n % blocks
        rows = pl.ds(k * BLOCK, BLOCK)
        return pltpu.make_async_copy(res_ref.at[s, rows], yb.at[n, :, pl.ds(model, model)], lsems.at[n])

    for n in range(seqs * blocks):
        load(n).start()
    onehot[...] = head_onehot(heads, inner)
    pl.semaphore_wait(barrier, len(greeted))

    def send(src, dst, to, sems, *at):
        return pltpu.make_async_remote_copy(
            src_ref=src, dst_ref=dst, send_sem=sems.at[(0,) + at], recv_sem=sems.at[(1,) + at],
            device_id=to, device_id_type=MESH,
        )

    def rows_piece(ref, out, at, to, wide, n):
        share = ref.shape[0]
        half = share // 2

        def source(which):
            return ref.at[pl.ds(pl.multiple_of(which * half, 16), half), pl.ds(at, wide)]

        def target(owner, which):
            return out.at[pl.ds(pl.multiple_of(owner * share + which * half, 16), half), pl.ds(to, wide)]

        return source, target, n

    def table_piece(ref, out, n):
        owned = ref.shape[1]
        return (lambda which: ref.at[which]), (lambda owner, which: out.at[which, pl.ds(owner * owned, owned)]), n

    width = wmix.shape[1]
    split = width // 2 // LANES * LANES
    groups = [
        [
            table_piece(early_ref, early, 0),
            rows_piece(win_ref, wmix, inner, 0, split, 1),
            rows_piece(win_ref, wmix, inner + split, split, width - split, 2),
        ],
        [
            table_piece(late_ref, late, 3),
            rows_piece(win_ref, wgate, 0, 0, inner, 4),
            rows_piece(wout_ref, wout, 0, 0, wout_ref.shape[1], 5),
        ],
    ]

    def shards(k):
        return lax.rem(dp - 2 * k + dp_count, dp_count)

    def over_x(group):
        return [send(source(side), target(dp, side), others[k - 1], wsems, 0, k, n) for source, target, n in group for k in range(1, chips)]

    def own(group):
        copies = []
        for source, target, n in group:
            for which in range(2):
                copies.append(pltpu.make_async_copy(source(which), target(dp, which), wsems.at[0, 6 + which, 0, n]))
                copies.append(send(source(which), target(dp, which), sibling, wsems, 3 + which, 0, n))
        return copies

    def forward(group, start_it):
        for source, target, n in group:
            for k in range(1, chips):
                here = target(shards(k), side)
                if start_it:
                    send(source(side), here, others[k - 1], wsems, 0, k, n).wait_recv()
                across = send(here, here, partner, wsems, 1, k, n)
                over = send(here, here, sibling, wsems, 2, k, n)
                if start_it:
                    across.start()
                    over.start()
                else:
                    across.wait_send()
                    over.wait()

    def relay(group, start_it):
        for source, target, n in group:
            for k in range(1, chips):
                there = target(shards(k), 1 - side)
                over = send(there, there, sibling, wsems, 5, k, n)
                if start_it:
                    send(there, there, partner, wsems, 1, k, n).wait_recv()
                    over.start()
                else:
                    over.wait()

    edge = send(res_ref.at[:, pl.ds(tokens - RIM, RIM)], halo, later, hsems, 0)
    for copy in over_x(groups[0]):
        copy.start()

    @pl.when(seq < seq_count - 1)
    def _():
        edge.start()

    for copy in own(groups[0]):
        copy.start()
    gain = par[NORM_GAIN, :model]

    def norm_block(n, _):
        load(n).wait()
        write_normed(yb.at[n, :, pl.ds(0, model)], yb.at[n, :, pl.ds(model, model)], gain, 32)
        return 0

    lax.fori_loop(0, seqs * blocks, norm_block, 0)
    forward(groups[0], True)
    relay(groups[0], True)

    @pl.when(seq == 0)
    def _():
        halo[...] = jnp.zeros_like(halo)

    @pl.when(seq > 0)
    def _():
        edge.wait_recv()

    @pl.when(seq < seq_count - 1)
    def _():
        edge.wait_send()

    for copy in over_x(groups[0]):
        copy.wait_send()
    for copy in over_x(groups[1]):
        copy.start()
    for copy in own(groups[0]):
        copy.wait()
    forward(groups[0], False)
    relay(groups[0], False)
    for copy in own(groups[1]):
        copy.start()

    def pick(table, dests):
        half = table.shape[3] // LANES
        n = 0
        for dst, at, wide, idx_ref in dests:
            for k in range(wide // LANES):
                src = slice(n % half * LANES, n % half * LANES + LANES)
                for s in range(seqs):
                    dst[s, :, at + k * LANES : at + (k + 1) * LANES] = table[n // half, idx_ref[s, 0], :, src]
                n += 1

    lanes = up_in.shape[2]
    pick(early, [(up_in, inner, lanes - inner, in_idx), (down_in, 0, model, in_idx)])

    half = inner // 2
    wide = half // PARTS

    def cols(base, q):
        return pl.ds(pl.multiple_of(base * half + q * wide, LANES), wide)

    def chain(d, s):
        my_pair = pairs - 1 - pair if d else pair
        my_side = 1 - side if d else side
        ahead = lower if d else upper
        total, result = (gown, end) if d else (tot, start)

        def decs():
            return send(dtot.at[s], theirs_dec.at[d, s], partner, csems, d, s, 3, 0)

        def swap(q):
            return send(total.at[s, :, cols(1 - my_side, q)], theirs.at[d, s, q], partner, csems, d, s, 0, q)

        def hop(q):
            return send(passed.at[d, s, q], prefix.at[d, s, q], ahead, csems, d, s, 1, q)

        def give(q):
            return send(tail.at[d, s, q], result.at[s, :, cols(my_side, q)], partner, csems, d, s, 2, q)

        return my_pair, my_side, total, result, decs, swap, hop, give

    def chain_start(d, s):
        _, _, _, _, decs, swap, _, _ = chain(d, s)
        decs().start()
        for q in range(PARTS):
            swap(q).start()

    def chain_tick(d, s, tick, final):
        my_pair, my_side, total, result, decs, swap, hop, give = chain(d, s)
        for q in range(PARTS):
            turn = jnp.minimum(my_pair + (1 if q else 0), final)

            @pl.when(tick == turn)
            def _(q=q):
                if q == 0:
                    decs().wait_recv()
                swap(q).wait_recv()

                @pl.when(my_pair == 0)
                def _():
                    prefix[d, s, q] = jnp.zeros_like(prefix[d, s, q])

                @pl.when(my_pair > 0)
                def _():
                    hop(q).wait_recv()

                own_dec = dtot[s, 0:1, cols(my_side, q)]
                their_dec = theirs_dec[d, s, 0:1, cols(my_side, q)]
                own_total = total[s, :, cols(my_side, q)].astype(F32)
                other = theirs[d, s, q].astype(F32)
                before = prefix[d, s, q].astype(F32)
                left = my_side == 0
                first = jnp.where(left, own_total, other)
                second = jnp.where(left, other, own_total)
                first_dec = jnp.where(left, own_dec, their_dec)
                second_dec = jnp.where(left, their_dec, own_dec)
                middle = first_dec * before + first
                passed[d, s, q] = (second_dec * middle + second).astype(BF)

                @pl.when(my_pair < pairs - 1)
                def _():
                    hop(q).start()

                result[s, :, cols(my_side, q)] = jnp.where(left, before, middle).astype(BF)
                tail[d, s, q] = jnp.where(left, middle, before).astype(BF)
                give(q).start()

    def chain_end(d, s):
        my_pair, _, _, _, decs, swap, hop, give = chain(d, s)
        decs().wait_send()
        for q in range(PARTS):
            give(q).wait()
            swap(q).wait_send()

            @pl.when(my_pair < pairs - 1)
            def _(q=q):
                hop(q).wait_send()

    def chunk_of(n):
        return pl.ds(n * per, per)

    def project_block(n, _):
        s, k = n // blocks, lax.rem(n, blocks)
        project_step(
            k == 0, yb.at[n, :, pl.ds(0, model)], halo.at[s], wmix, down_in.at[s], up_in.at[s], par, low.at[n],
            xbc.at[n], dact.at[n], wid.at[n], cum.at[n], sig.at[n], sloc.at[chunk_of(n)], cpre.at[chunk_of(n)],
            ext, state, run, onehot,
        )

        @pl.when(k == blocks - 1)
        def _():
            tot[s] = state[...].astype(BF)
            dtot[s] = spread(jnp.exp(run[...]), onehot[...])

        @pl.when(n == blocks - 1)
        def _():
            forward(groups[1], True)
            chain_start(0, 0)

        @pl.when(n >= blocks)
        def _():
            chain_tick(0, 0, n - blocks, 2 * blocks)

        return 0

    lax.fori_loop(0, seqs * blocks, project_block, 0)
    chain_start(0, 1)
    relay(groups[1], True)
    for copy in over_x(groups[1]):
        copy.wait_send()
    for copy in own(groups[1]):
        copy.wait()
    forward(groups[1], False)
    relay(groups[1], False)
    pick(late, [(up_in, 0, inner, in_idx), (down_out, 0, inner, out_idx), (up_out, 0, model, out_idx)])

    def intra_block(n, _):
        s = n // blocks
        intra_step(
            yb.at[n, :, pl.ds(0, model)], low.at[n], wgate, up_in.at[s], xbc.at[n], wid.at[n], cum.at[n], gate.at[n],
            yb.at[n], onehot,
        )

        @pl.when(n <= blocks)
        def _():
            chain_tick(0, 0, n + blocks, 2 * blocks)

        chain_tick(0, 1, n, seqs * blocks - 1)
        return 0

    lax.fori_loop(0, seqs * blocks, intra_block, 0)
    chain_end(0, 0)

    def staged(s, k):
        rows = pl.ds(k * BLOCK, BLOCK)
        return [
            pltpu.make_async_copy(res_ref.at[s, rows], stage_res, lsems.at[0]),
            pltpu.make_async_copy(cot_ref.at[s, rows], stage_cot, lsems.at[1]),
        ]

    def stored(ref, s, k):
        return pltpu.make_async_copy(stage_out, ref.at[s, pl.ds(k * BLOCK, BLOCK)], lsems.at[2])

    def output_block(i, _):
        s, k = i // blocks, blocks - 1 - lax.rem(i, blocks)
        n = s * blocks + k
        for copy in staged(s, k):
            copy.start()

        @pl.when(i == blocks)
        def _():
            chain_end(0, 1)

        def middle():
            @pl.when(i >= blocks)
            def _():
                chain_tick(1, 0, 2 * (i - blocks), 2 * blocks - 1)

        def loaded():
            for copy in staged(s, k):
                copy.wait()

            @pl.when(i > 0)
            def _():
                stored(out_ref, s, k).wait()

        output_step(
            k == blocks - 1, middle, loaded, yb.at[n], xbc.at[n], gate.at[n], cum.at[n], sloc.at[chunk_of(n)],
            cpre.at[chunk_of(n)], csuf.at[chunk_of(n)], start.at[s], stage_res, stage_cot, stage_out, wout, down_out.at[s],
            up_out.at[s], par, dreads.at[n], rowt.at[n], gup_out.at[s], gdown_out.at[s], onehot, snow, state, run, gated,
            nout, ext, prod,
        )
        stored(out_ref, s, k).start()

        @pl.when(k == 0)
        def _():
            gown[s] = state[...].astype(BF)

        @pl.when(i == blocks - 1)
        def _():
            chain_start(1, 0)

        @pl.when(i >= blocks)
        def _():
            chain_tick(1, 0, 2 * (i - blocks) + 1, 2 * blocks - 1)

        return 0

    lax.fori_loop(0, seqs * blocks, output_block, 0)
    stored(out_ref, seqs - 1, 0).wait()
    chain_start(1, 1)

    def rim_edge(s):
        return send(dact.at[s * blocks, pl.ds(0, RIM)], rim.at[s], earlier, hsems, 1 + s)

    period = 2 * blocks - 1
    steps = seqs * period + seqs

    def back_block(i, _):
        late_one = i >= seqs * period
        s = jnp.where(late_one, i - seqs * period, i // period)
        r = jnp.where(late_one, 2 * blocks - 1, lax.rem(i, period))

        @pl.when(r < blocks)
        def _():
            k = blocks - 1 - r
            n = s * blocks + k

            @pl.when(i == 0)
            def _():
                chain_end(1, 0)

            @pl.when(i == period)
            def _():
                chain_end(1, 1)

            def between(j):
                @pl.when(i < blocks)
                def _():
                    chain_tick(1, 1, per * i + (per - 1 - j), per * blocks - 1)

            adjoint_step(
                k == blocks - 1, between, xbc.at[n], dact.at[n], wid.at[n], cum.at[n], sig.at[n], yb.at[n], dreads.at[n],
                rowt.at[n], sloc.at[chunk_of(n)], csuf.at[chunk_of(n)], end.at[s],
                lambda t: tot[s, :, t].astype(F32) + dtot[s, 0:1, t] * start[s, :, t].astype(F32),
                par, onehot, nout.at[pl.ds(0, CHUNK)], prod, z, held,
            )

            @pl.when(k == 0)
            def _():
                for q in range(seqs):
                    @pl.when((s == q) & (seq > 0))
                    def _(q=q):
                        rim_edge(q).start()

        @pl.when(r >= blocks)
        def _():
            k = r - blocks
            n = s * blocks + k
            for copy in staged(s, k):
                copy.start()
            for q in range(seqs):
                @pl.when((s == q) & (k == 0) & (seq > 0))
                def _(q=q):
                    rim_edge(q).wait_send()

                @pl.when((s == q) & late_one & (seq < seq_count - 1))
                def _(q=q):
                    rim_edge(q).wait_recv()

                @pl.when((s == q) & late_one & (seq == seq_count - 1))
                def _(q=q):
                    rim[q] = jnp.zeros_like(rim[q])

            def loaded():
                for copy in staged(s, k):
                    copy.wait()

                @pl.when(i > blocks)
                def _():
                    stored(gin_ref, s, k).wait()

            def following():
                @pl.when(late_one)
                def _():
                    for m, t in enumerate(tiles(mixer)):
                        ext[m, BLOCK : BLOCK + RIM, :] = rim[s, :, t].astype(F32)

                @pl.when(jnp.logical_not(late_one))
                def _():
                    for m, t in enumerate(tiles(mixer)):
                        ext[m, BLOCK : BLOCK + RIM, :] = dact[n + 1, 0:RIM, t].astype(F32)

            input_step(
                k == 0, loaded, following, dact.at[n], gate.at[n], sig.at[n], low.at[n], stage_res, stage_cot, stage_out,
                wgate, wmix, down_in.at[s], up_in.at[s], par, gup_in.at[s], gdown_in.at[s], ext, gn,
                nout.at[:, pl.ds(0, model)],
            )
            stored(gin_ref, s, k).start()

        return 0

    lax.fori_loop(0, steps, back_block, 0)
    stored(gin_ref, seqs - 1, blocks - 1).wait()


def block_call(in_index, out_index, residual, cotangent, in_weight, out_weight, early, late, params, sizes, dp_count, seq_count):
    heads, inner, mixer, rank = sizes
    seqs, tokens, model = residual.shape
    states = (mixer - inner) // 2
    count = tokens // BLOCK * seqs
    chunks = tokens // CHUNK * seqs
    proj = in_weight.shape[1]
    lanes = -(-proj // LANES) * LANES
    rows = lambda width, kind: pltpu.VMEM((count, BLOCK, width), kind)
    state = lambda: pltpu.VMEM((seqs, states, inner), BF)
    slots = lambda: pltpu.VMEM((2, seqs, PARTS, states, inner // 2 // PARTS), BF)
    stage = lambda: pltpu.VMEM((BLOCK, model), BF)
    picked = lambda width: pltpu.VMEM((seqs, rank, width), BF)
    any_space = pl.BlockSpec(memory_space=pl.ANY)
    vmem = pl.BlockSpec(memory_space=pltpu.VMEM)
    smem = pl.BlockSpec(memory_space=pltpu.SMEM)
    return pl.pallas_call(
        functools.partial(block_kernel, dp_count, seq_count),
        out_shape=[
            jax.ShapeDtypeStruct(residual.shape, BF),
            jax.ShapeDtypeStruct(residual.shape, BF),
            jax.ShapeDtypeStruct((seqs, rank, proj), F32),
            jax.ShapeDtypeStruct((seqs, rank, model), F32),
            jax.ShapeDtypeStruct((seqs, rank, model), F32),
            jax.ShapeDtypeStruct((seqs, rank, inner), F32),
        ],
        in_specs=[smem, smem] + [any_space] * 6 + [vmem],
        out_specs=[any_space] * 2 + [vmem] * 4,
        scratch_shapes=[
            rows(mixer, BF),
            rows(mixer, BF),
            rows(inner, BF),
            rows(inner, BF),
            pltpu.VMEM((chunks, states, inner), BF),
            rows(rank, BF),
            rows(heads, F32),
            rows(heads, F32),
            rows(heads, F32),
            rows(heads, F32),
            rows(states, F32),
            pltpu.VMEM((chunks, 8, heads), F32),
            pltpu.VMEM((chunks, 8, heads), F32),
            state(),
            pltpu.VMEM((seqs, 8, inner), F32),
            state(),
            state(),
            state(),
            slots(),
            pltpu.VMEM((2, seqs, 8, inner), F32),
            slots(),
            slots(),
            slots(),
            pltpu.VMEM((model, proj - inner), BF),
            pltpu.VMEM((model, inner), BF),
            pltpu.VMEM((inner, model), BF),
            pltpu.VMEM((2, early.shape[1] * dp_count) + early.shape[2:], BF),
            pltpu.VMEM((2, late.shape[1] * dp_count) + late.shape[2:], BF),
            picked(lanes),
            picked(model),
            picked(model),
            picked(inner),
            pltpu.VMEM((seqs, RIM, model), BF),
            pltpu.VMEM((seqs, RIM, mixer), BF),
            stage(),
            stage(),
            stage(),
            pltpu.VMEM((mixer // LANES, BLOCK + RIM, LANES), F32),
            pltpu.VMEM((states, inner), F32),
            pltpu.VMEM((BLOCK // CHUNK, states, inner), BF),
            pltpu.VMEM((BLOCK, inner), BF),
            pltpu.VMEM((BLOCK, inner), BF),
            pltpu.VMEM((CHUNK, inner), BF),
            pltpu.VMEM((8, heads), F32),
            pltpu.VMEM((8, heads), F32),
            pltpu.VMEM((heads, inner), BF),
            pltpu.VMEM((CHUNK, inner), F32),
            pltpu.VMEM((BLOCK, model), F32),
            pltpu.SemaphoreType.DMA((2, 8, max(dp_count // 2, 1), 6)),
            pltpu.SemaphoreType.DMA((2, 2, seqs, 4, PARTS)),
            pltpu.SemaphoreType.DMA((2, 1 + seqs)),
            pltpu.SemaphoreType.DMA((max(count, 3),)),
        ],
        compiler_params=pltpu.CompilerParams(collective_id=1, has_side_effects=True, vmem_limit_bytes=VMEM_LIMIT),
        name="block",
    )(in_index, out_index, residual, cotangent, in_weight, out_weight, early, late, params)


def sums_kernel(
    count, dp_count, up_in_ref, down_in_ref, up_out_ref, down_out_ref, coef_ref,
    final,
    pack, half, half_sent, first, line, red, give, owners, sems,
):
    dp = lax.axis_index("dp")
    seq = lax.axis_index("seq")
    pair, side = seq // 2, lax.rem(seq, 2)
    pairs = count // 2
    share = red.shape[0]
    seqs, rank, _ = up_in_ref.shape
    owned = final.shape[1] // rank
    partner = (seq + 1 - 2 * side, dp)
    along = [(lax.rem(pair + k, pairs) * 2 + side, dp) for k in range(1, pairs)]
    across = [(seq, lax.rem(dp + k, dp_count)) for k in range(1, dp_count)]
    barrier = pltpu.get_barrier_semaphore()
    for other in [partner] + along + across:
        pl.semaphore_signal(barrier, inc=1, device_id=other, device_id_type=MESH)

    places = []
    for n, ref in enumerate((up_in_ref, down_in_ref, up_out_ref, down_out_ref)):
        if n == 2:
            in_tiles = len(places)
        places += [(ref, t.start, t.stop - t.start) for t in tiles(ref.shape[2])]
    for n, (ref, at, wide) in enumerate(places):
        for s in range(seqs):
            v = ref[s, :, at : at + wide]
            if wide < LANES:
                v = jnp.concatenate([v, jnp.zeros((rank, LANES - wide), F32)], axis=1)
            pack[n, s * rank : (s + 1) * rank, :] = v.astype(BF)
    for n in range(len(places), pack.shape[0]):
        pack[n] = jnp.zeros_like(pack[n])
    pl.semaphore_wait(barrier, 1 + len(along) + len(across))

    def send(src, dst, to, *at):
        return pltpu.make_async_remote_copy(
            src_ref=src, dst_ref=dst, send_sem=sems.at[(0,) + at], recv_sem=sems.at[(1,) + at],
            device_id=to, device_id_type=MESH,
        )

    wide = pairs * share
    copy = send(pack.at[pl.ds((1 - side) * wide, wide)], first, partner, 0, 0)
    copy.start()
    copy.wait()

    def add(n, _):
        v = pack[side * wide + n].astype(F32) + first[n].astype(F32)
        half[n] = v
        half_sent[n] = v.astype(BF)
        return 0

    lax.fori_loop(0, wide, add, 0)
    copies = []
    for k in range(1, pairs):
        there = lax.rem(pair + k, pairs)
        copies.append(send(half_sent.at[pl.ds(there * share, share)], line.at[k - 1], along[k - 1], 1, k))
        copies[-1].start()
    for copy in copies:
        copy.wait()
    for n in range(share):
        v = half[pair * share + n]
        for k in range(pairs - 1):
            v = v + line[k, n].astype(F32)
        red[n] = v

    def part(owner, n, a):
        tile = (side * pairs + pair) * share + n
        kind = jnp.where(tile < in_tiles, 0, 1)
        total = None
        for s in range(seqs):
            c = coef_ref[kind, (owner * owned + a) * seqs + s]
            term = c * red[n, s * rank : (s + 1) * rank, :]
            total = term if total is None else total + term
        return total

    copies = []
    for k in range(1, dp_count):
        owner = lax.rem(dp + k, dp_count)
        for n in range(share):
            for a in range(owned):
                give[k - 1, n, a * rank : (a + 1) * rank, :] = part(owner, n, a).astype(BF)
        copies.append(send(give.at[k - 1], owners.at[k - 1], across[k - 1], 2, k))
        copies[-1].start()
    mine = [[part(dp, n, a) for a in range(owned)] for n in range(share)]
    for copy in copies:
        copy.wait()
    here = pl.ds((side * pairs + pair) * share, share)
    for n in range(share):
        for a in range(owned):
            v = mine[n][a]
            for k in range(dp_count - 1):
                v = v + owners[k, n, a * rank : (a + 1) * rank, :].astype(F32)
            final[(side * pairs + pair) * share + n, a * rank : (a + 1) * rank, :] = v.astype(BF)
    copies = []
    for k in range(1, pairs):
        copies.append(send(final.at[here], final.at[here], along[k - 1], 3, k))
        copies[-1].start()
    for copy in copies:
        copy.wait()
    ours = final.at[pl.ds(side * wide, wide)]
    copy = send(ours, ours, partner, 4, 0)
    copy.start()
    copy.wait()

def unpack_kernel(final, up_in_out, down_in_out, up_out_out, down_out_out):
    owned, rank, _ = up_in_out.shape
    n = 0
    for out in (up_in_out, down_in_out, up_out_out, down_out_out):
        for t in tiles(out.shape[2]):
            for a in range(owned):
                out[a, :, t] = final[n, a * rank : (a + 1) * rank, : t.stop - t.start].astype(F32)
            n += 1


def adapter_sums(grads, coef, owned, count, dp_count):
    up_in, down_in, up_out, down_out = grads
    seqs, rank, _ = up_in.shape
    total = sum(-(-g.shape[2] // LANES) for g in grads)
    share = -(-total // count)
    pairs = count // 2
    rows = seqs * rank
    own_rows = owned * rank
    whole = pl.BlockSpec(memory_space=pltpu.VMEM)
    final = pl.pallas_call(
        functools.partial(sums_kernel, count, dp_count),
        out_shape=jax.ShapeDtypeStruct((share * count, own_rows, LANES), BF),
        in_specs=[whole] * 4 + [pl.BlockSpec(memory_space=pltpu.SMEM)],
        out_specs=whole,
        scratch_shapes=[
            pltpu.VMEM((share * count, rows, LANES), BF),
            pltpu.VMEM((share * pairs, rows, LANES), F32),
            pltpu.VMEM((share * pairs, rows, LANES), BF),
            pltpu.VMEM((share * pairs, rows, LANES), BF),
            pltpu.VMEM((max(pairs - 1, 1), share, rows, LANES), BF),
            pltpu.VMEM((share, rows, LANES), F32),
            pltpu.VMEM((max(dp_count - 1, 1), share, own_rows, LANES), BF),
            pltpu.VMEM((max(dp_count - 1, 1), share, own_rows, LANES), BF),
            pltpu.SemaphoreType.DMA((2, 5, max(pairs, dp_count))),
        ],
        compiler_params=pltpu.CompilerParams(collective_id=4, has_side_effects=True, vmem_limit_bytes=VMEM_LIMIT),
        name="adapter_sums",
    )(up_in, down_in, up_out, down_out, coef)
    return pl.pallas_call(
        unpack_kernel,
        out_shape=[jax.ShapeDtypeStruct((owned, rank, g.shape[2]), F32) for g in grads],
        in_specs=[whole],
        out_specs=[whole] * 4,
        name="unpack",
    )(final)


def halves(parts):
    padded = [jnp.pad(part, ((0, 0), (0, 0), (0, -part.shape[2] % LANES))) for part in parts]
    whole = jnp.concatenate(padded, axis=2)
    whole = jnp.pad(whole, ((0, 0), (0, 0), (0, -whole.shape[2] % (2 * LANES))))
    half = whole.shape[2] // 2
    return jnp.stack([whole[:, :, :half], whole[:, :, half:]])


def on_device(
    residual_in,
    cotangent,
    norm_gain,
    in_weight,
    conv_weight,
    conv_bias,
    step_bias,
    decay_log,
    skip_gain,
    gate_gain,
    out_weight,
    in_down,
    in_up,
    out_down,
    out_up,
    in_index,
    out_index,
):
    heads = step_bias.shape[0]
    inner = gate_gain.shape[0]
    mixer = conv_weight.shape[0]
    rank = in_up.shape[1]
    seq_count = lax.axis_size("seq")
    dp_count = lax.axis_size("dp")
    adapters = in_down.shape[0] * dp_count

    taps = conv_weight.T
    small = [conv_bias, gate_gain, norm_gain, jnp.repeat(skip_gain, inner // heads), step_bias, -jnp.exp(decay_log)]
    small = [jnp.pad(v, (0, mixer - v.shape[0]))[None, :] for v in small]
    params = jnp.concatenate([taps] + small, axis=0)
    early = halves([in_up[:, :, inner:], in_down.transpose(0, 2, 1)])
    late = halves([in_up[:, :, :inner], out_down.transpose(0, 2, 1), out_up])
    block_out, grad_input, gin_up, gin_down, gout_up, gout_down = block_call(
        in_index, out_index, residual_in, cotangent, in_weight, out_weight, early, late, params,
        (heads, inner, mixer, rank), dp_count, seq_count,
    )
    owners = jnp.arange(adapters)[:, None]
    coef = jnp.stack([(index[:, 0][None, :] == owners).astype(F32).reshape(-1) for index in (in_index, out_index)])
    gin_up, gin_down, gout_up, gout_down = adapter_sums(
        (gin_up, gin_down, gout_up, gout_down), coef, in_down.shape[0], seq_count, dp_count
    )
    gin_down, gout_down = (g.transpose(0, 2, 1) for g in (gin_down, gout_down))
    return (block_out, grad_input, gin_down, gin_up, gout_down, gout_up)


def solution(mesh):
    rows = P("dp", "seq", None)
    split = P("dp", None, None)
    return jax.shard_map(
        on_device,
        mesh=mesh,
        in_specs=(
            rows,
            rows,
            P(),
            P("dp", None),
            P(),
            P(),
            P(),
            P(),
            P(),
            P(),
            P("dp", None),
            split,
            split,
            split,
            split,
            P("dp", None),
            P("dp", None),
        ),
        out_specs=(rows, rows, split, split, split, split),
        check_vma=False,
    )
```

time: 322 us -> 241 us (0.75)
  Pallas kernels: 293 us -> 226 us
  between operations: 14.3 us -> 0.88 us
  local copies, waits for them, and re-layouts: 5.21 us -> 10.6 us
  waiting for transfers between devices: 5.38 us -> 0 us
    pallas_call x9 -> x1, Pallas kernels: 260 us -> 190 us  [block_call(): pl.pallas_call(functools.partial(block_kernel, dp_count, seq_count), out_...]
    unnamed x20 -> x24, local copies, waits for them, and re-layouts: 0.68 us -> 6.11 us
    ppermute x1 -> x0, waiting for transfers between devices: 4.64 us -> none  [on_device(): rim = lax.ppermute(gpre[:, :RIM], 'seq', [(j, i) for i, j in route])]
  transfers between devices with their start and end apart: 3 -> 0, of which waited for: 1 -> 0; matrix products, arithmetic and copies ran while one was open for 1% -> 0% of each run, Pallas kernels for 26% -> 0%
where the time goes in v3:
time: 241 us
  Pallas kernels  226 us (94%)
  local copies, waits for them, and re-layouts  10.6 us (4%)
  other arithmetic  3.76 us (2%)
    pallas_call x1, Pallas kernels, block_call(): pl.pallas_call(functools.partial(block_kernel, dp_count, seq_count), out_...  190 us
    pallas_call x1, Pallas kernels, adapter_sums(): pl.pallas_call(functools.partial(sums_kernel, count, dp_count), out_shape...  34 us
    unnamed x24, local copies, waits for them, and re-layouts  6.11 us

profile of v3, /device:TPU:0, one launch (start us, length us, event | category | flops | bytes accessed | tf_op | source)
XLA Modules:
  0.0 240.9 jit_solution(10393866362467317055)
XLA Ops:
  0.6 0.0 copy-start.5
  0.6 0.0 copy-start.7
  0.7 0.0 copy-start.2
  0.7 0.0 copy-start.4
  0.7 0.0 copy-start.6
  0.7 0.0 copy-start.3
  0.7 0.0 copy-start.1
  0.7 0.0 copy-start.8
  0.7 0.0 copy-start.9
  0.7 1.0 slice.27
  1.7 0.9 fusion.3
  2.6 0.7 pad_maximum_fusion.late_ref
  3.3 0.9 slice.25
  4.2 0.8 fusion.1
  5.1 0.9 fusion.4
  6.0 0.7 pad_maximum_fusion.1.early_ref
  6.7 0.0 copy-done.5
  6.7 0.1 broadcast_in_dim.25
  6.7 0.1 reshape.71
  6.9 0.0 copy-done.2
  7.0 1.3 concatenate.16.par
  8.4 0.6 copy.25.in_idx
  9.0 0.0 copy-done.9
  9.0 0.6 copy.26.out_idx
  9.7 189.8 %block.1 = (bf16[2,768,768]{2,1,0:T(8,128)(2,1)}, bf16[2,768,768]{2,1,0:T(8,128)(2,1)}, f32[2,16,3352]{2,1,0:T(8,128)}, f32[2,16,768]{2,1,0:T(8,128)}, f32[2,16,768]{2,1,0:T(8,128)}, /*index=5*/f32[2,16,1536]{2,1,0:T(8,128)}) custom-call(s32[2,1]{1,0:T(2,128)} %copy.25.in_idx, s32[2,1]{1,0:T(2,128)} %copy.26.out_idx, bf16[2,768,768]{2,1,0:T(8,128)(2,1)} %res_ref.1, ...), custom_call_target="tpu_custom_call" | custom-call | tf_op jit(solution)/shard_map/block/pallas_call | solution.py:897
  199.5 0.1 convert_element_type.34
  199.6 0.1 convert_element_type.35
  199.7 0.6 add_convert_fusion.coef_ref
  200.3 34.0 %adapter_sums.1.final = bf16[56,32,128]{2,1,0:T(8,128)(2,1)} custom-call(f32[2,16,3352]{2,1,0:T(8,128)} %get-tuple-element.18.up_in_ref, f32[2,16,768]{2,1,0:T(8,128)} %get-tuple-element.19.down_in_ref, f32[2,16,768]{2,1,0:T(8,128)} %get-tuple-element.20.up_out_ref, f32[2,16,1536]{2,1,0:T(8,128)} %get-tuple-element.21.down_out_ref, ...), custom_call_target="tpu_custom_call" | custom-call | tf_op jit(solution)/shard_map/adapter_sums/pallas_call | solution.py:1091
  234.2 1.9 unpack.1
  236.1 3.4 %copy.29 = bf16[2,768,768]{2,1,0:T(8,128)(2,1)} copy(bf16[2,768,768]{2,1,0:T(8,128)(2,1)} %get-tuple-element.36) | data formatting | bytes 4718592
  239.5 1.4 copy.30
  (22 shorter events, 0.1 us)
Async XLA Ops:
  0.6 6.0 %copy-start.5 = (f32[24]{0:T(128)S(1)}, f32[24]{0:T(128)}, u32[]{:S(2)}) copy-start(f32[24]{0:T(128)} %param.25) | copy-start | bytes 292
  0.6 6.2 %copy-start.7 = (f32[24]{0:T(128)S(1)}, f32[24]{0:T(128)}, u32[]{:S(2)}) copy-start(f32[24]{0:T(128)} %param.24) | copy-start | bytes 292
  0.7 6.2 %copy-start.2 = (f32[1536]{0:T(1024)S(1)}, f32[1536]{0:T(1024)}, u32[]{:S(2)}) copy-start(f32[1536]{0:T(1024)} %param.26) | copy-start | bytes 18436
  0.7 6.3 %copy-start.4 = (f32[768]{0:T(1024)S(1)}, f32[768]{0:T(1024)}, u32[]{:S(2)}) copy-start(f32[768]{0:T(1024)} %param.19) | copy-start | bytes 9220
  0.7 6.3 %copy-start.6 = (f32[24]{0:T(128)S(1)}, f32[24]{0:T(128)}, u32[]{:S(2)}) copy-start(f32[24]{0:T(128)} %param.23) | copy-start | bytes 292
  0.7 6.3 %copy-start.3 = (f32[1792]{0:T(1024)S(1)}, f32[1792]{0:T(1024)}, u32[]{:S(2)}) copy-start(f32[1792]{0:T(1024)} %param.22) | copy-start | bytes 21508
  0.7 6.3 %copy-start.1 = (f32[1792,4]{0,1:T(4,128)S(1)}, f32[1792,4]{0,1:T(4,128)}, u32[]{:S(2)}) copy-start(f32[1792,4]{0,1:T(4,128)} %param.21) | copy-start | bytes 86020
  0.7 7.6 %copy-start.8 = (s32[2,1]{0,1:T(1,128)S(1)}, s32[2,1]{0,1:T(1,128)}, u32[]{:S(2)}) copy-start(s32[2,1]{0,1:T(1,128)} %param.32) | copy-start | bytes 28
  0.7 8.3 %copy-start.9 = (s32[2,1]{0,1:T(1,128)S(1)}, s32[2,1]{0,1:T(1,128)}, u32[]{:S(2)}) copy-start(s32[2,1]{0,1:T(1,128)} %param.33) | copy-start | bytes 28
  236.1 3.4 %copy-start = (bf16[2,768,768]{2,1,0:T(8,128)(2,1)S(1)}, bf16[2,768,768]{2,1,0:T(8,128)(2,1)}, u32[]{:S(2)}) copy-start(bf16[2,768,768]{2,1,0:T(8,128)(2,1)} %get-tuple-element.37) | copy-start | bytes 7077892

commit v4 on v3

--- a/solution.py
+++ b/solution.py
@@ -18,6 +18,7 @@
 MESH = pl.DeviceIdType.MESH
 VMEM_LIMIT = 62 * 2**20
 PARTS = 3
+FINAL = 4
 CONV_BIAS, GATE_GAIN, NORM_GAIN, SKIP, STEP_BIAS, RATE = (slice(4 + n, 5 + n) for n in range(6))
 
 
@@ -33,30 +34,37 @@
     return lax.dot_general(a, b, (((0,), (0,)), ((), ())), preferred_element_type=F32)
 
 
-def exact(a, b):
-    return lax.dot_general(
-        a, b, (((1,), (0,)), ((), ())), precision=lax.Precision.HIGHEST, preferred_element_type=F32
-    )
-
-
 def sigmoid(v):
     return 0.5 * jnp.tanh(0.5 * v) + 0.5
 
 
-def spread(values, onehot):
-    high = values.astype(BF)
-    rest = (values - high.astype(F32)).astype(BF)
-    return nn(high, onehot) + nn(rest, onehot)
-
-
-def gather_heads(values, onehot):
-    return nt(values.astype(BF), onehot)
+def two_terms(values, heads):
+    lane = lax.broadcasted_iota(jnp.int32, values.shape, 1)
+    values = jnp.where(lane < heads, values, 0.0)
+    high = values.astype(BF).astype(F32)
+    return (high + pltpu.roll(values - high, LANES // 2, 1)).astype(BF)
+
+
+def spread(values, onehot, heads):
+    return nn(two_terms(values, heads), onehot)
+
+
+def gather_heads(values, onehot, heads):
+    sums = nt(values, onehot)
+    lane = lax.broadcasted_iota(jnp.int32, sums.shape, 1)
+    return jnp.where(lane < heads, sums, 0.0)
+
+
+def running(ones, values, heads):
+    sums = nn(ones.astype(BF), two_terms(values, heads))
+    return sums + pltpu.roll(sums, LANES // 2, 1)
 
 
 def head_onehot(heads, inner):
     width = inner // heads
-    row = lax.broadcasted_iota(jnp.int32, (heads, inner), 0)
-    col = lax.broadcasted_iota(jnp.int32, (heads, inner), 1)
+    row = lax.broadcasted_iota(jnp.int32, (LANES, inner), 0)
+    col = lax.broadcasted_iota(jnp.int32, (LANES, inner), 1)
+    row = jnp.where(row < LANES // 2, row, row - LANES // 2)
     low = row * width
     return jnp.where((col >= low) & (col < low + width), 1.0, 0.0).astype(BF)
 
@@ -94,9 +102,9 @@
     lax.fori_loop(0, rows // step, body, 0)
 
 
-def project_step(first_block, normed, halo, win, down, up, par, low_ref, xbc, dact, wid, cum, sig, sloc, cpre, ext, state, run, onehot):
+def project_step(heads, first_block, normed, halo, win, wtail, down, up, par, low_ref, xbc, dact, wid, cum, sig, sloc, cpre, ext, state, run, onehot):
     rows = normed.shape[0]
-    heads, inner = onehot.shape
+    inner = onehot.shape[1]
     mixer = xbc.shape[1]
     states = (mixer - inner) // 2
 
@@ -107,10 +115,10 @@
         v = halo[...].astype(F32)
         scale = lax.rsqrt(jnp.mean(v * v, axis=1, keepdims=True) + EPS)
         first = (v * scale * par[NORM_GAIN, : normed.shape[1]]).astype(BF)
-        low_first = nt(first, down[...]).astype(BF)
+        both = jnp.concatenate([first, nt(first, down[...]).astype(BF)], axis=1)
         for at in range(0, mixer, 2 * LANES):
             t = slice(at, at + 2 * LANES)
-            v = nn(first, win[:, t]) + nn(low_first, up[:, inner + at : inner + at + 2 * LANES])
+            v = nn(both, jnp.concatenate([win[:, t], up[:, inner + at : inner + at + 2 * LANES]], axis=0))
             ext[at // LANES, 0:RIM, :] = v[:, :LANES]
             ext[at // LANES + 1, 0:RIM, :] = v[:, LANES:]
 
@@ -121,13 +129,14 @@
     tokens = normed[...]
     low = nt(tokens, down[...]).astype(BF)
     low_ref[...] = low
+    both = jnp.concatenate([tokens, low], axis=1)
     for at in range(0, mixer, 2 * LANES):
         t = slice(at, at + 2 * LANES)
-        v = nn(tokens, win[:, t]) + nn(low, up[:, inner + at : inner + at + 2 * LANES])
+        v = nn(both, jnp.concatenate([win[:, t], up[:, inner + at : inner + at + 2 * LANES]], axis=0))
         ext[at // LANES, RIM : RIM + rows, :] = v[:, :LANES]
         ext[at // LANES + 1, RIM : RIM + rows, :] = v[:, LANES:]
-    cols = slice(inner + mixer, inner + mixer + heads)
-    raw = nn(tokens, win[:, mixer : mixer + heads]) + nn(low, up[:, cols]) + par[STEP_BIAS, :heads]
+    raw = nn(both, jnp.concatenate([wtail[...], up[:, inner + mixer :]], axis=0))
+    raw = raw + par[STEP_BIAS, :LANES]
     sig[...] = sigmoid(raw)
     widths = jnp.maximum(raw, 0.0) + jnp.log1p(jnp.exp(-jnp.abs(raw)))
     wid[...] = widths
@@ -144,10 +153,10 @@
             dact[rows_of(j), t] = (s + act * (1.0 - s)).astype(BF)
     for j in range(rows // CHUNK):
         w = widths[rows_of(j)]
-        c = exact(ones, w * par[RATE, :heads])
+        c = running(ones, w * par[RATE, :LANES], heads)
         cum[rows_of(j)] = c
         last = c[CHUNK - 1 : CHUNK]
-        tail = spread(jnp.exp(last - c) * w, onehot[...])
+        tail = spread(jnp.exp(last - c) * w, onehot[...], heads)
         weighted = jnp.concatenate(
             [(xbc[rows_of(j), t].astype(F32) * tail[:, t]).astype(BF) for t in tiles(inner)], axis=1
         )
@@ -155,7 +164,7 @@
         update = nn(inputs_t, weighted)
         before = run[...]
         cpre[j] = before
-        keep = spread(jnp.exp(jnp.broadcast_to(last, before.shape)), onehot[...])[0:1]
+        keep = spread(jnp.exp(jnp.broadcast_to(last, before.shape)), onehot[...], heads)[0:1]
         for t in tiles(inner):
             old = state[:, t]
             sloc[j, :, t] = old.astype(BF)
@@ -163,21 +172,21 @@
         run[...] = before + last
 
 
-def intra_step(normed, low_ref, win, up, xbc, wid, cum, gate, y, onehot):
-    heads, inner = onehot.shape
+def intra_step(heads, normed, low_ref, win, up, xbc, wid, cum, gate, y, onehot):
+    inner = onehot.shape[1]
     states = (xbc.shape[1] - inner) // 2
     width = inner // heads
     per = LANES // width
-    tokens, low = normed[...], low_ref[...]
+    both = jnp.concatenate([normed[...], low_ref[...]], axis=1)
     for at in range(0, inner, 2 * LANES):
         t = slice(at, at + 2 * LANES)
-        gate[:, t] = (nn(tokens, win[:, t]) + nn(low, up[:, t])).astype(BF)
+        gate[:, t] = nn(both, jnp.concatenate([win[:, t], up[:, t]], axis=0)).astype(BF)
     lane = lax.broadcasted_iota(jnp.int32, (CHUNK, LANES), 1)
     mask = lower_ones(CHUNK)
     for j in range(xbc.shape[0] // CHUNK):
         c = cum[rows_of(j)] * LOG2E
         c_rows = c.T
-        wide = spread(wid[rows_of(j)], onehot[...])
+        wide = spread(wid[rows_of(j)], onehot[...], heads)
         inputs = xbc[rows_of(j), inner : inner + states]
         reads = xbc[rows_of(j), inner + states :]
         scores = nt(reads, inputs) * mask
@@ -194,11 +203,11 @@
 
 
 def output_step(
-    first_block, middle, loaded, y, xbc, gate, cum, sloc, cpre, csuf, start, res, cot, out, wout, down, up, par,
+    heads, first_block, middle, loaded, y, xbc, gate, cum, sloc, cpre, csuf, start, res, cot, out, wout, down, up, par,
     dreads, rowt, gup, gdown, onehot, snow, adj, run, gated, nout, gno, prod,
 ):
     rows = res.shape[0]
-    heads, inner = onehot.shape
+    inner = onehot.shape[1]
     states = (xbc.shape[1] - inner) // 2
     chunks = rows // CHUNK
 
@@ -211,11 +220,11 @@
 
     reach, scale = [], []
     for j in range(chunks):
-        since = spread(jnp.exp(cpre[j]), onehot[...])
+        since = spread(jnp.exp(cpre[j]), onehot[...], heads)
         for t in tiles(inner):
             snow[j, :, t] = (sloc[j, :, t].astype(F32) + since[0:1, t] * start[:, t].astype(F32)).astype(BF)
         carried = nn(xbc[rows_of(j), inner + states :], snow[j])
-        grow = spread(jnp.exp(cum[rows_of(j)]), onehot[...])
+        grow = spread(jnp.exp(cum[rows_of(j)]), onehot[...], heads)
         reach.append(grow)
         total = jnp.zeros((CHUNK, LANES), F32)
         for t in tiles(inner):
@@ -235,9 +244,10 @@
     normed_out = nout[...]
     cot_rows = cot[...]
     low_out = nt(normed_out, down[...]).astype(BF)
+    both = jnp.concatenate([normed_out, low_out], axis=1)
     for at in range(0, out.shape[1], 2 * LANES):
         t = slice(at, at + 2 * LANES)
-        part = nn(normed_out, wout[:, t]) + nn(low_out, up[:, t])
+        part = nn(both, jnp.concatenate([wout[:, t], up[:, t]], axis=0))
         out[:, t] = (res[:, t].astype(F32) + part).astype(BF)
     grad_low = nt(cot_rows, up[...]).astype(BF)
     for at in range(0, inner, 2 * LANES):
@@ -268,7 +278,7 @@
             gate[rows_of(j), t] = (grad * full * (s * (1.0 + g * (1.0 - s)))).astype(BF)
             prod[:, t] = (dy * local).astype(BF)
             scaled.append((dy * reach[j][:, t]).astype(BF))
-        rowt[rows_of(j)] = nt(prod[...], onehot[...])
+        rowt[rows_of(j)] = gather_heads(prod[...], onehot[...], heads)
         scaled = jnp.concatenate(scaled, axis=1)
         reads_t = xbc[rows_of(j), inner + states :].astype(F32).T.astype(BF)
         update = nn(reads_t, scaled)
@@ -284,8 +294,8 @@
         run[...] = before + last
 
 
-def adjoint_step(first_block, between, xbc, dact, wid, cum, sig, dy, dreads, rowt, gloc, csuf, end, final, par, onehot, adj, prod, z, held):
-    heads, inner = onehot.shape
+def adjoint_step(heads, first_block, between, xbc, dact, wid, cum, sig, dy, dreads, rowt, gloc, csuf, end, final, par, onehot, adj, prod, z, held):
+    inner = onehot.shape[1]
     states = (xbc.shape[1] - inner) // 2
     width = inner // heads
     per = LANES // width
@@ -299,7 +309,8 @@
             overlap.append(jnp.sum(end[:, t].astype(F32) * final(t), axis=0, keepdims=True))
         v = jnp.broadcast_to(jnp.concatenate(overlap, axis=1), (8, inner))
         high = v.astype(BF)
-        held[...] = nt(high, onehot[...]) + nt((v - high.astype(F32)).astype(BF), onehot[...])
+        rest = (v - high.astype(F32)).astype(BF)
+        held[...] = gather_heads(high, onehot[...], heads) + gather_heads(rest, onehot[...], heads)
 
     for j in reversed(range(xbc.shape[0] // CHUNK)):
         at = rows_of(j)
@@ -307,35 +318,35 @@
         w = wid[at]
         c_two = c * LOG2E
         c_rows = c_two.T
-        wide = spread(w, onehot[...])
+        wide = spread(w, onehot[...], heads)
         inputs = xbc[at, inner : inner + states]
         reads = xbc[at, inner + states :]
         scores_t = nt(inputs, reads) * mask
         total = jnp.zeros((CHUNK, CHUNK), F32)
         for k, t in enumerate(tiles(inner)):
-            weighted = xbc[at, t].astype(F32) * wide[:, t]
-            grads = dy[at, t]
-            mixing, left, right = [], [], []
+            weighted = (xbc[at, t].astype(F32) * wide[:, t]).astype(BF)
+            grads = dy[at, t].astype(F32)
+            mixing, right = [], []
             for p in range(per):
                 inside = (lane >= p * width) & (lane < (p + 1) * width)
-                left.append(jnp.where(inside, weighted, 0.0).astype(BF))
-                right.append(jnp.where(inside, grads.astype(F32), 0.0).astype(BF))
-            products = nt(jnp.concatenate(left, axis=0), grads)
+                right.append(jnp.where(inside, grads, 0.0).astype(BF))
+            right = jnp.concatenate(right, axis=0)
+            products = nt(weighted, right)
             for p in range(per):
                 h = k * per + p
                 kernel = jnp.exp2(jnp.minimum(c_rows[h : h + 1, :] - c_two[:, h : h + 1], 0.0))
                 mixing.append((kernel * scores_t).astype(BF))
-                total = total + kernel * products[p * CHUNK : (p + 1) * CHUNK]
-            z[:, t] = nn(jnp.concatenate(mixing, axis=1), jnp.concatenate(right, axis=0))
+                total = total + kernel * products[:, p * CHUNK : (p + 1) * CHUNK]
+            z[:, t] = nn(jnp.concatenate(mixing, axis=1), right)
         total = total * mask
         dinputs = nn(total.astype(BF), reads)
         dreads_all = dreads[at] + nn(total.T.astype(BF), inputs)
 
-        since = spread(jnp.exp(csuf[j]), onehot[...])
+        since = spread(jnp.exp(csuf[j]), onehot[...], heads)
         for t in tiles(inner):
             adj[:, t] = (gloc[j, :, t].astype(F32) + since[0:1, t] * end[:, t].astype(F32)).astype(BF)
         last = c[CHUNK - 1 : CHUNK]
-        tail = spread(jnp.exp(last - c), onehot[...])
+        tail = spread(jnp.exp(last - c), onehot[...], heads)
         carried = nn(inputs, adj[...])
         weighted = []
         for t in tiles(inner):
@@ -350,18 +361,18 @@
         dact[at, t] = (dinputs * dact[at, t].astype(F32)).astype(BF)
         t = slice(inner + states, inner + 2 * states)
         dact[at, t] = (dreads_all * dact[at, t].astype(F32)).astype(BF)
-        direct = nt(prod[...], onehot[...])
-        grad_rate = held[0:1] + exact(mask, rowt[at] - w * direct)
+        direct = gather_heads(prod[...], onehot[...], heads)
+        grad_rate = held[0:1] + running(mask, rowt[at] - w * direct, heads)
         held[...] = jnp.broadcast_to(grad_rate[0:1], held.shape)
-        sig[at] = (direct + par[RATE, :heads] * grad_rate) * sig[at]
+        sig[at] = (direct + par[RATE, :LANES] * grad_rate) * sig[at]
         between(j)
 
 
-def input_step(first_block, loaded, following, gpre, ggate, graw, low_ref, res, cot, gin, wgate, win, down, up, par, gup, gdown, ext, gn, nrm):
+def input_step(heads, first_block, loaded, following, gpre, ggate, graw, low_ref, res, cot, gin, wgate, win, wtail, down, up, par, gup, gdown, ext, gn, nrm):
     rows = res.shape[0]
     inner = ggate.shape[1]
     mixer = gpre.shape[1]
-    proj = inner + win.shape[1]
+    proj = inner + mixer + heads
     model = res.shape[1]
     gain = par[NORM_GAIN, :model]
 
@@ -382,14 +393,12 @@
                 term = par[k : k + 1, t] * ext[n, at : at + CHUNK, :]
                 total = term if total is None else total + term
             gpre[rows_of(j), t] = total.astype(BF)
-    whole = slice(inner, inner + mixer)
-    rest = slice(inner + mixer, proj)
-    grads_gate, grads_mix, grads_rest = ggate[...], gpre[...], graw[...].astype(BF)
-    grad_low = (nt(grads_gate, up[:, :inner]) + nt(grads_mix, up[:, whole]) + nt(grads_rest, up[:, rest])).astype(BF)
+    grads_gate, grads_mix = ggate[...], jnp.concatenate([gpre[...], graw[...].astype(BF)], axis=1)
+    grad_low = (nt(grads_gate, up[:, :inner]) + nt(grads_mix, up[:, inner:])).astype(BF)
     for at in range(0, model, 2 * LANES):
         t = slice(at, at + 2 * LANES)
-        part = nt(grads_gate, wgate[t, :]) + nt(grads_mix, win[t, :mixer])
-        gn[:, t] = part + nt(grads_rest, win[t, mixer:]) + nn(grad_low, down[:, t])
+        mix = jnp.concatenate([win[t, :mixer], wtail[t, :]], axis=1)
+        gn[:, t] = nt(grads_gate, wgate[t, :]) + nt(grads_mix, mix) + nn(grad_low, down[:, t])
     loaded()
 
     def body(k, _):
@@ -405,17 +414,18 @@
     lax.fori_loop(0, rows // 32, body, 0)
     low = low_ref[...]
     gup[:, :inner] += tn(low, grads_gate)
-    gup[:, whole] += tn(low, grads_mix)
-    gup[:, rest] += tn(low, grads_rest)
+    gup[:, inner:] += tn(low, grads_mix)[:, : proj - inner]
     gdown[...] += tn(grad_low, nrm[...])
 
 
 def block_kernel(
     dp_count, seq_count,
-    in_idx, out_idx, res_ref, cot_ref, win_ref, wout_ref, early_ref, late_ref, par,
+    in_idx, out_idx, res_ref, cot_ref, win_ref, wout_ref, up_in_ref, down_in_ref, up_out_ref, down_out_ref,
+    taps_ref, conv_bias_ref, gate_gain_ref, norm_gain_ref, skip_ref, step_bias_ref, decay_ref,
     out_ref, gin_ref, gup_in, gdown_in, gup_out, gdown_out,
     xbc, dact, gate, yb, sloc, low, wid, cum, sig, rowt, dreads, cpre, csuf, tot, dtot, start, gown, end,
-    theirs, theirs_dec, prefix, passed, tail, wmix, wgate, wout, early, late, up_in, down_in, up_out, down_out,
+    theirs, theirs_dec, prefix, passed, tail, wmix, wtail, wgate, wout, up_mix_all, up_gate_all, down_in_all, up_out_all, down_out_all,
+    up_in, down_in, up_out, down_out, par,
     halo, rim, stage_res, stage_cot, stage_out, ext, state, snow, gated, nout, prod, run, held, onehot, z, gn,
     wsems, csems, hsems, lsems,
 ):
@@ -424,9 +434,10 @@
     seqs, tokens, model = res_ref.shape
     blocks = tokens // BLOCK
     per = BLOCK // CHUNK
-    heads, inner = onehot.shape
+    heads = step_bias_ref.shape[0]
+    inner = onehot.shape[1]
     mixer = xbc.shape[2]
-    rank = up_in.shape[1]
+    proj = win_ref.shape[1]
     pairs = seq_count // 2
     side = lax.rem(seq, 2)
     pair = seq // 2
@@ -451,6 +462,18 @@
     for n in range(seqs * blocks):
         load(n).start()
     onehot[...] = head_onehot(heads, inner)
+    par[...] = jnp.zeros_like(par)
+    par[0:4] = taps_ref[...]
+    par[CONV_BIAS] = conv_bias_ref[...][None, :]
+    par[GATE_GAIN, :inner] = gate_gain_ref[...][None, :]
+    par[NORM_GAIN, :model] = norm_gain_ref[...][None, :]
+    par[STEP_BIAS, :heads] = step_bias_ref[...][None, :]
+    par[RATE, :heads] = -jnp.exp(decay_ref[...][None, :])
+    par[SKIP, :heads] = skip_ref[...][None, :]
+    v = jnp.broadcast_to(par[SKIP, :LANES], (8, LANES))
+    par[SKIP, :inner] = spread(v, onehot[...], heads)[0:1]
+    wtail[...] = jnp.zeros_like(wtail)
+    up_in[:, :, inner + mixer :] = jnp.zeros(up_in.shape[:2] + (LANES,), BF)
     pl.semaphore_wait(barrier, len(greeted))
 
     def send(src, dst, to, sems, *at):
@@ -471,22 +494,30 @@
 
         return source, target, n
 
-    def table_piece(ref, out, n):
-        owned = ref.shape[1]
-        return (lambda which: ref.at[which]), (lambda owner, which: out.at[which, pl.ds(owner * owned, owned)]), n
-
-    width = wmix.shape[1]
-    split = width // 2 // LANES * LANES
+    def table_piece(ref, out, at, wide, n):
+        owned = ref.shape[0]
+        return (lambda _: ref.at[:, :, pl.ds(at, wide)]), (lambda owner, _: out.at[pl.ds(owner * owned, owned)]), n, None, 0
+
+    width = proj - inner
+    split = mixer // 2 // LANES * LANES
+    odd = lax.rem(pair, 2)
+    across_y = (partner, side)
+    across_z = (((pair + 1 - 2 * odd) * 2 + side, dp), odd)
     groups = [
         [
-            table_piece(early_ref, early, 0),
-            rows_piece(win_ref, wmix, inner, 0, split, 1),
-            rows_piece(win_ref, wmix, inner + split, split, width - split, 2),
+            (*rows_piece(win_ref, wmix, inner, 0, split, 0), *across_y),
+            (*rows_piece(win_ref, wmix, inner + split, split, width - split, 1), *across_y),
+            table_piece(down_in_ref, down_in_all, 0, model, 2),
+            table_piece(up_in_ref, up_mix_all, inner, width, 3),
         ],
         [
-            table_piece(late_ref, late, 3),
-            rows_piece(win_ref, wgate, 0, 0, inner, 4),
-            rows_piece(wout_ref, wout, 0, 0, wout_ref.shape[1], 5),
+            table_piece(up_in_ref, up_gate_all, 0, inner, 4),
+            (*rows_piece(win_ref, wgate, 0, 0, inner, 5), *across_z),
+        ],
+        [
+            (*rows_piece(wout_ref, wout, 0, 0, wout_ref.shape[1], 6), *across_z),
+            table_piece(down_out_ref, down_out_all, 0, inner, 7),
+            table_piece(up_out_ref, up_out_all, 0, model, 8),
         ],
     ]
 
@@ -494,41 +525,58 @@
         return lax.rem(dp - 2 * k + dp_count, dp_count)
 
     def over_x(group):
-        return [send(source(side), target(dp, side), others[k - 1], wsems, 0, k, n) for source, target, n in group for k in range(1, chips)]
+        return [
+            send(source(mine), target(dp, mine), others[k - 1], wsems, 0, k, n)
+            for source, target, n, _, mine in group
+            for k in range(1, chips)
+        ]
 
     def own(group):
         copies = []
-        for source, target, n in group:
-            for which in range(2):
+        for source, target, n, mate, _ in group:
+            for which in range(1 if mate is None else 2):
                 copies.append(pltpu.make_async_copy(source(which), target(dp, which), wsems.at[0, 6 + which, 0, n]))
                 copies.append(send(source(which), target(dp, which), sibling, wsems, 3 + which, 0, n))
         return copies
 
     def forward(group, start_it):
-        for source, target, n in group:
+        for source, target, n, mate, mine in group:
             for k in range(1, chips):
-                here = target(shards(k), side)
+                here = target(shards(k), mine)
                 if start_it:
-                    send(source(side), here, others[k - 1], wsems, 0, k, n).wait_recv()
-                across = send(here, here, partner, wsems, 1, k, n)
-                over = send(here, here, sibling, wsems, 2, k, n)
+                    send(source(mine), here, others[k - 1], wsems, 0, k, n).wait_recv()
+                copies = [send(here, here, sibling, wsems, 2, k, n)]
+                if mate is not None:
+                    copies.append(send(here, here, mate, wsems, 1, k, n))
                 if start_it:
-                    across.start()
-                    over.start()
+                    for copy in copies:
+                        copy.start()
                 else:
-                    across.wait_send()
-                    over.wait()
+                    copies[0].wait()
+                    if mate is not None:
+                        copies[1].wait_send()
 
     def relay(group, start_it):
-        for source, target, n in group:
+        for source, target, n, mate, mine in group:
+            if mate is None:
+                continue
             for k in range(1, chips):
-                there = target(shards(k), 1 - side)
+                there = target(shards(k), 1 - mine)
+                if start_it:
+                    send(there, there, mate, wsems, 1, k, n).wait_recv()
                 over = send(there, there, sibling, wsems, 5, k, n)
                 if start_it:
-                    send(there, there, partner, wsems, 1, k, n).wait_recv()
                     over.start()
                 else:
                     over.wait()
+
+    def settle(group):
+        for copy in over_x(group):
+            copy.wait_send()
+        for copy in own(group):
+            copy.wait()
+        forward(group, False)
+        relay(group, False)
 
     edge = send(res_ref.at[:, pl.ds(tokens - RIM, RIM)], halo, later, hsems, 0)
     for copy in over_x(groups[0]):
@@ -549,6 +597,9 @@
 
     lax.fori_loop(0, seqs * blocks, norm_block, 0)
     forward(groups[0], True)
+    for group in groups[1:]:
+        for copy in over_x(group):
+            copy.start()
     relay(groups[0], True)
 
     @pl.when(seq == 0)
@@ -563,29 +614,18 @@
     def _():
         edge.wait_send()
 
-    for copy in over_x(groups[0]):
-        copy.wait_send()
-    for copy in over_x(groups[1]):
-        copy.start()
-    for copy in own(groups[0]):
-        copy.wait()
-    forward(groups[0], False)
-    relay(groups[0], False)
-    for copy in own(groups[1]):
-        copy.start()
-
-    def pick(table, dests):
-        half = table.shape[3] // LANES
-        n = 0
-        for dst, at, wide, idx_ref in dests:
-            for k in range(wide // LANES):
-                src = slice(n % half * LANES, n % half * LANES + LANES)
-                for s in range(seqs):
-                    dst[s, :, at + k * LANES : at + (k + 1) * LANES] = table[n // half, idx_ref[s, 0], :, src]
-                n += 1
-
-    lanes = up_in.shape[2]
-    pick(early, [(up_in, inner, lanes - inner, in_idx), (down_in, 0, model, in_idx)])
+    settle(groups[0])
+    for group in groups[1:]:
+        for copy in own(group):
+            copy.start()
+
+    def pick(dst, table, idx_ref, at=0):
+        for q in range(seqs):
+            dst[q, :, at : at + table.shape[2]] = table[idx_ref[q]]
+
+    pick(down_in, down_in_all, in_idx)
+    pick(up_in, up_mix_all, in_idx, inner)
+    wtail[:, :heads] = wmix[:, mixer:]
 
     half = inner // 2
     wide = half // PARTS
@@ -676,7 +716,7 @@
     def project_block(n, _):
         s, k = n // blocks, lax.rem(n, blocks)
         project_step(
-            k == 0, yb.at[n, :, pl.ds(0, model)], halo.at[s], wmix, down_in.at[s], up_in.at[s], par, low.at[n],
+            heads, k == 0, yb.at[n, :, pl.ds(0, model)], halo.at[s], wmix, wtail, down_in.at[s], up_in.at[s], par, low.at[n],
             xbc.at[n], dact.at[n], wid.at[n], cum.at[n], sig.at[n], sloc.at[chunk_of(n)], cpre.at[chunk_of(n)],
             ext, state, run, onehot,
         )
@@ -684,46 +724,35 @@
         @pl.when(k == blocks - 1)
         def _():
             tot[s] = state[...].astype(BF)
-            dtot[s] = spread(jnp.exp(run[...]), onehot[...])
+            dtot[s] = spread(jnp.exp(run[...]), onehot[...], heads)
+
+        @pl.when(n == blocks - 2)
+        def _():
+            forward(groups[1], True)
 
         @pl.when(n == blocks - 1)
         def _():
-            forward(groups[1], True)
+            forward(groups[2], True)
             chain_start(0, 0)
 
         @pl.when(n >= blocks)
         def _():
-            chain_tick(0, 0, n - blocks, 2 * blocks)
+            chain_tick(0, 0, n - blocks, FINAL)
 
         return 0
 
     lax.fori_loop(0, seqs * blocks, project_block, 0)
     chain_start(0, 1)
     relay(groups[1], True)
-    for copy in over_x(groups[1]):
-        copy.wait_send()
-    for copy in own(groups[1]):
-        copy.wait()
-    forward(groups[1], False)
-    relay(groups[1], False)
-    pick(late, [(up_in, 0, inner, in_idx), (down_out, 0, inner, out_idx), (up_out, 0, model, out_idx)])
-
-    def intra_block(n, _):
+    settle(groups[1])
+    pick(up_in, up_gate_all, in_idx)
+
+    def intra_block(n):
         s = n // blocks
         intra_step(
-            yb.at[n, :, pl.ds(0, model)], low.at[n], wgate, up_in.at[s], xbc.at[n], wid.at[n], cum.at[n], gate.at[n],
+            heads, yb.at[n, :, pl.ds(0, model)], low.at[n], wgate, up_in.at[s], xbc.at[n], wid.at[n], cum.at[n], gate.at[n],
             yb.at[n], onehot,
         )
-
-        @pl.when(n <= blocks)
-        def _():
-            chain_tick(0, 0, n + blocks, 2 * blocks)
-
-        chain_tick(0, 1, n, seqs * blocks - 1)
-        return 0
-
-    lax.fori_loop(0, seqs * blocks, intra_block, 0)
-    chain_end(0, 0)
 
     def staged(s, k):
         rows = pl.ds(k * BLOCK, BLOCK)
@@ -735,31 +764,41 @@
     def stored(ref, s, k):
         return pltpu.make_async_copy(stage_out, ref.at[s, pl.ds(k * BLOCK, BLOCK)], lsems.at[2])
 
-    def output_block(i, _):
-        s, k = i // blocks, blocks - 1 - lax.rem(i, blocks)
+    first = blocks + 1
+    second = seqs * blocks + blocks
+
+    def output_block(i):
+        s = jnp.where(i < second, 0, 1)
+        k = blocks - 1 - (i - jnp.where(i < second, first, second))
         n = s * blocks + k
         for copy in staged(s, k):
             copy.start()
 
-        @pl.when(i == blocks)
+        @pl.when(i == first)
+        def _():
+            relay(groups[2], True)
+            settle(groups[2])
+            pick(down_out, down_out_all, out_idx)
+            pick(up_out, up_out_all, out_idx)
+            chain_end(0, 0)
+
+        @pl.when(i == second)
         def _():
             chain_end(0, 1)
 
         def middle():
-            @pl.when(i >= blocks)
-            def _():
-                chain_tick(1, 0, 2 * (i - blocks), 2 * blocks - 1)
+            chain_tick(1, 0, among(i, {second: 1, second + 2: FINAL}), FINAL)
 
         def loaded():
             for copy in staged(s, k):
                 copy.wait()
 
-            @pl.when(i > 0)
+            @pl.when(i > first)
             def _():
                 stored(out_ref, s, k).wait()
 
         output_step(
-            k == blocks - 1, middle, loaded, yb.at[n], xbc.at[n], gate.at[n], cum.at[n], sloc.at[chunk_of(n)],
+            heads, k == blocks - 1, middle, loaded, yb.at[n], xbc.at[n], gate.at[n], cum.at[n], sloc.at[chunk_of(n)],
             cpre.at[chunk_of(n)], csuf.at[chunk_of(n)], start.at[s], stage_res, stage_cot, stage_out, wout, down_out.at[s],
             up_out.at[s], par, dreads.at[n], rowt.at[n], gup_out.at[s], gdown_out.at[s], onehot, snow, state, run, gated,
             nout, ext, prod,
@@ -770,30 +809,43 @@
         def _():
             gown[s] = state[...].astype(BF)
 
-        @pl.when(i == blocks - 1)
+        @pl.when(i == first + blocks - 1)
         def _():
             chain_start(1, 0)
 
-        @pl.when(i >= blocks)
+    def among(i, turns):
+        found = -1
+        for at, tick in turns.items():
+            found = jnp.where(i == at, tick, found)
+        return found
+
+    def middle_block(i, _):
+        inside = (i < first) | ((i >= first + blocks) & (i < second))
+
+        @pl.when(inside)
         def _():
-            chain_tick(1, 0, 2 * (i - blocks) + 1, 2 * blocks - 1)
-
+            intra_block(jnp.where(i < first, i, i - blocks))
+
+        @pl.when(jnp.logical_not(inside))
+        def _():
+            output_block(i)
+
+        chain_tick(0, 0, among(i, {1: FINAL - 1, blocks: FINAL}), FINAL)
+        chain_tick(0, 1, among(i, {1: 0, blocks: 1, first: 2, first + 1: 3, first + 2: FINAL}), FINAL)
+        chain_tick(1, 0, among(i, {second - 1: 0, second: 2, second + 1: 3}), FINAL)
         return 0
 
-    lax.fori_loop(0, seqs * blocks, output_block, 0)
+    lax.fori_loop(0, 2 * seqs * blocks, middle_block, 0)
     stored(out_ref, seqs - 1, 0).wait()
     chain_start(1, 1)
 
     def rim_edge(s):
         return send(dact.at[s * blocks, pl.ds(0, RIM)], rim.at[s], earlier, hsems, 1 + s)
 
-    period = 2 * blocks - 1
-    steps = seqs * period + seqs
+    period = 2 * blocks
 
     def back_block(i, _):
-        late_one = i >= seqs * period
-        s = jnp.where(late_one, i - seqs * period, i // period)
-        r = jnp.where(late_one, 2 * blocks - 1, lax.rem(i, period))
+        s, r = i // period, lax.rem(i, period)
 
         @pl.when(r < blocks)
         def _():
@@ -809,12 +861,11 @@
                 chain_end(1, 1)
 
             def between(j):
-                @pl.when(i < blocks)
-                def _():
-                    chain_tick(1, 1, per * i + (per - 1 - j), per * blocks - 1)
+                if j == 0:
+                    chain_tick(1, 1, jnp.where(i < blocks, i, -1), FINAL)
 
             adjoint_step(
-                k == blocks - 1, between, xbc.at[n], dact.at[n], wid.at[n], cum.at[n], sig.at[n], yb.at[n], dreads.at[n],
+                heads, k == blocks - 1, between, xbc.at[n], dact.at[n], wid.at[n], cum.at[n], sig.at[n], yb.at[n], dreads.at[n],
                 rowt.at[n], sloc.at[chunk_of(n)], csuf.at[chunk_of(n)], end.at[s],
                 lambda t: tot[s, :, t].astype(F32) + dtot[s, 0:1, t] * start[s, :, t].astype(F32),
                 par, onehot, nout.at[pl.ds(0, CHUNK)], prod, z, held,
@@ -831,6 +882,7 @@
         def _():
             k = r - blocks
             n = s * blocks + k
+            late_one = k == blocks - 1
             for copy in staged(s, k):
                 copy.start()
             for q in range(seqs):
@@ -866,26 +918,30 @@
                         ext[m, BLOCK : BLOCK + RIM, :] = dact[n + 1, 0:RIM, t].astype(F32)
 
             input_step(
-                k == 0, loaded, following, dact.at[n], gate.at[n], sig.at[n], low.at[n], stage_res, stage_cot, stage_out,
-                wgate, wmix, down_in.at[s], up_in.at[s], par, gup_in.at[s], gdown_in.at[s], ext, gn,
+                heads, k == 0, loaded, following, dact.at[n], gate.at[n], sig.at[n], low.at[n], stage_res, stage_cot, stage_out,
+                wgate, wmix, wtail, down_in.at[s], up_in.at[s], par, gup_in.at[s], gdown_in.at[s], ext, gn,
                 nout.at[:, pl.ds(0, model)],
             )
             stored(gin_ref, s, k).start()
+            chain_tick(1, 1, jnp.where(i < period, i, -1), FINAL)
 
         return 0
 
-    lax.fori_loop(0, steps, back_block, 0)
+    lax.fori_loop(0, seqs * period, back_block, 0)
     stored(gin_ref, seqs - 1, blocks - 1).wait()
 
 
-def block_call(in_index, out_index, residual, cotangent, in_weight, out_weight, early, late, params, sizes, dp_count, seq_count):
+def block_call(in_index, out_index, tensors, tables, vectors, sizes, dp_count, seq_count):
     heads, inner, mixer, rank = sizes
+    residual, _, in_weight, _ = tensors
     seqs, tokens, model = residual.shape
     states = (mixer - inner) // 2
     count = tokens // BLOCK * seqs
     chunks = tokens // CHUNK * seqs
     proj = in_weight.shape[1]
     lanes = -(-proj // LANES) * LANES
+    adapters = tables[0].shape[0] * dp_count
+    every = lambda width: pltpu.VMEM((adapters, rank, width), BF)
     rows = lambda width, kind: pltpu.VMEM((count, BLOCK, width), kind)
     state = lambda: pltpu.VMEM((seqs, states, inner), BF)
     slots = lambda: pltpu.VMEM((2, seqs, PARTS, states, inner // 2 // PARTS), BF)
@@ -904,7 +960,7 @@
             jax.ShapeDtypeStruct((seqs, rank, model), F32),
             jax.ShapeDtypeStruct((seqs, rank, inner), F32),
         ],
-        in_specs=[smem, smem] + [any_space] * 6 + [vmem],
+        in_specs=[smem, smem] + [any_space] * 8 + [vmem] * len(vectors),
         out_specs=[any_space] * 2 + [vmem] * 4,
         scratch_shapes=[
             rows(mixer, BF),
@@ -913,13 +969,13 @@
             rows(inner, BF),
             pltpu.VMEM((chunks, states, inner), BF),
             rows(rank, BF),
-            rows(heads, F32),
-            rows(heads, F32),
-            rows(heads, F32),
-            rows(heads, F32),
+            rows(LANES, F32),
+            rows(LANES, F32),
+            rows(LANES, F32),
+            rows(LANES, F32),
             rows(states, F32),
-            pltpu.VMEM((chunks, 8, heads), F32),
-            pltpu.VMEM((chunks, 8, heads), F32),
+            pltpu.VMEM((chunks, 8, LANES), F32),
+            pltpu.VMEM((chunks, 8, LANES), F32),
             state(),
             pltpu.VMEM((seqs, 8, inner), F32),
             state(),
@@ -931,14 +987,19 @@
             slots(),
             slots(),
             pltpu.VMEM((model, proj - inner), BF),
+            pltpu.VMEM((model, LANES), BF),
             pltpu.VMEM((model, inner), BF),
             pltpu.VMEM((inner, model), BF),
-            pltpu.VMEM((2, early.shape[1] * dp_count) + early.shape[2:], BF),
-            pltpu.VMEM((2, late.shape[1] * dp_count) + late.shape[2:], BF),
+            every(proj - inner),
+            every(inner),
+            every(model),
+            every(model),
+            every(inner),
             picked(lanes),
             picked(model),
             picked(model),
             picked(inner),
+            pltpu.VMEM((16, mixer), F32),
             pltpu.VMEM((seqs, RIM, model), BF),
             pltpu.VMEM((seqs, RIM, mixer), BF),
             stage(),
@@ -950,19 +1011,19 @@
             pltpu.VMEM((BLOCK, inner), BF),
             pltpu.VMEM((BLOCK, inner), BF),
             pltpu.VMEM((CHUNK, inner), BF),
-            pltpu.VMEM((8, heads), F32),
-            pltpu.VMEM((8, heads), F32),
-            pltpu.VMEM((heads, inner), BF),
+            pltpu.VMEM((8, LANES), F32),
+            pltpu.VMEM((8, LANES), F32),
+            pltpu.VMEM((LANES, inner), BF),
             pltpu.VMEM((CHUNK, inner), F32),
             pltpu.VMEM((BLOCK, model), F32),
-            pltpu.SemaphoreType.DMA((2, 8, max(dp_count // 2, 1), 6)),
+            pltpu.SemaphoreType.DMA((2, 8, max(dp_count // 2, 1), 9)),
             pltpu.SemaphoreType.DMA((2, 2, seqs, 4, PARTS)),
             pltpu.SemaphoreType.DMA((2, 1 + seqs)),
             pltpu.SemaphoreType.DMA((max(count, 3),)),
         ],
         compiler_params=pltpu.CompilerParams(collective_id=1, has_side_effects=True, vmem_limit_bytes=VMEM_LIMIT),
         name="block",
-    )(in_index, out_index, residual, cotangent, in_weight, out_weight, early, late, params)
+    )(in_index, out_index, *tensors, *tables, *vectors)
 
 
 def sums_kernel(
@@ -1116,14 +1177,6 @@
     )(final)
 
 
-def halves(parts):
-    padded = [jnp.pad(part, ((0, 0), (0, 0), (0, -part.shape[2] % LANES))) for part in parts]
-    whole = jnp.concatenate(padded, axis=2)
-    whole = jnp.pad(whole, ((0, 0), (0, 0), (0, -whole.shape[2] % (2 * LANES))))
-    half = whole.shape[2] // 2
-    return jnp.stack([whole[:, :, :half], whole[:, :, half:]])
-
-
 def on_device(
     residual_in,
     cotangent,
@@ -1151,15 +1204,15 @@
     dp_count = lax.axis_size("dp")
     adapters = in_down.shape[0] * dp_count
 
-    taps = conv_weight.T
-    small = [conv_bias, gate_gain, norm_gain, jnp.repeat(skip_gain, inner // heads), step_bias, -jnp.exp(decay_log)]
-    small = [jnp.pad(v, (0, mixer - v.shape[0]))[None, :] for v in small]
-    params = jnp.concatenate([taps] + small, axis=0)
-    early = halves([in_up[:, :, inner:], in_down.transpose(0, 2, 1)])
-    late = halves([in_up[:, :, :inner], out_down.transpose(0, 2, 1), out_up])
     block_out, grad_input, gin_up, gin_down, gout_up, gout_down = block_call(
-        in_index, out_index, residual_in, cotangent, in_weight, out_weight, early, late, params,
-        (heads, inner, mixer, rank), dp_count, seq_count,
+        in_index.reshape(-1),
+        out_index.reshape(-1),
+        (residual_in, cotangent, in_weight, out_weight),
+        (in_up, in_down.transpose(0, 2, 1), out_up, out_down.transpose(0, 2, 1)),
+        (conv_weight.T, conv_bias, gate_gain, norm_gain, skip_gain, step_bias, decay_log),
+        (heads, inner, mixer, rank),
+        dp_count,
+        seq_count,
     )
     owners = jnp.arange(adapters)[:, None]
     coef = jnp.stack([(index[:, 0][None, :] == owners).astype(F32).reshape(-1) for index in (in_index, out_index)])

time: 241 us -> 214 us (0.89)
  Pallas kernels: 226 us -> 208 us
  local copies, waits for them, and re-layouts: 10.6 us -> 4.96 us
  other arithmetic: 3.76 us -> 0.59 us
    pallas_call x1, Pallas kernels: 190 us -> 171 us  [block_call(): pl.pallas_call(functools.partial(block_kernel, dp_count, seq_count), out_...]
    unnamed x24 -> x8, local copies, waits for them, and re-layouts: 6.11 us -> 4.79 us
where the time goes in v4:
time: 214 us
  Pallas kernels  208 us (97%)
  local copies, waits for them, and re-layouts  4.96 us (2%)
    pallas_call x1, Pallas kernels, block_call(): pl.pallas_call(functools.partial(block_kernel, dp_count, seq_count), out_...  171 us
    pallas_call x1, Pallas kernels, adapter_sums(): pl.pallas_call(functools.partial(sums_kernel, count, dp_count), out_shape...  35.4 us
    unnamed x8, local copies, waits for them, and re-layouts  4.79 us

profile of v4, /device:TPU:0, one launch (start us, length us, event | category | flops | bytes accessed | tf_op | source)
XLA Modules:
  0.0 214.2 jit_solution(18267413082012001936)
XLA Ops:
  0.6 0.0 copy-start.1
  0.6 0.0 copy-start.2
  0.7 170.7 %block.1 = (bf16[2,768,768]{2,1,0:T(8,128)(2,1)}, bf16[2,768,768]{2,1,0:T(8,128)(2,1)}, f32[2,16,3352]{2,1,0:T(8,128)}, f32[2,16,768]{2,1,0:T(8,128)}, f32[2,16,768]{2,1,0:T(8,128)}, /*index=5*/f32[2,16,1536]{2,1,0:T(8,128)}) custom-call(s32[2]{0:T(128)} %bitcast.10, s32[2]{0:T(128)} %bitcast.12, bf16[2,768,768]{2,1,0:T(8,128)(2,1)} %res_ref.1, ...), custom_call_target="tpu_custom_call" | custom-call | tf_op jit(solution)/shard_map/block/pallas_call | solution.py:953
  171.4 0.0 copy-done.1
  171.4 0.1 convert_element_type.22
  171.5 0.0 copy-done.2
  171.5 0.1 convert_element_type.23
  171.6 0.6 add_convert_fusion.coef_ref
  172.2 35.4 %adapter_sums.1.final = bf16[56,32,128]{2,1,0:T(8,128)(2,1)} custom-call(f32[2,16,3352]{2,1,0:T(8,128)} %get-tuple-element.18.up_in_ref, f32[2,16,768]{2,1,0:T(8,128)} %get-tuple-element.19.down_in_ref, f32[2,16,768]{2,1,0:T(8,128)} %get-tuple-element.20.up_out_ref, f32[2,16,1536]{2,1,0:T(8,128)} %get-tuple-element.21.down_out_ref, ...), custom_call_target="tpu_custom_call" | custom-call | tf_op jit(solution)/shard_map/adapter_sums/pallas_call | solution.py:1152
  207.5 1.9 unpack.1
  209.4 0.0 copy-start
  209.5 3.4 %copy.25 = bf16[2,768,768]{2,1,0:T(8,128)(2,1)} copy(bf16[2,768,768]{2,1,0:T(8,128)(2,1)} %get-tuple-element.32) | data formatting | bytes 4718592
  212.8 0.0 copy-done
  212.8 1.4 copy.26
  (2 shorter events, 0.0 us)
Async XLA Ops:
  0.6 170.7 %copy-start.1 = (s32[2,1]{0,1:T(1,128)S(1)}, s32[2,1]{0,1:T(1,128)}, u32[]{:S(2)}) copy-start(s32[2,1]{0,1:T(1,128)} %param.32) | copy-start | bytes 28
  0.6 170.8 %copy-start.2 = (s32[2,1]{0,1:T(1,128)S(1)}, s32[2,1]{0,1:T(1,128)}, u32[]{:S(2)}) copy-start(s32[2,1]{0,1:T(1,128)} %param.33) | copy-start | bytes 28
  209.4 3.4 %copy-start = (bf16[2,768,768]{2,1,0:T(8,128)(2,1)S(1)}, bf16[2,768,768]{2,1,0:T(8,128)(2,1)}, u32[]{:S(2)}) copy-start(bf16[2,768,768]{2,1,0:T(8,128)(2,1)} %get-tuple-element.33) | copy-start | bytes 7077892

commit v5 on v4

--- a/solution.py
+++ b/solution.py
@@ -10,6 +10,7 @@
 EPS = 1e-05
 CHUNK = 128
 BLOCK = 256
+BAND = 32
 RIM = 16
 LANES = 128
 LOG2E = 1.4426950408889634
@@ -87,6 +88,10 @@
 
 def rows_of(j):
     return slice(j * CHUNK, (j + 1) * CHUNK)
+
+
+def bands(j):
+    return [(slice(at, at + BAND), slice(j * CHUNK + at, j * CHUNK + at + BAND)) for at in range(0, CHUNK, BAND)]
 
 
 def write_normed(dst, src, gain, step):
@@ -130,27 +135,34 @@
     low = nt(tokens, down[...]).astype(BF)
     low_ref[...] = low
     both = jnp.concatenate([tokens, low], axis=1)
-    for at in range(0, mixer, 2 * LANES):
-        t = slice(at, at + 2 * LANES)
-        v = nn(both, jnp.concatenate([win[:, t], up[:, inner + at : inner + at + 2 * LANES]], axis=0))
-        ext[at // LANES, RIM : RIM + rows, :] = v[:, :LANES]
-        ext[at // LANES + 1, RIM : RIM + rows, :] = v[:, LANES:]
     raw = nn(both, jnp.concatenate([wtail[...], up[:, inner + mixer :]], axis=0))
     raw = raw + par[STEP_BIAS, :LANES]
     sig[...] = sigmoid(raw)
     widths = jnp.maximum(raw, 0.0) + jnp.log1p(jnp.exp(-jnp.abs(raw)))
     wid[...] = widths
     ones = lower_ones(CHUNK)
-    for j in range(rows // CHUNK):
-        for n, t in enumerate(tiles(mixer)):
+
+    def convolve(n):
+        t = slice(n * LANES, n * LANES + LANES)
+        for start in range(0, rows, BAND):
             pre = par[CONV_BIAS, t]
             for k in range(4):
-                at = RIM - 3 + k + j * CHUNK
-                pre = pre + par[k : k + 1, t] * ext[n, at : at + CHUNK, :]
+                at = RIM - 3 + k + start
+                pre = pre + par[k : k + 1, t] * ext[n, at : at + BAND, :]
             s = sigmoid(pre)
             act = pre * s
-            xbc[rows_of(j), t] = act.astype(BF)
-            dact[rows_of(j), t] = (s + act * (1.0 - s)).astype(BF)
+            xbc[start : start + BAND, t] = act.astype(BF)
+            dact[start : start + BAND, t] = (s + act * (1.0 - s)).astype(BF)
+
+    for n in range(0, mixer // LANES + 2, 2):
+        if n < mixer // LANES:
+            at = n * LANES
+            v = nn(both, jnp.concatenate([win[:, at : at + 2 * LANES], up[:, inner + at : inner + at + 2 * LANES]], axis=0))
+            ext[n, RIM : RIM + rows, :] = v[:, :LANES]
+            ext[n + 1, RIM : RIM + rows, :] = v[:, LANES:]
+        if n > 0:
+            convolve(n - 2)
+            convolve(n - 1)
     for j in range(rows // CHUNK):
         w = widths[rows_of(j)]
         c = running(ones, w * par[RATE, :LANES], heads)
@@ -178,19 +190,23 @@
     width = inner // heads
     per = LANES // width
     both = jnp.concatenate([normed[...], low_ref[...]], axis=1)
-    for at in range(0, inner, 2 * LANES):
-        t = slice(at, at + 2 * LANES)
-        gate[:, t] = nn(both, jnp.concatenate([win[:, t], up[:, t]], axis=0)).astype(BF)
     lane = lax.broadcasted_iota(jnp.int32, (CHUNK, LANES), 1)
     mask = lower_ones(CHUNK)
+    ready = []
     for j in range(xbc.shape[0] // CHUNK):
         c = cum[rows_of(j)] * LOG2E
-        c_rows = c.T
         wide = spread(wid[rows_of(j)], onehot[...], heads)
         inputs = xbc[rows_of(j), inner : inner + states]
         reads = xbc[rows_of(j), inner + states :]
-        scores = nt(reads, inputs) * mask
-        for k, t in enumerate(tiles(inner)):
+        ready.append((c, c.T, wide, nt(reads, inputs) * mask))
+    columns = tiles(inner)
+    order = list(range(normed.shape[1] // LANES, len(columns))) + list(range(normed.shape[1] // LANES))
+    for n, k in enumerate(order):
+        t = columns[k]
+        if n < inner // (2 * LANES):
+            g = slice(n * 2 * LANES, (n + 1) * 2 * LANES)
+            gate[:, g] = nn(both, jnp.concatenate([win[:, g], up[:, g]], axis=0)).astype(BF)
+        for j, (c, c_rows, wide, scores) in enumerate(ready):
             weighted = xbc[rows_of(j), t].astype(F32) * wide[:, t]
             mixing, parts = [], []
             for p in range(per):
@@ -226,18 +242,19 @@
         carried = nn(xbc[rows_of(j), inner + states :], snow[j])
         grow = spread(jnp.exp(cum[rows_of(j)]), onehot[...], heads)
         reach.append(grow)
-        total = jnp.zeros((CHUNK, LANES), F32)
-        for t in tiles(inner):
-            local = y[rows_of(j), t].astype(F32) + grow[:, t] * carried[:, t]
-            y[rows_of(j), t] = local.astype(BF)
-            g = gate[rows_of(j), t].astype(F32)
-            v = (local + par[SKIP, t] * xbc[rows_of(j), t].astype(F32)) * (g * sigmoid(g))
-            gated[rows_of(j), t] = v.astype(BF)
-            total = total + v * v
-        r = lax.rsqrt(jnp.sum(total, axis=1, keepdims=True) * (1.0 / inner) + EPS)
-        scale.append(r)
-        for t in tiles(inner):
-            nout[rows_of(j), t] = (gated[rows_of(j), t].astype(F32) * r * par[GATE_GAIN, t]).astype(BF)
+        for here, at in bands(j):
+            total = jnp.zeros((BAND, LANES), F32)
+            for t in tiles(inner):
+                local = y[at, t].astype(F32) + grow[here, t] * carried[here, t]
+                y[at, t] = local.astype(BF)
+                g = gate[at, t].astype(F32)
+                v = (local + par[SKIP, t] * xbc[at, t].astype(F32)) * (g * sigmoid(g))
+                gated[at, t] = v.astype(BF)
+                total = total + v * v
+            r = lax.rsqrt(jnp.sum(total, axis=1, keepdims=True) * (1.0 / inner) + EPS)
+            scale.append(r)
+            for t in tiles(inner):
+                nout[at, t] = (gated[at, t].astype(F32) * r * par[GATE_GAIN, t]).astype(BF)
 
     middle()
     loaded()
@@ -259,27 +276,30 @@
     gdown[...] += tn(grad_low, normed_out)
 
     for j in reversed(range(chunks)):
-        total = jnp.zeros((CHUNK, LANES), F32)
-        for n, t in enumerate(tiles(inner)):
-            q = gno[n, rows_of(j), :] * par[GATE_GAIN, t]
-            total = total + gated[rows_of(j), t].astype(F32) * q
-        r = scale[j]
-        shrink = jnp.sum(total, axis=1, keepdims=True) * (1.0 / inner) * (r * r * r)
-        scaled = []
-        for n, t in enumerate(tiles(inner)):
-            q = gno[n, rows_of(j), :] * par[GATE_GAIN, t]
-            grad = r * q - gated[rows_of(j), t].astype(F32) * shrink
-            local = y[rows_of(j), t].astype(F32)
-            g = gate[rows_of(j), t].astype(F32)
-            s = sigmoid(g)
-            dy = grad * (g * s)
-            y[rows_of(j), t] = dy.astype(BF)
-            full = local + par[SKIP, t] * xbc[rows_of(j), t].astype(F32)
-            gate[rows_of(j), t] = (grad * full * (s * (1.0 + g * (1.0 - s)))).astype(BF)
-            prod[:, t] = (dy * local).astype(BF)
-            scaled.append((dy * reach[j][:, t]).astype(BF))
+        pieces = []
+        for m, (here, at) in enumerate(bands(j)):
+            total = jnp.zeros((BAND, LANES), F32)
+            for n, t in enumerate(tiles(inner)):
+                q = gno[n, at, :] * par[GATE_GAIN, t]
+                total = total + gated[at, t].astype(F32) * q
+            r = scale[j * (CHUNK // BAND) + m]
+            shrink = jnp.sum(total, axis=1, keepdims=True) * (1.0 / inner) * (r * r * r)
+            scaled = []
+            for n, t in enumerate(tiles(inner)):
+                q = gno[n, at, :] * par[GATE_GAIN, t]
+                grad = r * q - gated[at, t].astype(F32) * shrink
+                local = y[at, t].astype(F32)
+                g = gate[at, t].astype(F32)
+                s = sigmoid(g)
+                dy = grad * (g * s)
+                y[at, t] = dy.astype(BF)
+                full = local + par[SKIP, t] * xbc[at, t].astype(F32)
+                gate[at, t] = (grad * full * (s * (1.0 + g * (1.0 - s)))).astype(BF)
+                prod[here, t] = (dy * local).astype(BF)
+                scaled.append((dy * reach[j][here, t]).astype(BF))
+            pieces.append(jnp.concatenate(scaled, axis=1))
         rowt[rows_of(j)] = gather_heads(prod[...], onehot[...], heads)
-        scaled = jnp.concatenate(scaled, axis=1)
+        scaled = jnp.concatenate(pieces, axis=0)
         reads_t = xbc[rows_of(j), inner + states :].astype(F32).T.astype(BF)
         update = nn(reads_t, scaled)
         dreads[rows_of(j)] = nt(scaled, snow[j])
@@ -385,14 +405,14 @@
         for j in range(rows // CHUNK):
             ext[n, rows_of(j), :] = gpre[rows_of(j), t].astype(F32)
     following()
-    for j in range(rows // CHUNK):
-        for n, t in enumerate(tiles(mixer)):
+    for n, t in enumerate(tiles(mixer)):
+        for start in range(0, rows, BAND):
             total = None
             for k in range(4):
-                at = 3 - k + j * CHUNK
-                term = par[k : k + 1, t] * ext[n, at : at + CHUNK, :]
+                at = 3 - k + start
+                term = par[k : k + 1, t] * ext[n, at : at + BAND, :]
                 total = term if total is None else total + term
-            gpre[rows_of(j), t] = total.astype(BF)
+            gpre[start : start + BAND, t] = total.astype(BF)
     grads_gate, grads_mix = ggate[...], jnp.concatenate([gpre[...], graw[...].astype(BF)], axis=1)
     grad_low = (nt(grads_gate, up[:, :inner]) + nt(grads_mix, up[:, inner:])).astype(BF)
     for at in range(0, model, 2 * LANES):
@@ -420,14 +440,15 @@
 
 def block_kernel(
     dp_count, seq_count,
-    in_idx, out_idx, res_ref, cot_ref, win_ref, wout_ref, up_in_ref, down_in_ref, up_out_ref, down_out_ref,
+    in_idx, out_idx, coef_ref, res_ref, cot_ref, win_ref, wout_ref, up_in_ref, down_in_ref, up_out_ref, down_out_ref,
     taps_ref, conv_bias_ref, gate_gain_ref, norm_gain_ref, skip_ref, step_bias_ref, decay_ref,
-    out_ref, gin_ref, gup_in, gdown_in, gup_out, gdown_out,
+    out_ref, gin_ref, sums_ref,
     xbc, dact, gate, yb, sloc, low, wid, cum, sig, rowt, dreads, cpre, csuf, tot, dtot, start, gown, end,
     theirs, theirs_dec, prefix, passed, tail, wmix, wtail, wgate, wout, up_mix_all, up_gate_all, down_in_all, up_out_all, down_out_all,
     up_in, down_in, up_out, down_out, par,
     halo, rim, stage_res, stage_cot, stage_out, ext, state, snow, gated, nout, prod, run, held, onehot, z, gn,
-    wsems, csems, hsems, lsems,
+    gup_in, gdown_in, gup_out, gdown_out, pack, first_half, half_sum, half_sent, line, red, give, owners,
+    wsems, csems, hsems, lsems, rsems,
 ):
     dp = lax.axis_index("dp")
     seq = lax.axis_index("seq")
@@ -450,9 +471,17 @@
     lower = (lax.rem(pair + pairs - 1, pairs) * 2 + side, dp)
     others = [(seq, lax.rem(dp + 2 * k, dp_count)) for k in range(1, chips)]
     barrier = pltpu.get_barrier_semaphore()
-    greeted = [partner, sibling, later, earlier, upper, lower] + others
-    for other in greeted:
+    along = [(lax.rem(pair + k, pairs) * 2 + side, dp) for k in range(1, pairs)]
+    across = [(seq, lax.rem(dp + k, dp_count)) for k in range(1, dp_count)]
+    for other in [partner] + along + across:
         pl.semaphore_signal(barrier, inc=1, device_id=other, device_id_type=MESH)
+    greeted = pairs + dp_count - 1
+    for other, there in ((later, seq < seq_count - 1), (earlier, seq > 0)):
+        greeted = greeted + jnp.where(there, 1, 0)
+
+        @pl.when(there)
+        def _(other=other):
+            pl.semaphore_signal(barrier, inc=1, device_id=other, device_id_type=MESH)
 
     def load(n):
         s, k = n // blocks, lax.rem(n, blocks) if not isinstance(n, int) else n % blocks
@@ -474,7 +503,7 @@
     par[SKIP, :inner] = spread(v, onehot[...], heads)[0:1]
     wtail[...] = jnp.zeros_like(wtail)
     up_in[:, :, inner + mixer :] = jnp.zeros(up_in.shape[:2] + (LANES,), BF)
-    pl.semaphore_wait(barrier, len(greeted))
+    pl.semaphore_wait(barrier, greeted)
 
     def send(src, dst, to, sems, *at):
         return pltpu.make_async_remote_copy(
@@ -710,6 +739,109 @@
             def _(q=q):
                 hop(q).wait_send()
 
+    rank = gup_in.shape[1]
+    owned = up_in_ref.shape[0]
+
+    def reduction(number, parts):
+        counts = [sum(-(-g.shape[2] // LANES) for g in pair_of) for pair_of in ((gup_out, gdown_out), (gup_in, gdown_in))]
+        shares = [-(-n // seq_count) for n in counts]
+        share = shares[number]
+        wide = pairs * share
+        before = sum(shares[:number])
+        base, middle, small = before * seq_count, before * pairs, pl.ds(before, share)
+        place = pl.ds(base + (side * pairs + pair) * share, share)
+
+        def swap():
+            theirs_of = pack.at[pl.ds(base + (1 - side) * wide, wide)]
+            return send(theirs_of, first_half.at[pl.ds(middle, wide)], partner, rsems, number, 0, 0)
+
+        def along_line(k):
+            there = lax.rem(pair + k, pairs)
+            mine = half_sent.at[pl.ds(middle + there * share, share)]
+            return send(mine, line.at[k - 1, small], along[k - 1], rsems, number, 1, k)
+
+        def to_owner(k):
+            return send(give.at[k - 1, small], owners.at[k - 1, small], across[k - 1], rsems, number, 2, k)
+
+        def back_along(k):
+            return send(sums_ref.at[place], sums_ref.at[place], along[k - 1], rsems, number, 3, k)
+
+        def back_across():
+            ours = sums_ref.at[pl.ds(base + side * wide, wide)]
+            return send(ours, ours, partner, rsems, number, 4, 0)
+
+        def part(owner, n, a):
+            total = None
+            for q in range(seqs):
+                c = coef_ref[1 - number, (owner * owned + a) * seqs + q]
+                term = c * red[before + n, q * rank : (q + 1) * rank, :]
+                total = term if total is None else total + term
+            return total
+
+        def start():
+            n = base
+            for ref in parts:
+                for t in tiles(ref.shape[2]):
+                    for q in range(seqs):
+                        v = ref[q, :, t]
+                        if t.stop - t.start < LANES:
+                            v = jnp.concatenate([v, jnp.zeros((rank, LANES - t.stop + t.start), F32)], axis=1)
+                        pack[n, q * rank : (q + 1) * rank, :] = v.astype(BF)
+                    n += 1
+            for m in range(n, base + share * seq_count):
+                pack[m] = jnp.zeros_like(pack[m])
+            swap().start()
+
+        def second():
+            swap().wait()
+
+            def add(n, _):
+                v = pack[base + side * wide + n].astype(F32) + first_half[middle + n].astype(F32)
+                half_sum[n] = v
+                half_sent[middle + n] = v.astype(BF)
+                return 0
+
+            lax.fori_loop(0, wide, add, 0)
+            for k in range(1, pairs):
+                along_line(k).start()
+
+        def third():
+            for k in range(1, pairs):
+                along_line(k).wait()
+            for n in range(share):
+                v = half_sum[pair * share + n]
+                for k in range(pairs - 1):
+                    v = v + line[k, before + n].astype(F32)
+                red[before + n] = v
+            for k in range(1, dp_count):
+                owner = lax.rem(dp + k, dp_count)
+                for n in range(share):
+                    for a in range(owned):
+                        give[k - 1, before + n, a * rank : (a + 1) * rank, :] = part(owner, n, a).astype(BF)
+                to_owner(k).start()
+
+        def fourth():
+            for k in range(1, dp_count):
+                to_owner(k).wait()
+            for n in range(share):
+                for a in range(owned):
+                    v = part(dp, n, a)
+                    for k in range(dp_count - 1):
+                        v = v + owners[k, before + n, a * rank : (a + 1) * rank, :].astype(F32)
+                    sums_ref[base + (side * pairs + pair) * share + n, a * rank : (a + 1) * rank, :] = v.astype(BF)
+            for k in range(1, pairs):
+                back_along(k).start()
+
+        def fifth():
+            for k in range(1, pairs):
+                back_along(k).wait()
+            back_across().start()
+
+        def finish():
+            back_across().wait()
+
+        return [start, second, third, fourth, fifth, finish]
+
     def chunk_of(n):
         return pl.ds(n * per, per)
 
@@ -754,15 +886,19 @@
             yb.at[n], onehot,
         )
 
-    def staged(s, k):
+    def staged(s, k, slot):
         rows = pl.ds(k * BLOCK, BLOCK)
         return [
-            pltpu.make_async_copy(res_ref.at[s, rows], stage_res, lsems.at[0]),
-            pltpu.make_async_copy(cot_ref.at[s, rows], stage_cot, lsems.at[1]),
+            pltpu.make_async_copy(res_ref.at[s, rows], stage_res.at[slot], lsems.at[slot]),
+            pltpu.make_async_copy(cot_ref.at[s, rows], stage_cot.at[slot], lsems.at[2 + slot]),
         ]
 
     def stored(ref, s, k):
-        return pltpu.make_async_copy(stage_out, ref.at[s, pl.ds(k * BLOCK, BLOCK)], lsems.at[2])
+        return pltpu.make_async_copy(stage_out, ref.at[s, pl.ds(k * BLOCK, BLOCK)], lsems.at[4])
+
+    def stage(n, backwards):
+        s, k = n // blocks, lax.rem(n, blocks)
+        return staged(s, blocks - 1 - k if backwards else k, lax.rem(n, 2))
 
     first = blocks + 1
     second = seqs * blocks + blocks
@@ -771,8 +907,8 @@
         s = jnp.where(i < second, 0, 1)
         k = blocks - 1 - (i - jnp.where(i < second, first, second))
         n = s * blocks + k
-        for copy in staged(s, k):
-            copy.start()
+        turn = s * blocks + blocks - 1 - k
+        slot = lax.rem(turn, 2)
 
         @pl.when(i == first)
         def _():
@@ -790,8 +926,13 @@
             chain_tick(1, 0, among(i, {second: 1, second + 2: FINAL}), FINAL)
 
         def loaded():
-            for copy in staged(s, k):
+            for copy in stage(turn, True):
                 copy.wait()
+
+            @pl.when(turn < seqs * blocks - 1)
+            def _():
+                for copy in stage(turn + 1, True):
+                    copy.start()
 
             @pl.when(i > first)
             def _():
@@ -799,7 +940,7 @@
 
         output_step(
             heads, k == blocks - 1, middle, loaded, yb.at[n], xbc.at[n], gate.at[n], cum.at[n], sloc.at[chunk_of(n)],
-            cpre.at[chunk_of(n)], csuf.at[chunk_of(n)], start.at[s], stage_res, stage_cot, stage_out, wout, down_out.at[s],
+            cpre.at[chunk_of(n)], csuf.at[chunk_of(n)], start.at[s], stage_res.at[slot], stage_cot.at[slot], stage_out, wout, down_out.at[s],
             up_out.at[s], par, dreads.at[n], rowt.at[n], gup_out.at[s], gdown_out.at[s], onehot, snow, state, run, gated,
             nout, ext, prod,
         )
@@ -835,6 +976,8 @@
         chain_tick(1, 0, among(i, {second - 1: 0, second: 2, second + 1: 3}), FINAL)
         return 0
 
+    for copy in stage(0, True):
+        copy.start()
     lax.fori_loop(0, 2 * seqs * blocks, middle_block, 0)
     stored(out_ref, seqs - 1, 0).wait()
     chain_start(1, 1)
@@ -883,8 +1026,7 @@
             k = r - blocks
             n = s * blocks + k
             late_one = k == blocks - 1
-            for copy in staged(s, k):
-                copy.start()
+            slot = lax.rem(n, 2)
             for q in range(seqs):
                 @pl.when((s == q) & (k == 0) & (seq > 0))
                 def _(q=q):
@@ -899,8 +1041,13 @@
                     rim[q] = jnp.zeros_like(rim[q])
 
             def loaded():
-                for copy in staged(s, k):
+                for copy in stage(n, False):
                     copy.wait()
+
+                @pl.when(n < seqs * blocks - 1)
+                def _():
+                    for copy in stage(n + 1, False):
+                        copy.start()
 
                 @pl.when(i > blocks)
                 def _():
@@ -918,20 +1065,26 @@
                         ext[m, BLOCK : BLOCK + RIM, :] = dact[n + 1, 0:RIM, t].astype(F32)
 
             input_step(
-                heads, k == 0, loaded, following, dact.at[n], gate.at[n], sig.at[n], low.at[n], stage_res, stage_cot, stage_out,
+                heads, k == 0, loaded, following, dact.at[n], gate.at[n], sig.at[n], low.at[n], stage_res.at[slot], stage_cot.at[slot], stage_out,
                 wgate, wmix, wtail, down_in.at[s], up_in.at[s], par, gup_in.at[s], gdown_in.at[s], ext, gn,
                 nout.at[:, pl.ds(0, model)],
             )
             stored(gin_ref, s, k).start()
             chain_tick(1, 1, jnp.where(i < period, i, -1), FINAL)
 
+        for at, step in zip((2, 4, 5, 6, 7, 9), reduction(0, (gup_out, gdown_out))):
+            pl.when(i == at)(step)
         return 0
 
+    for copy in stage(0, False):
+        copy.start()
     lax.fori_loop(0, seqs * period, back_block, 0)
+    for step in reduction(1, (gup_in, gdown_in)):
+        step()
     stored(gin_ref, seqs - 1, blocks - 1).wait()
 
 
-def block_call(in_index, out_index, tensors, tables, vectors, sizes, dp_count, seq_count):
+def block_call(in_index, out_index, coef, tensors, tables, vectors, sizes, dp_count, seq_count):
     heads, inner, mixer, rank = sizes
     residual, _, in_weight, _ = tensors
     seqs, tokens, model = residual.shape
@@ -941,11 +1094,14 @@
     proj = in_weight.shape[1]
     lanes = -(-proj // LANES) * LANES
     adapters = tables[0].shape[0] * dp_count
+    own_rows = tables[0].shape[0] * rank
+    pairs = seq_count // 2
+    shares = tile_shares((model, inner), (proj, model), seq_count)
     every = lambda width: pltpu.VMEM((adapters, rank, width), BF)
     rows = lambda width, kind: pltpu.VMEM((count, BLOCK, width), kind)
     state = lambda: pltpu.VMEM((seqs, states, inner), BF)
     slots = lambda: pltpu.VMEM((2, seqs, PARTS, states, inner // 2 // PARTS), BF)
-    stage = lambda: pltpu.VMEM((BLOCK, model), BF)
+    stage = lambda *slots: pltpu.VMEM((*slots, BLOCK, model), BF)
     picked = lambda width: pltpu.VMEM((seqs, rank, width), BF)
     any_space = pl.BlockSpec(memory_space=pl.ANY)
     vmem = pl.BlockSpec(memory_space=pltpu.VMEM)
@@ -955,13 +1111,10 @@
         out_shape=[
             jax.ShapeDtypeStruct(residual.shape, BF),
             jax.ShapeDtypeStruct(residual.shape, BF),
-            jax.ShapeDtypeStruct((seqs, rank, proj), F32),
-            jax.ShapeDtypeStruct((seqs, rank, model), F32),
-            jax.ShapeDtypeStruct((seqs, rank, model), F32),
-            jax.ShapeDtypeStruct((seqs, rank, inner), F32),
+            jax.ShapeDtypeStruct((sum(shares) * seq_count, own_rows, LANES), BF),
         ],
-        in_specs=[smem, smem] + [any_space] * 8 + [vmem] * len(vectors),
-        out_specs=[any_space] * 2 + [vmem] * 4,
+        in_specs=[smem, smem, smem] + [any_space] * 8 + [vmem] * len(vectors),
+        out_specs=[any_space] * 2 + [vmem],
         scratch_shapes=[
             rows(mixer, BF),
             rows(mixer, BF),
@@ -1002,8 +1155,8 @@
             pltpu.VMEM((16, mixer), F32),
             pltpu.VMEM((seqs, RIM, model), BF),
             pltpu.VMEM((seqs, RIM, mixer), BF),
-            stage(),
-            stage(),
+            stage(2),
+            stage(2),
             stage(),
             pltpu.VMEM((mixer // LANES, BLOCK + RIM, LANES), F32),
             pltpu.VMEM((states, inner), F32),
@@ -1016,165 +1169,54 @@
             pltpu.VMEM((LANES, inner), BF),
             pltpu.VMEM((CHUNK, inner), F32),
             pltpu.VMEM((BLOCK, model), F32),
+            pltpu.VMEM((seqs, rank, proj), F32),
+            pltpu.VMEM((seqs, rank, model), F32),
+            pltpu.VMEM((seqs, rank, model), F32),
+            pltpu.VMEM((seqs, rank, inner), F32),
+            pltpu.VMEM((sum(shares) * seq_count, seqs * rank, LANES), BF),
+            pltpu.VMEM((sum(shares) * pairs, seqs * rank, LANES), BF),
+            pltpu.VMEM((max(shares) * pairs, seqs * rank, LANES), F32),
+            pltpu.VMEM((sum(shares) * pairs, seqs * rank, LANES), BF),
+            pltpu.VMEM((max(pairs - 1, 1), sum(shares), seqs * rank, LANES), BF),
+            pltpu.VMEM((sum(shares), seqs * rank, LANES), F32),
+            pltpu.VMEM((max(dp_count - 1, 1), sum(shares), own_rows, LANES), BF),
+            pltpu.VMEM((max(dp_count - 1, 1), sum(shares), own_rows, LANES), BF),
             pltpu.SemaphoreType.DMA((2, 8, max(dp_count // 2, 1), 9)),
             pltpu.SemaphoreType.DMA((2, 2, seqs, 4, PARTS)),
             pltpu.SemaphoreType.DMA((2, 1 + seqs)),
-            pltpu.SemaphoreType.DMA((max(count, 3),)),
+            pltpu.SemaphoreType.DMA((max(count, 5),)),
+            pltpu.SemaphoreType.DMA((2, 2, 5, max(pairs, dp_count))),
         ],
         compiler_params=pltpu.CompilerParams(collective_id=1, has_side_effects=True, vmem_limit_bytes=VMEM_LIMIT),
         name="block",
-    )(in_index, out_index, *tensors, *tables, *vectors)
-
-
-def sums_kernel(
-    count, dp_count, up_in_ref, down_in_ref, up_out_ref, down_out_ref, coef_ref,
-    final,
-    pack, half, half_sent, first, line, red, give, owners, sems,
-):
-    dp = lax.axis_index("dp")
-    seq = lax.axis_index("seq")
-    pair, side = seq // 2, lax.rem(seq, 2)
-    pairs = count // 2
-    share = red.shape[0]
-    seqs, rank, _ = up_in_ref.shape
-    owned = final.shape[1] // rank
-    partner = (seq + 1 - 2 * side, dp)
-    along = [(lax.rem(pair + k, pairs) * 2 + side, dp) for k in range(1, pairs)]
-    across = [(seq, lax.rem(dp + k, dp_count)) for k in range(1, dp_count)]
-    barrier = pltpu.get_barrier_semaphore()
-    for other in [partner] + along + across:
-        pl.semaphore_signal(barrier, inc=1, device_id=other, device_id_type=MESH)
-
-    places = []
-    for n, ref in enumerate((up_in_ref, down_in_ref, up_out_ref, down_out_ref)):
-        if n == 2:
-            in_tiles = len(places)
-        places += [(ref, t.start, t.stop - t.start) for t in tiles(ref.shape[2])]
-    for n, (ref, at, wide) in enumerate(places):
-        for s in range(seqs):
-            v = ref[s, :, at : at + wide]
-            if wide < LANES:
-                v = jnp.concatenate([v, jnp.zeros((rank, LANES - wide), F32)], axis=1)
-            pack[n, s * rank : (s + 1) * rank, :] = v.astype(BF)
-    for n in range(len(places), pack.shape[0]):
-        pack[n] = jnp.zeros_like(pack[n])
-    pl.semaphore_wait(barrier, 1 + len(along) + len(across))
-
-    def send(src, dst, to, *at):
-        return pltpu.make_async_remote_copy(
-            src_ref=src, dst_ref=dst, send_sem=sems.at[(0,) + at], recv_sem=sems.at[(1,) + at],
-            device_id=to, device_id_type=MESH,
-        )
-
-    wide = pairs * share
-    copy = send(pack.at[pl.ds((1 - side) * wide, wide)], first, partner, 0, 0)
-    copy.start()
-    copy.wait()
-
-    def add(n, _):
-        v = pack[side * wide + n].astype(F32) + first[n].astype(F32)
-        half[n] = v
-        half_sent[n] = v.astype(BF)
-        return 0
-
-    lax.fori_loop(0, wide, add, 0)
-    copies = []
-    for k in range(1, pairs):
-        there = lax.rem(pair + k, pairs)
-        copies.append(send(half_sent.at[pl.ds(there * share, share)], line.at[k - 1], along[k - 1], 1, k))
-        copies[-1].start()
-    for copy in copies:
-        copy.wait()
-    for n in range(share):
-        v = half[pair * share + n]
-        for k in range(pairs - 1):
-            v = v + line[k, n].astype(F32)
-        red[n] = v
-
-    def part(owner, n, a):
-        tile = (side * pairs + pair) * share + n
-        kind = jnp.where(tile < in_tiles, 0, 1)
-        total = None
-        for s in range(seqs):
-            c = coef_ref[kind, (owner * owned + a) * seqs + s]
-            term = c * red[n, s * rank : (s + 1) * rank, :]
-            total = term if total is None else total + term
-        return total
-
-    copies = []
-    for k in range(1, dp_count):
-        owner = lax.rem(dp + k, dp_count)
-        for n in range(share):
-            for a in range(owned):
-                give[k - 1, n, a * rank : (a + 1) * rank, :] = part(owner, n, a).astype(BF)
-        copies.append(send(give.at[k - 1], owners.at[k - 1], across[k - 1], 2, k))
-        copies[-1].start()
-    mine = [[part(dp, n, a) for a in range(owned)] for n in range(share)]
-    for copy in copies:
-        copy.wait()
-    here = pl.ds((side * pairs + pair) * share, share)
-    for n in range(share):
-        for a in range(owned):
-            v = mine[n][a]
-            for k in range(dp_count - 1):
-                v = v + owners[k, n, a * rank : (a + 1) * rank, :].astype(F32)
-            final[(side * pairs + pair) * share + n, a * rank : (a + 1) * rank, :] = v.astype(BF)
-    copies = []
-    for k in range(1, pairs):
-        copies.append(send(final.at[here], final.at[here], along[k - 1], 3, k))
-        copies[-1].start()
-    for copy in copies:
-        copy.wait()
-    ours = final.at[pl.ds(side * wide, wide)]
-    copy = send(ours, ours, partner, 4, 0)
-    copy.start()
-    copy.wait()
-
-def unpack_kernel(final, up_in_out, down_in_out, up_out_out, down_out_out):
-    owned, rank, _ = up_in_out.shape
-    n = 0
-    for out in (up_in_out, down_in_out, up_out_out, down_out_out):
-        for t in tiles(out.shape[2]):
-            for a in range(owned):
-                out[a, :, t] = final[n, a * rank : (a + 1) * rank, : t.stop - t.start].astype(F32)
-            n += 1
-
-
-def adapter_sums(grads, coef, owned, count, dp_count):
-    up_in, down_in, up_out, down_out = grads
-    seqs, rank, _ = up_in.shape
-    total = sum(-(-g.shape[2] // LANES) for g in grads)
-    share = -(-total // count)
-    pairs = count // 2
-    rows = seqs * rank
-    own_rows = owned * rank
+    )(in_index, out_index, coef, *tensors, *tables, *vectors)
+
+
+def tile_shares(outs, ins, count):
+    return [-(-sum(-(-width // LANES) for width in widths) // count) for widths in (outs, ins)]
+
+
+def unpack_kernel(second, sums, up_out, down_out, up_in, down_in):
+    owned, rank, _ = up_out.shape
+    for n, pair_of in ((0, (up_out, down_out)), (second, (up_in, down_in))):
+        for out in pair_of:
+            for t in tiles(out.shape[2]):
+                for a in range(owned):
+                    out[a, :, t] = sums[n, a * rank : (a + 1) * rank, : t.stop - t.start].astype(F32)
+                n += 1
+
+
+def unpack(sums, owned, rank, widths, count):
+    up_out, down_out, up_in, down_in = widths
+    shares = tile_shares((up_out, down_out), (up_in, down_in), count)
     whole = pl.BlockSpec(memory_space=pltpu.VMEM)
-    final = pl.pallas_call(
-        functools.partial(sums_kernel, count, dp_count),
-        out_shape=jax.ShapeDtypeStruct((share * count, own_rows, LANES), BF),
-        in_specs=[whole] * 4 + [pl.BlockSpec(memory_space=pltpu.SMEM)],
-        out_specs=whole,
-        scratch_shapes=[
-            pltpu.VMEM((share * count, rows, LANES), BF),
-            pltpu.VMEM((share * pairs, rows, LANES), F32),
-            pltpu.VMEM((share * pairs, rows, LANES), BF),
-            pltpu.VMEM((share * pairs, rows, LANES), BF),
-            pltpu.VMEM((max(pairs - 1, 1), share, rows, LANES), BF),
-            pltpu.VMEM((share, rows, LANES), F32),
-            pltpu.VMEM((max(dp_count - 1, 1), share, own_rows, LANES), BF),
-            pltpu.VMEM((max(dp_count - 1, 1), share, own_rows, LANES), BF),
-            pltpu.SemaphoreType.DMA((2, 5, max(pairs, dp_count))),
-        ],
-        compiler_params=pltpu.CompilerParams(collective_id=4, has_side_effects=True, vmem_limit_bytes=VMEM_LIMIT),
-        name="adapter_sums",
-    )(up_in, down_in, up_out, down_out, coef)
     return pl.pallas_call(
-        unpack_kernel,
-        out_shape=[jax.ShapeDtypeStruct((owned, rank, g.shape[2]), F32) for g in grads],
+        functools.partial(unpack_kernel, shares[0] * count),
+        out_shape=[jax.ShapeDtypeStruct((owned, rank, width), F32) for width in widths],
         in_specs=[whole],
         out_specs=[whole] * 4,
         name="unpack",
-    )(final)
+    )(sums)
 
 
 def on_device(
@@ -1204,9 +1246,12 @@
     dp_count = lax.axis_size("dp")
     adapters = in_down.shape[0] * dp_count
 
-    block_out, grad_input, gin_up, gin_down, gout_up, gout_down = block_call(
+    owners = jnp.arange(adapters)[:, None]
+    coef = jnp.stack([(index[:, 0][None, :] == owners).astype(F32).reshape(-1) for index in (in_index, out_index)])
+    block_out, grad_input, sums = block_call(
         in_index.reshape(-1),
         out_index.reshape(-1),
+        coef,
         (residual_in, cotangent, in_weight, out_weight),
         (in_up, in_down.transpose(0, 2, 1), out_up, out_down.transpose(0, 2, 1)),
         (conv_weight.T, conv_bias, gate_gain, norm_gain, skip_gain, step_bias, decay_log),
@@ -1214,11 +1259,8 @@
         dp_count,
         seq_count,
     )
-    owners = jnp.arange(adapters)[:, None]
-    coef = jnp.stack([(index[:, 0][None, :] == owners).astype(F32).reshape(-1) for index in (in_index, out_index)])
-    gin_up, gin_down, gout_up, gout_down = adapter_sums(
-        (gin_up, gin_down, gout_up, gout_down), coef, in_down.shape[0], seq_count, dp_count
-    )
+    model, proj = in_weight.shape[0] * dp_count, in_weight.shape[1]
+    gout_up, gout_down, gin_up, gin_down = unpack(sums, in_down.shape[0], rank, (model, inner, proj, model), seq_count)
     gin_down, gout_down = (g.transpose(0, 2, 1) for g in (gin_down, gout_down))
     return (block_out, grad_input, gin_down, gin_up, gout_down, gout_up)
 

time: 214 us -> 207 us (0.967)
  Pallas kernels: 208 us -> 199 us
    pallas_call x2 -> x1, Pallas kernels: 37.3 us -> 1.94 us  [unpack(): pl.pallas_call(functools.partial(unpack_kernel, shares[0] * count), out_s...]
    pallas_call x1, Pallas kernels: 171 us -> 197 us  [block_call(): pl.pallas_call(functools.partial(block_kernel, dp_count, seq_count), out_...]
    unnamed x8 -> x4, local copies, waits for them, and re-layouts: 4.79 us -> 4.78 us
where the time goes in v5:
time: 207 us; the launch traced here: 206 us
  Pallas kernels  199 us (96%)
  local copies, waits for them, and re-layouts  4.96 us (2%)
    pallas_call x1, Pallas kernels, block_call(): pl.pallas_call(functools.partial(block_kernel, dp_count, seq_count), out_...  197 us
    unnamed x4, local copies, waits for them, and re-layouts  4.78 us

profile of v5, /device:TPU:0, one launch (start us, length us, event | category | flops | bytes accessed | tf_op | source)
XLA Modules:
  0.0 206.3 jit_solution(12276667866289826032)
XLA Ops:
  0.6 0.7 iota_compare_fusion
  1.3 0.1 convert_element_type.23
  1.4 0.7 iota_compare_fusion.1
  2.0 0.1 convert_element_type.22
  2.1 0.6 add_convert_fusion.coef_ref
  2.7 196.8 %block.1 = (bf16[2,768,768]{2,1,0:T(8,128)(2,1)}, bf16[2,768,768]{2,1,0:T(8,128)(2,1)}, bf16[64,32,128]{2,1,0:T(8,128)(2,1)}) custom-call(s32[2]{0:T(128)} %bitcast.11, s32[2]{0:T(128)} %bitcast.13, f32[2,16]{1,0:T(2,128)} %add_convert_fusion.coef_ref, bf16[2,768,768]{2,1,0:T(8,128)(2,1)} %res_ref.1, bf16[2,768,768]{2,1,0:T(8,128)(2,1)} %cot_ref.1, ...), custom_call_target="tpu_custom_call" | custom-call | tf_op jit(solution)/shard_map/block/pallas_call | solution.py:1109
  199.5 1.9 unpack.1
  201.5 0.0 copy-start
  201.5 3.4 %copy.25 = bf16[2,768,768]{2,1,0:T(8,128)(2,1)} copy(bf16[2,768,768]{2,1,0:T(8,128)(2,1)} %get-tuple-element.26) | data formatting | bytes 4718592
  204.9 0.0 copy-done
  204.9 1.4 copy.26
Async XLA Ops:
  201.5 3.4 %copy-start = (bf16[2,768,768]{2,1,0:T(8,128)(2,1)S(1)}, bf16[2,768,768]{2,1,0:T(8,128)(2,1)}, u32[]{:S(2)}) copy-start(bf16[2,768,768]{2,1,0:T(8,128)(2,1)} %get-tuple-element.27) | copy-start | bytes 7077892

commit v6 on v5

--- a/solution.py
+++ b/solution.py
@@ -272,8 +272,16 @@
         v = nt(cot_rows, wout[t, :]) + nn(grad_low, down[:, t])
         gno[at // LANES, 0:rows, :] = v[:, :LANES]
         gno[at // LANES + 1, 0:rows, :] = v[:, LANES:]
-    gup[...] += tn(low_out, cot_rows)
-    gdown[...] += tn(grad_low, normed_out)
+
+    def down_gradient(at):
+        gdown[:, at : at + 2 * LANES] += tn(grad_low, normed_out[:, at : at + 2 * LANES])
+
+    def up_gradient(at):
+        gup[:, at : at + 2 * LANES] += tn(low_out, cot_rows[:, at : at + 2 * LANES])
+
+    tasks = [(up_gradient, at) for at in range(0, out.shape[1], 2 * LANES)]
+    tasks += [(down_gradient, at) for at in range(0, inner, 2 * LANES)]
+    each = -(-len(tasks) // (rows // BAND))
 
     for j in reversed(range(chunks)):
         pieces = []
@@ -298,6 +306,9 @@
                 prod[here, t] = (dy * local).astype(BF)
                 scaled.append((dy * reach[j][here, t]).astype(BF))
             pieces.append(jnp.concatenate(scaled, axis=1))
+            for task, first_column in tasks[:each]:
+                task(first_column)
+            tasks = tasks[each:]
         rowt[rows_of(j)] = gather_heads(prod[...], onehot[...], heads)
         scaled = jnp.concatenate(pieces, axis=0)
         reads_t = xbc[rows_of(j), inner + states :].astype(F32).T.astype(BF)
@@ -421,20 +432,26 @@
         gn[:, t] = nt(grads_gate, wgate[t, :]) + nt(grads_mix, mix) + nn(grad_low, down[:, t])
     loaded()
 
-    def body(k, _):
-        at = pl.ds(pl.multiple_of(k * 32, 32), 32)
+    low = low_ref[...]
+    tasks = []
+    for at in range(0, proj, 2 * LANES):
+        tasks.append(slice(at, min(at + 2 * LANES, proj)))
+
+    def up_gradient(t):
+        grads = grads_gate[:, t] if t.stop <= inner else grads_mix[:, t.start - inner : -(-t.stop // LANES) * LANES - inner]
+        gup[:, t] += tn(low, grads)[:, : t.stop - t.start]
+
+    each = -(-len(tasks) // (rows // BAND))
+    for n, start in enumerate(range(0, rows, BAND)):
+        at = slice(start, start + BAND)
         v = res[at, :].astype(F32)
         u = lax.rsqrt(jnp.mean(v * v, axis=1, keepdims=True) + EPS)
         nrm[at, :] = (v * u * gain).astype(BF)
         w = gn[at, :] * gain
         m = jnp.mean(v * w, axis=1, keepdims=True)
         gin[at, :] = (cot[at, :].astype(F32) + u * w - v * (u * u * u * m)).astype(BF)
-        return 0
-
-    lax.fori_loop(0, rows // 32, body, 0)
-    low = low_ref[...]
-    gup[:, :inner] += tn(low, grads_gate)
-    gup[:, inner:] += tn(low, grads_mix)[:, : proj - inner]
+        for t in tasks[n * each : (n + 1) * each]:
+            up_gradient(t)
     gdown[...] += tn(grad_low, nrm[...])
 
 
@@ -626,9 +643,8 @@
 
     lax.fori_loop(0, seqs * blocks, norm_block, 0)
     forward(groups[0], True)
-    for group in groups[1:]:
-        for copy in over_x(group):
-            copy.start()
+    for copy in over_x(groups[1]):
+        copy.start()
     relay(groups[0], True)
 
     @pl.when(seq == 0)
@@ -644,9 +660,8 @@
         edge.wait_send()
 
     settle(groups[0])
-    for group in groups[1:]:
-        for copy in own(group):
-            copy.start()
+    for copy in own(groups[1]):
+        copy.start()
 
     def pick(dst, table, idx_ref, at=0):
         for q in range(seqs):
@@ -751,9 +766,10 @@
         base, middle, small = before * seq_count, before * pairs, pl.ds(before, share)
         place = pl.ds(base + (side * pairs + pair) * share, share)
 
-        def swap():
-            theirs_of = pack.at[pl.ds(base + (1 - side) * wide, wide)]
-            return send(theirs_of, first_half.at[pl.ds(middle, wide)], partner, rsems, number, 0, 0)
+        def swap(there):
+            theirs_of = pack.at[pl.ds(base + ((1 - side) * pairs + there) * share, share)]
+            here = first_half.at[pl.ds(middle + there * share, share)]
+            return send(theirs_of, here, partner, rsems, number, 0, there)
 
         def along_line(k):
             there = lax.rem(pair + k, pairs)
@@ -766,9 +782,10 @@
         def back_along(k):
             return send(sums_ref.at[place], sums_ref.at[place], along[k - 1], rsems, number, 3, k)
 
-        def back_across():
-            ours = sums_ref.at[pl.ds(base + side * wide, wide)]
-            return send(ours, ours, partner, rsems, number, 4, 0)
+        def back_across(k):
+            there = lax.rem(pair + pairs - k, pairs)
+            ours = sums_ref.at[pl.ds(base + (side * pairs + there) * share, share)]
+            return send(ours, ours, partner, rsems, number, 4, k)
 
         def part(owner, n, a):
             total = None
@@ -790,20 +807,24 @@
                     n += 1
             for m in range(n, base + share * seq_count):
                 pack[m] = jnp.zeros_like(pack[m])
-            swap().start()
+            for k in list(range(1, pairs)) + [0]:
+                swap(lax.rem(pair + k, pairs)).start()
 
         def second():
-            swap().wait()
-
-            def add(n, _):
-                v = pack[base + side * wide + n].astype(F32) + first_half[middle + n].astype(F32)
-                half_sum[n] = v
-                half_sent[middle + n] = v.astype(BF)
-                return 0
-
-            lax.fori_loop(0, wide, add, 0)
-            for k in range(1, pairs):
-                along_line(k).start()
+            for k in list(range(1, pairs)) + [0]:
+                there = lax.rem(pair + k, pairs)
+                swap(there).wait()
+
+                def add(n, _, there=there):
+                    at = there * share + n
+                    v = pack[base + side * wide + at].astype(F32) + first_half[middle + at].astype(F32)
+                    half_sum[at] = v
+                    half_sent[middle + at] = v.astype(BF)
+                    return 0
+
+                lax.fori_loop(0, share, add, 0)
+                if k:
+                    along_line(k).start()
 
         def third():
             for k in range(1, pairs):
@@ -831,14 +852,16 @@
                     sums_ref[base + (side * pairs + pair) * share + n, a * rank : (a + 1) * rank, :] = v.astype(BF)
             for k in range(1, pairs):
                 back_along(k).start()
+            back_across(0).start()
 
         def fifth():
             for k in range(1, pairs):
                 back_along(k).wait()
-            back_across().start()
+                back_across(k).start()
 
         def finish():
-            back_across().wait()
+            for k in range(pairs):
+                back_across(k).wait()
 
         return [start, second, third, fourth, fifth, finish]
 
@@ -861,11 +884,16 @@
         @pl.when(n == blocks - 2)
         def _():
             forward(groups[1], True)
+            for copy in over_x(groups[2]) + own(groups[2]):
+                copy.start()
 
         @pl.when(n == blocks - 1)
         def _():
+            chain_start(0, 0)
+
+        @pl.when(n == blocks + 1)
+        def _():
             forward(groups[2], True)
-            chain_start(0, 0)
 
         @pl.when(n >= blocks)
         def _():

time: 207 us -> 196 us (0.947)
  Pallas kernels: 199 us -> 188 us
    pallas_call x1, Pallas kernels: 197 us -> 186 us  [block_call(): pl.pallas_call(functools.partial(block_kernel, dp_count, seq_count), out_...]
where the time goes in v6:
time: 196 us
  Pallas kernels  188 us (96%)
  local copies, waits for them, and re-layouts  4.96 us (3%)
    pallas_call x1, Pallas kernels, block_call(): pl.pallas_call(functools.partial(block_kernel, dp_count, seq_count), out_...  186 us
    unnamed x4, local copies, waits for them, and re-layouts  4.78 us

profile of v6, /device:TPU:0, one launch (start us, length us, event | category | flops | bytes accessed | tf_op | source)
XLA Modules:
  0.0 195.7 jit_solution(14735639497046337699)
XLA Ops:
  0.6 0.7 iota_compare_fusion
  1.3 0.1 convert_element_type.23
  1.4 0.7 iota_compare_fusion.1
  2.0 0.1 convert_element_type.22
  2.1 0.6 add_convert_fusion.coef_ref
  2.7 186.2 %block.1 = (bf16[2,768,768]{2,1,0:T(8,128)(2,1)}, bf16[2,768,768]{2,1,0:T(8,128)(2,1)}, bf16[64,32,128]{2,1,0:T(8,128)(2,1)}) custom-call(s32[2]{0:T(128)} %bitcast.11, s32[2]{0:T(128)} %bitcast.13, f32[2,16]{1,0:T(2,128)} %add_convert_fusion.coef_ref, bf16[2,768,768]{2,1,0:T(8,128)(2,1)} %res_ref.1, bf16[2,768,768]{2,1,0:T(8,128)(2,1)} %cot_ref.1, ...), custom_call_target="tpu_custom_call" | custom-call | tf_op jit(solution)/shard_map/block/pallas_call | solution.py:1137
  189.0 1.9 unpack.1
  190.9 0.0 copy-start
  190.9 3.4 %copy.25 = bf16[2,768,768]{2,1,0:T(8,128)(2,1)} copy(bf16[2,768,768]{2,1,0:T(8,128)(2,1)} %get-tuple-element.26) | data formatting | bytes 4718592
  194.3 0.0 copy-done
  194.3 1.4 copy.26
Async XLA Ops:
  190.9 3.4 %copy-start = (bf16[2,768,768]{2,1,0:T(8,128)(2,1)S(1)}, bf16[2,768,768]{2,1,0:T(8,128)(2,1)}, u32[]{:S(2)}) copy-start(bf16[2,768,768]{2,1,0:T(8,128)(2,1)} %get-tuple-element.27) | copy-start | bytes 7077892

commit v7 on v6

--- a/solution.py
+++ b/solution.py
@@ -457,7 +457,7 @@
 
 def block_kernel(
     dp_count, seq_count,
-    in_idx, out_idx, coef_ref, res_ref, cot_ref, win_ref, wout_ref, up_in_ref, down_in_ref, up_out_ref, down_out_ref,
+    in_idx, out_idx, res_ref, cot_ref, win_ref, wout_ref, up_in_ref, down_in_ref, up_out_ref, down_out_ref,
     taps_ref, conv_bias_ref, gate_gain_ref, norm_gain_ref, skip_ref, step_bias_ref, decay_ref,
     out_ref, gin_ref, sums_ref,
     xbc, dact, gate, yb, sloc, low, wid, cum, sig, rowt, dreads, cpre, csuf, tot, dtot, start, gown, end,
@@ -766,71 +766,76 @@
         base, middle, small = before * seq_count, before * pairs, pl.ds(before, share)
         place = pl.ds(base + (side * pairs + pair) * share, share)
 
-        def swap(there):
-            theirs_of = pack.at[pl.ds(base + ((1 - side) * pairs + there) * share, share)]
-            here = first_half.at[pl.ds(middle + there * share, share)]
-            return send(theirs_of, here, partner, rsems, number, 0, there)
-
-        def along_line(k):
+        def rows_of_seq(q):
+            return pl.ds(q * rank, rank)
+
+        def swap(there, q):
+            theirs_of = pack.at[pl.ds(base + ((1 - side) * pairs + there) * share, share), rows_of_seq(q)]
+            here = first_half.at[pl.ds(middle + there * share, share), rows_of_seq(q)]
+            return send(theirs_of, here, partner, rsems, number, 0, there, q)
+
+        def along_line(k, q):
             there = lax.rem(pair + k, pairs)
-            mine = half_sent.at[pl.ds(middle + there * share, share)]
-            return send(mine, line.at[k - 1, small], along[k - 1], rsems, number, 1, k)
+            mine = half_sent.at[pl.ds(middle + there * share, share), rows_of_seq(q)]
+            return send(mine, line.at[k - 1, small, rows_of_seq(q)], along[k - 1], rsems, number, 1, k, q)
 
         def to_owner(k):
-            return send(give.at[k - 1, small], owners.at[k - 1, small], across[k - 1], rsems, number, 2, k)
+            return send(give.at[k - 1, small], owners.at[k - 1, small], across[k - 1], rsems, number, 2, k, 0)
 
         def back_along(k):
-            return send(sums_ref.at[place], sums_ref.at[place], along[k - 1], rsems, number, 3, k)
+            return send(sums_ref.at[place], sums_ref.at[place], along[k - 1], rsems, number, 3, k, 0)
 
         def back_across(k):
             there = lax.rem(pair + pairs - k, pairs)
             ours = sums_ref.at[pl.ds(base + (side * pairs + there) * share, share)]
-            return send(ours, ours, partner, rsems, number, 4, k)
+            return send(ours, ours, partner, rsems, number, 4, k, 0)
 
         def part(owner, n, a):
             total = None
             for q in range(seqs):
-                c = coef_ref[1 - number, (owner * owned + a) * seqs + q]
+                index = in_idx[q] if number else out_idx[q]
+                c = jnp.where(index == owner * owned + a, 1.0, 0.0)
                 term = c * red[before + n, q * rank : (q + 1) * rank, :]
                 total = term if total is None else total + term
             return total
 
-        def start():
+        def start(q):
             n = base
             for ref in parts:
                 for t in tiles(ref.shape[2]):
-                    for q in range(seqs):
-                        v = ref[q, :, t]
-                        if t.stop - t.start < LANES:
-                            v = jnp.concatenate([v, jnp.zeros((rank, LANES - t.stop + t.start), F32)], axis=1)
-                        pack[n, q * rank : (q + 1) * rank, :] = v.astype(BF)
+                    v = ref[q, :, t]
+                    if t.stop - t.start < LANES:
+                        v = jnp.concatenate([v, jnp.zeros((rank, LANES - t.stop + t.start), F32)], axis=1)
+                    pack[n, q * rank : (q + 1) * rank, :] = v.astype(BF)
                     n += 1
             for m in range(n, base + share * seq_count):
-                pack[m] = jnp.zeros_like(pack[m])
+                pack[m, q * rank : (q + 1) * rank, :] = jnp.zeros((rank, LANES), BF)
             for k in list(range(1, pairs)) + [0]:
-                swap(lax.rem(pair + k, pairs)).start()
-
-        def second():
+                swap(lax.rem(pair + k, pairs), q).start()
+
+        def second(q):
+            rows = slice(q * rank, (q + 1) * rank)
             for k in list(range(1, pairs)) + [0]:
                 there = lax.rem(pair + k, pairs)
-                swap(there).wait()
+                swap(there, q).wait()
 
                 def add(n, _, there=there):
                     at = there * share + n
-                    v = pack[base + side * wide + at].astype(F32) + first_half[middle + at].astype(F32)
-                    half_sum[at] = v
-                    half_sent[middle + at] = v.astype(BF)
+                    v = pack[base + side * wide + at, rows, :].astype(F32) + first_half[middle + at, rows, :].astype(F32)
+                    half_sum[middle + at, rows, :] = v
+                    half_sent[middle + at, rows, :] = v.astype(BF)
                     return 0
 
                 lax.fori_loop(0, share, add, 0)
                 if k:
-                    along_line(k).start()
+                    along_line(k, q).start()
 
         def third():
             for k in range(1, pairs):
-                along_line(k).wait()
+                for q in range(seqs):
+                    along_line(k, q).wait()
             for n in range(share):
-                v = half_sum[pair * share + n]
+                v = half_sum[middle + pair * share + n]
                 for k in range(pairs - 1):
                     v = v + line[k, before + n].astype(F32)
                 red[before + n] = v
@@ -863,7 +868,14 @@
             for k in range(pairs):
                 back_across(k).wait()
 
-        return [start, second, third, fourth, fifth, finish]
+        def every_seq(step):
+            def steps():
+                for q in range(seqs):
+                    step(q)
+
+            return steps
+
+        return start, second, [every_seq(start), every_seq(second), third, fourth, fifth, finish]
 
     def chunk_of(n):
         return pl.ds(n * per, per)
@@ -1100,19 +1112,26 @@
             stored(gin_ref, s, k).start()
             chain_tick(1, 1, jnp.where(i < period, i, -1), FINAL)
 
-        for at, step in zip((2, 4, 5, 6, 7, 9), reduction(0, (gup_out, gdown_out))):
+        for at, step in zip((2, 4, 5, 6, 7, 9), reduction(0, (gup_out, gdown_out))[2]):
             pl.when(i == at)(step)
+        begin, again, _ = reduction(1, (gup_in, gdown_in))
+        for q in range(seqs - 1):
+            pl.when(i == (q + 1) * period)(functools.partial(begin, q))
+            pl.when(i == (q + 1) * period + 2)(functools.partial(again, q))
         return 0
 
     for copy in stage(0, False):
         copy.start()
     lax.fori_loop(0, seqs * period, back_block, 0)
-    for step in reduction(1, (gup_in, gdown_in)):
+    begin, again, rest = reduction(1, (gup_in, gdown_in))
+    begin(seqs - 1)
+    again(seqs - 1)
+    for step in rest[2:]:
         step()
     stored(gin_ref, seqs - 1, blocks - 1).wait()
 
 
-def block_call(in_index, out_index, coef, tensors, tables, vectors, sizes, dp_count, seq_count):
+def block_call(in_index, out_index, tensors, tables, vectors, sizes, dp_count, seq_count):
     heads, inner, mixer, rank = sizes
     residual, _, in_weight, _ = tensors
     seqs, tokens, model = residual.shape
@@ -1141,7 +1160,7 @@
             jax.ShapeDtypeStruct(residual.shape, BF),
             jax.ShapeDtypeStruct((sum(shares) * seq_count, own_rows, LANES), BF),
         ],
-        in_specs=[smem, smem, smem] + [any_space] * 8 + [vmem] * len(vectors),
+        in_specs=[smem, smem] + [any_space] * 8 + [vmem] * len(vectors),
         out_specs=[any_space] * 2 + [vmem],
         scratch_shapes=[
             rows(mixer, BF),
@@ -1203,7 +1222,7 @@
             pltpu.VMEM((seqs, rank, inner), F32),
             pltpu.VMEM((sum(shares) * seq_count, seqs * rank, LANES), BF),
             pltpu.VMEM((sum(shares) * pairs, seqs * rank, LANES), BF),
-            pltpu.VMEM((max(shares) * pairs, seqs * rank, LANES), F32),
+            pltpu.VMEM((sum(shares) * pairs, seqs * rank, LANES), F32),
             pltpu.VMEM((sum(shares) * pairs, seqs * rank, LANES), BF),
             pltpu.VMEM((max(pairs - 1, 1), sum(shares), seqs * rank, LANES), BF),
             pltpu.VMEM((sum(shares), seqs * rank, LANES), F32),
@@ -1213,38 +1232,48 @@
             pltpu.SemaphoreType.DMA((2, 2, seqs, 4, PARTS)),
             pltpu.SemaphoreType.DMA((2, 1 + seqs)),
             pltpu.SemaphoreType.DMA((max(count, 5),)),
-            pltpu.SemaphoreType.DMA((2, 2, 5, max(pairs, dp_count))),
+            pltpu.SemaphoreType.DMA((2, 2, 5, max(pairs, dp_count), seqs)),
         ],
         compiler_params=pltpu.CompilerParams(collective_id=1, has_side_effects=True, vmem_limit_bytes=VMEM_LIMIT),
         name="block",
-    )(in_index, out_index, coef, *tensors, *tables, *vectors)
+    )(in_index, out_index, *tensors, *tables, *vectors)
 
 
 def tile_shares(outs, ins, count):
     return [-(-sum(-(-width // LANES) for width in widths) // count) for widths in (outs, ins)]
 
 
-def unpack_kernel(second, sums, up_out, down_out, up_in, down_in):
+def unpack_kernel(second, out_ref, gin_ref, sums, block_out, grad_input, up_out, down_out, up_in, down_in):
     owned, rank, _ = up_out.shape
-    for n, pair_of in ((0, (up_out, down_out)), (second, (up_in, down_in))):
-        for out in pair_of:
-            for t in tiles(out.shape[2]):
-                for a in range(owned):
-                    out[a, :, t] = sums[n, a * rank : (a + 1) * rank, : t.stop - t.start].astype(F32)
-                n += 1
-
-
-def unpack(sums, owned, rank, widths, count):
+    block_out[...] = out_ref[...]
+    grad_input[...] = gin_ref[...]
+
+    @pl.when(pl.program_id(0) == 0)
+    def _():
+        for start, pair_of in ((0, (up_out, down_out)), (second, (up_in, down_in))):
+            n = start
+            for out in pair_of:
+                for t in tiles(out.shape[2]):
+                    for a in range(owned):
+                        out[a, :, t] = sums[n, a * rank : (a + 1) * rank, : t.stop - t.start].astype(F32)
+                    n += 1
+
+
+def unpack(block_out, grad_input, sums, owned, rank, widths, count):
     up_out, down_out, up_in, down_in = widths
     shares = tile_shares((up_out, down_out), (up_in, down_in), count)
-    whole = pl.BlockSpec(memory_space=pltpu.VMEM)
+    seqs, tokens, model = block_out.shape
+    large = pl.BlockSpec((1, tokens, model), lambda s: (s, 0, 0))
+    small = [jax.ShapeDtypeStruct((owned, rank, width), F32) for width in widths]
     return pl.pallas_call(
         functools.partial(unpack_kernel, shares[0] * count),
-        out_shape=[jax.ShapeDtypeStruct((owned, rank, width), F32) for width in widths],
-        in_specs=[whole],
-        out_specs=[whole] * 4,
+        grid=(seqs,),
+        out_shape=[jax.ShapeDtypeStruct(block_out.shape, BF)] * 2 + small,
+        in_specs=[large, large, pl.BlockSpec(sums.shape, lambda s: (0, 0, 0))],
+        out_specs=[large, large] + [pl.BlockSpec(v.shape, lambda s: (0, 0, 0)) for v in small],
+        compiler_params=pltpu.CompilerParams(vmem_limit_bytes=VMEM_LIMIT // 2),
         name="unpack",
-    )(sums)
+    )(block_out, grad_input, sums)
 
 
 def on_device(
@@ -1272,14 +1301,9 @@
     rank = in_up.shape[1]
     seq_count = lax.axis_size("seq")
     dp_count = lax.axis_size("dp")
-    adapters = in_down.shape[0] * dp_count
-
-    owners = jnp.arange(adapters)[:, None]
-    coef = jnp.stack([(index[:, 0][None, :] == owners).astype(F32).reshape(-1) for index in (in_index, out_index)])
     block_out, grad_input, sums = block_call(
         in_index.reshape(-1),
         out_index.reshape(-1),
-        coef,
         (residual_in, cotangent, in_weight, out_weight),
         (in_up, in_down.transpose(0, 2, 1), out_up, out_down.transpose(0, 2, 1)),
         (conv_weight.T, conv_bias, gate_gain, norm_gain, skip_gain, step_bias, decay_log),
@@ -1288,7 +1312,9 @@
         seq_count,
     )
     model, proj = in_weight.shape[0] * dp_count, in_weight.shape[1]
-    gout_up, gout_down, gin_up, gin_down = unpack(sums, in_down.shape[0], rank, (model, inner, proj, model), seq_count)
+    block_out, grad_input, gout_up, gout_down, gin_up, gin_down = unpack(
+        block_out, grad_input, sums, in_down.shape[0], rank, (model, inner, proj, model), seq_count
+    )
     gin_down, gout_down = (g.transpose(0, 2, 1) for g in (gin_down, gout_down))
     return (block_out, grad_input, gin_down, gin_up, gout_down, gout_up)
 

time: 196 us -> 194 us (0.990)
    unnamed x4 -> x6, local copies, waits for them, and re-layouts: 4.78 us -> 4.36 us
where the time goes in v7:
time: 194 us
  Pallas kernels  189 us (97%)
  local copies, waits for them, and re-layouts  4.36 us (2%)
    pallas_call x1, Pallas kernels, block_call(): pl.pallas_call(functools.partial(block_kernel, dp_count, seq_count), out_...  186 us
    unnamed x6, local copies, waits for them, and re-layouts  4.36 us

profile of v7, /device:TPU:0, one launch (start us, length us, event | category | flops | bytes accessed | tf_op | source)
XLA Modules:
  0.0 193.8 jit_solution(17874482343933987697)
XLA Ops:
  0.6 186.0 %block.1 = (bf16[2,768,768]{2,1,0:T(8,128)(2,1)}, bf16[2,768,768]{2,1,0:T(8,128)(2,1)}, bf16[64,32,128]{2,1,0:T(8,128)(2,1)}) custom-call(s32[2]{0:T(128)} %bitcast.10, s32[2]{0:T(128)} %bitcast.11, bf16[2,768,768]{2,1,0:T(8,128)(2,1)} %res_ref.1, bf16[2,768,768]{2,1,0:T(8,128)(2,1)} %cot_ref.1, bf16[192,3352]{1,0:T(8,128)(2,1)} %win_ref.1, ...), custom_call_target="tpu_custom_call" | custom-call | tf_op jit(solution)/shard_map/block/pallas_call | solution.py:1156
  186.6 0.0 copy-start
  186.6 1.7 copy-done
  188.3 0.0 copy-start.1
  188.3 1.7 copy-done.1
  190.0 0.0 copy-start.2
  190.0 1.0 copy-done.2
  191.0 2.6 %unpack.1 = (bf16[2,768,768]{2,1,0:T(8,128)(2,1)}, bf16[2,768,768]{2,1,0:T(8,128)(2,1)}, f32[2,16,768]{2,1,0:T(8,128)}, f32[2,16,1536]{2,1,0:T(8,128)}, f32[2,16,3352]{2,1,0:T(8,128)}, /*index=5*/f32[2,16,768]{2,1,0:T(8,128)}) custom-call(bf16[2,768,768]{2,1,0:T(8,128)(2,1)S(1)} %copy-done, bf16[2,768,768]{2,1,0:T(8,128)(2,1)S(1)} %copy-done.1, ...), custom_call_target="tpu_custom_call" | custom-call | tf_op jit(solution)/shard_map/unpack/pallas_call | solution.py:1268
Async XLA Ops:
  186.6 1.7 copy-start
  188.3 1.7 copy-start.1
  190.0 1.0 copy-start.2
